TPU v7x, 32 devices: a whole 2x2x4 slice. The times are simulated.
32 devices in a mesh: fsdp: 4 (over z), context: 2 (over x), tensor: 4 (over y, core).
Axes of the slice: x: 2, y: 2, z: 4, core: 2. Of those that a mesh axis runs over, the one named last changes fastest.
Arguments:
- inputs: bfloat16 [4096, 2048], P(('fsdp', 'context')), may hold values from -6 to 6
- attn_gain: bfloat16 [2048], replicated, may hold values from 0.5 to 1.5
- joined_projection_weight: bfloat16 [2048, 5120], P(('fsdp', 'context'), 'tensor'), may hold values from -0.125 to 0.125
- q_gain: bfloat16 [128], replicated, may hold values from 0.5 to 1.5
- k_gain: bfloat16 [128], replicated, may hold values from 0.5 to 1.5
- w_o: bfloat16 [2048, 4096], P(('fsdp', 'context'), 'tensor'), may hold values from -0.375 to 0.375
- moe_gain: bfloat16 [2048], replicated, may hold values from 0.5 to 1.5
- router: bfloat16 [2048, 16], replicated, may hold values from -0.0625 to 0.0625
- w_experts: bfloat16 [2048, 16, 3, 768], P(('fsdp', 'context'), None, None, 'tensor'), may hold values from -0.25 to 0.25
- segments: int32 [4096], P('fsdp'), may hold values from 0 to 4, as said below
- experts: int32 [4096, 8], P(('fsdp', 'context')), may hold values from 0 to 15, all different within a row
- out_grad: bfloat16 [4096, 2048], P(('fsdp', 'context')), may hold values from -6 to 6
Outputs:
- output: bfloat16 [4096, 2048], P(('fsdp', 'context'))
- inputs_grad: bfloat16 [4096, 2048], P(('fsdp', 'context'))
- attn_gain_grad: float32 [2048], replicated
- w_qkv_grad: float32 [2048, 5120], P(('fsdp', 'context'), 'tensor')
- q_gain_grad: float32 [128], replicated
- k_gain_grad: float32 [128], replicated
- w_o_grad: float32 [2048, 4096], P(('fsdp', 'context'), 'tensor')
- moe_gain_grad: float32 [2048], replicated
- router_grad: float32 [2048, 16], replicated
- w_experts_grad: float32 [2048, 16, 3, 768], P(('fsdp', 'context'), None, None, 'tensor')
Inputs may be any that keep to these rules, and one draw needn't show every extreme that they name: `segments`: within each sequence of 1024 tokens the numbers start at 0, rise by 0 or 1 from one token to the next and end at 4; one document covers the middle quarter of every sequence. Each row names 8 different experts, and every expert is named by some row.
All inputs are finite; a program needn't handle non-finite values.
Results may differ from a plain program's by a relative error of at most 0.02.
Values may be sent and summed in bfloat16 or wider, within the bound.
No kernel may reach another device: no remote copies, remote signals or barrier semaphores. Data moves between devices by JAX's collectives and lax.ppermute only.
A program may use at most 448 MiB of HBM per device.

v0:
```python
import jax
import jax.numpy as jnp
from jax import lax
from jax.sharding import PartitionSpec as P

QUERY_HEADS = 32
KEY_VALUE_HEADS = 4


EPSILON = 1e-06
ROPE_THETA = 1000000.0
NEGATIVE = -1e30
BEST_PRECISION = lax.Precision.HIGHEST


def norm_rows(matrix, scaling):
    return matrix * lax.rsqrt(jnp.mean(matrix * matrix, axis=-1, keepdims=True) + EPSILON) * scaling


def doc_positions(segment_ids):
    index_all = jnp.arange(segment_ids.shape[0], dtype=jnp.int32)
    starts = jnp.concatenate(
        [jnp.ones((1,), jnp.int32), (segment_ids[1:] != segment_ids[:-1]).astype(jnp.int32)]
    )
    return index_all - lax.cummax(index_all * starts, axis=0)


def rotate(tensor_array, positions):
    half_size = tensor_array.shape[-1] // 2
    inverse = ROPE_THETA ** (
        -2.0 * jnp.arange(half_size, dtype=jnp.float32) / tensor_array.shape[-1]
    )
    angles = positions.astype(jnp.float32)[:, None] * inverse[None, :]
    cosine = jnp.concatenate([jnp.cos(angles), jnp.cos(angles)], axis=-1)[:, None, :]
    sine_table = jnp.concatenate([jnp.sin(angles), jnp.sin(angles)], axis=-1)[:, None, :]
    turned = jnp.concatenate(
        [-tensor_array[..., half_size:], tensor_array[..., :half_size]], axis=-1
    )
    return tensor_array * cosine + turned * sine_table


def block_groups(group_sizes, first_row, row_count):
    group_ends = jnp.cumsum(group_sizes)
    begins = group_ends - group_sizes
    clipped_end = jnp.clip(group_ends, first_row, first_row + row_count)
    clipped_begin = jnp.clip(begins, first_row, first_row + row_count)
    return clipped_end - clipped_begin


def times_transposed(left_side, right_side):
    return lax.dot_general(
        left_side, right_side, (((1,), (1,)), ((), ())), preferred_element_type=jnp.float32
    )


def outer_rows(left_side, right_side):
    return lax.dot_general(
        left_side, right_side, (((0,), (0,)), ((), ())), preferred_element_type=jnp.float32
    )


def shards(
    inputs,
    attn_gain,
    joined_projection_weight,
    q_gain,
    k_gain,
    w_o,
    moe_gain,
    router,
    w_experts,
    segments,
    experts,
    out_grad,
):
    tok_rows, model_width = inputs.shape
    head_size = q_gain.shape[0]
    head_groups = KEY_VALUE_HEADS // lax.axis_size("tensor")
    queries_per_group = QUERY_HEADS // KEY_VALUE_HEADS
    local_heads = head_groups * queries_per_group
    top_count = experts.shape[1]
    expert_count = router.shape[1]
    sequence_length = segments.shape[0]
    weight_rows = joined_projection_weight.shape[0]
    span_start = lax.axis_index("context") * tok_rows
    first_tensor = (lax.axis_index("tensor") == 0).astype(jnp.float32)
    gain_attn = attn_gain.astype(jnp.float32)
    gain_moe = moe_gain.astype(jnp.float32)
    gain_query = q_gain.astype(jnp.float32)
    gain_key = k_gain.astype(jnp.float32)
    token_index = jnp.arange(sequence_length, dtype=jnp.int32)
    positions = lax.dynamic_slice_in_dim(doc_positions(segments), span_start, tok_rows)
    local_segments = lax.dynamic_slice_in_dim(segments, span_start, tok_rows)
    local_index = span_start + jnp.arange(tok_rows, dtype=jnp.int32)
    rows_per_block = min(512, tok_rows)
    score_scale = head_size ** (-0.5)
    attn_in, attn_out = (
        lax.all_gather(joined_projection_weight, ("fsdp", "context"), axis=0, tiled=True),
        lax.all_gather(w_o, ("fsdp", "context"), axis=0, tiled=True),
    )
    residual = inputs.astype(jnp.float32)
    inverse_attn = lax.rsqrt(jnp.mean(residual * residual, axis=-1, keepdims=True) + EPSILON)
    unit_attn = residual * inverse_attn
    normalized_input = (unit_attn * gain_attn).astype(jnp.bfloat16)
    projected_rows = jnp.dot(normalized_input, attn_in, preferred_element_type=jnp.float32).reshape(
        tok_rows, head_groups, queries_per_group + 2, head_size
    )
    query_raw = projected_rows[:, :, :queries_per_group].reshape(tok_rows, local_heads, head_size)
    key_raw = projected_rows[:, :, queries_per_group]
    value_raw = projected_rows[:, :, queries_per_group + 1]

    def prepare(query_part, key_part, query_gain, key_gain):
        return (
            rotate(norm_rows(query_part, query_gain), positions),
            rotate(norm_rows(key_part, key_gain), positions),
        )

    query_rot, key_rot = prepare(query_raw, key_raw, gain_query, gain_key)
    queries = query_rot.astype(jnp.bfloat16)
    key_values = jnp.concatenate([key_rot, value_raw], axis=-1).astype(jnp.bfloat16)
    gathered_pairs = lax.all_gather(key_values, "context", axis=0, tiled=True)
    all_keys = gathered_pairs[:, :, :head_size]
    all_values = gathered_pairs[:, :, head_size:]

    def block_scores(first_row):
        grouped_heads = queries.reshape(rows_per_block, head_groups, queries_per_group, head_size)
        scores = (
            jnp.einsum(
                "qghd,kgd->ghqk", grouped_heads, all_keys, preferred_element_type=jnp.float32
            )
            * score_scale
        )
        same_doc = local_segments[first_row : first_row + rows_per_block, None] == segments[None, :]
        earlier = local_index[first_row : first_row + rows_per_block, None] >= token_index[None, :]
        return (grouped_heads, jnp.where((same_doc & earlier)[None, None], scores, NEGATIVE))

    first_row = 0
    grouped_heads, scores = block_scores(first_row)
    row_peak = jnp.max(scores, axis=-1, keepdims=True)
    raised = jnp.exp(scores - row_peak)
    summed = jnp.sum(raised, axis=-1, keepdims=True)
    attn_probs = (raised / summed).astype(jnp.bfloat16)
    mixed_block = jnp.einsum(
        "ghqk,kgd->qghd", attn_probs, all_values, preferred_element_type=jnp.float32
    )
    mixed_parts = mixed_block.reshape(rows_per_block, local_heads * head_size)
    log_totals = [row_peak + jnp.log(summed)]
    attended = mixed_parts.astype(jnp.bfloat16)
    attn_sum = lax.psum(times_transposed(attended, attn_out), "tensor")
    hidden_state = residual + attn_sum
    inverse_moe = lax.rsqrt(jnp.mean(hidden_state * hidden_state, axis=-1, keepdims=True) + EPSILON)
    unit_moe = hidden_state * inverse_moe
    mixed_in = (unit_moe * gain_moe).astype(jnp.bfloat16)
    logits = jnp.dot(mixed_in, router, preferred_element_type=jnp.float32)
    chosen = jnp.take_along_axis(logits, experts, axis=1)
    raised_gate = jnp.exp(chosen - jnp.max(chosen, axis=-1, keepdims=True))
    gate_values = raised_gate / jnp.sum(raised_gate, axis=-1, keepdims=True)
    expert_all = lax.all_gather(w_experts, ("fsdp", "context"), axis=0, tiled=True)
    hidden_units = expert_all.shape[3]
    flat_ids = experts.reshape(-1)
    sort_order = jnp.argsort(flat_ids, stable=True)
    undo_order = jnp.argsort(sort_order, stable=True)
    token_of = sort_order // top_count
    expert_ids = jnp.arange(expert_count, dtype=jnp.int32)
    group_sizes = jnp.sum((flat_ids[:, None] == expert_ids[None, :]).astype(jnp.int32), axis=0)
    sorted_inputs = jnp.take(mixed_in, token_of, axis=0)
    sorted_gates = jnp.take(gate_values.reshape(-1), sort_order)
    weights_in = jnp.transpose(expert_all[:, :, :2], (1, 0, 2, 3)).reshape(
        expert_count, model_width, 2 * hidden_units
    )
    weights_out = jnp.transpose(expert_all[:, :, 2], (1, 2, 0))
    assigned = flat_ids.shape[0]
    slab_rows = min(2048, assigned)
    moe_part = jnp.zeros((tok_rows, model_width), jnp.float32)
    gate_up_parts = []
    active_parts = []
    gate_dot_parts = []
    for slab_start in range(0, assigned, slab_rows):
        slab_sizes = block_groups(group_sizes, slab_start, slab_rows)
        slab_tokens = token_of[slab_start : slab_start + slab_rows]
        gate_up = lax.ragged_dot(
            sorted_inputs[slab_start : slab_start + slab_rows],
            weights_in,
            slab_sizes,
            preferred_element_type=jnp.float32,
        )
        gate_half = gate_up[:, :hidden_units]
        active = (gate_half * jax.nn.sigmoid(gate_half) * gate_up[:, hidden_units:]).astype(
            jnp.bfloat16
        )
        outputs = lax.ragged_dot(
            active, weights_out, slab_sizes, preferred_element_type=jnp.float32
        )
        moe_part = moe_part.at[slab_tokens].add(
            outputs * sorted_gates[slab_start : slab_start + slab_rows][:, None]
        )
        gate_dot_parts.append(
            jnp.sum(jnp.take(out_grad, slab_tokens, axis=0).astype(jnp.float32) * outputs, axis=-1)
        )
        gate_up_parts.append(gate_up)
        active_parts.append(active)
    gate_dot_part = jnp.take(jnp.concatenate(gate_dot_parts), undo_order).reshape(
        tok_rows, top_count
    )
    moe_sum, gate_dot = (
        lax.psum(moe_part.astype(jnp.bfloat16), "tensor").astype(jnp.float32),
        lax.psum(gate_dot_part.astype(jnp.bfloat16), "tensor").astype(jnp.float32),
    )
    output = (hidden_state + moe_sum).astype(jnp.bfloat16)
    attn_in, attn_out = (
        lax.all_gather(joined_projection_weight, ("fsdp", "context"), axis=0, tiled=True),
        lax.all_gather(w_o, ("fsdp", "context"), axis=0, tiled=True),
    )
    expert_all = lax.all_gather(w_experts, ("fsdp", "context"), axis=0, tiled=True)
    cotangent = out_grad.astype(jnp.float32)
    gate_slope = gate_values * (gate_dot - jnp.sum(gate_values * gate_dot, axis=-1, keepdims=True))
    picked = (experts[:, :, None] == expert_ids[None, None, :]).astype(jnp.float32)
    logit_grad = jnp.einsum("tk,tke->te", gate_slope, picked, precision=BEST_PRECISION).astype(
        jnp.bfloat16
    )
    router_term = outer_rows(mixed_in, logit_grad) * first_tensor
    router_back = times_transposed(logit_grad, router)
    weights_down = jnp.transpose(expert_all[:, :, 2], (1, 0, 2))
    weights_back = jnp.transpose(expert_all[:, :, :2], (1, 2, 3, 0)).reshape(
        expert_count, 2 * hidden_units, model_width
    )
    back_part = jnp.zeros((tok_rows, model_width), jnp.float32)
    scaled_parts = []
    slope_parts = []
    for slab_index, slab_start in enumerate(range(0, assigned, slab_rows)):
        slab_sizes = block_groups(group_sizes, slab_start, slab_rows)
        slab_tokens = token_of[slab_start : slab_start + slab_rows]
        scaled = (
            jnp.take(out_grad, slab_tokens, axis=0).astype(jnp.float32)
            * sorted_gates[slab_start : slab_start + slab_rows][:, None]
        ).astype(jnp.bfloat16)
        act_grad = lax.ragged_dot(
            scaled, weights_down, slab_sizes, preferred_element_type=jnp.float32
        )
        gate_half = gate_up_parts[slab_index][:, :hidden_units]
        up_half = gate_up_parts[slab_index][:, hidden_units:]
        gate_sigmoid = jax.nn.sigmoid(gate_half)
        gate_up_grad = jnp.concatenate(
            [
                act_grad * up_half * gate_sigmoid * (1.0 + gate_half * (1.0 - gate_sigmoid)),
                act_grad * gate_half * gate_sigmoid,
            ],
            axis=1,
        ).astype(jnp.bfloat16)
        back_part = back_part.at[slab_tokens].add(
            lax.ragged_dot(
                gate_up_grad, weights_back, slab_sizes, preferred_element_type=jnp.float32
            )
        )
        scaled_parts.append(scaled)
        slope_parts.append(gate_up_grad)
    sorted_scaled = jnp.concatenate(scaled_parts, axis=0)
    sorted_slopes = jnp.concatenate(slope_parts, axis=0)
    active_all = jnp.concatenate(active_parts, axis=0)
    numbers = lax.RaggedDotDimensionNumbers(
        dot_dimension_numbers=(([0], [0]), ([], [])),
        lhs_ragged_dimensions=[0],
        rhs_group_dimensions=[],
    )
    grad_in = lax.ragged_dot_general(
        sorted_inputs, sorted_slopes, group_sizes, numbers, preferred_element_type=jnp.float32
    )
    grad_out = lax.ragged_dot_general(
        sorted_scaled, active_all, group_sizes, numbers, preferred_element_type=jnp.float32
    )
    stacked = jnp.concatenate(
        [
            grad_in.reshape(
                expert_count, weight_rows * lax.axis_size(("fsdp", "context")), 2, hidden_units
            ),
            grad_out[:, :, None],
        ],
        axis=2,
    )
    w_experts_grad = lax.psum_scatter(
        jnp.transpose(stacked, (1, 0, 2, 3)).astype(jnp.bfloat16),
        ("fsdp", "context"),
        scatter_dimension=0,
        tiled=True,
    ).astype(jnp.float32)
    moe_back = lax.psum(back_part, "tensor") + router_back
    unit_grad = moe_back * gain_moe
    state_grad = cotangent + inverse_moe * (
        unit_grad - unit_moe * jnp.mean(unit_grad * unit_moe, axis=-1, keepdims=True)
    )
    moe_gain_term = jnp.sum(moe_back * unit_moe, axis=0) * first_tensor
    branch_grad = state_grad.astype(jnp.bfloat16)
    attended_grad = jnp.dot(branch_grad, attn_out, preferred_element_type=jnp.float32).astype(
        jnp.bfloat16
    )
    w_o_grad = lax.psum_scatter(
        outer_rows(branch_grad, attended).astype(jnp.bfloat16),
        ("fsdp", "context"),
        scatter_dimension=0,
        tiled=True,
    ).astype(jnp.float32)
    key_grad = jnp.zeros((sequence_length, head_groups, head_size), jnp.float32)
    value_grad = jnp.zeros((sequence_length, head_groups, head_size), jnp.float32)
    query_parts = []
    for block_number, first_row in enumerate(range(0, tok_rows, rows_per_block)):
        grouped_heads, scores = block_scores(first_row)
        attn_probs = jnp.exp(scores - log_totals[block_number])
        attn_low = attn_probs.astype(jnp.bfloat16)
        mixed_grad = attended_grad.reshape(
            rows_per_block, head_groups, queries_per_group, head_size
        )
        prob_grad = jnp.einsum(
            "qghd,kgd->ghqk", mixed_grad, all_values, preferred_element_type=jnp.float32
        )
        score_grad = (
            attn_probs * (prob_grad - jnp.sum(attn_probs * prob_grad, axis=-1, keepdims=True))
        ).astype(jnp.bfloat16)
        block_of_queries = (
            jnp.einsum("ghqk,kgd->qghd", score_grad, all_keys, preferred_element_type=jnp.float32)
            * score_scale
        )
        query_parts.append(block_of_queries.reshape(rows_per_block, local_heads, head_size))
        key_grad = (
            jnp.einsum(
                "ghqk,qghd->kgd", score_grad, grouped_heads, preferred_element_type=jnp.float32
            )
            * score_scale
        )
        value_grad = jnp.einsum(
            "ghqk,qghd->kgd", attn_low, mixed_grad, preferred_element_type=jnp.float32
        )
    pair_grad = lax.psum_scatter(
        jnp.concatenate([key_grad, value_grad], axis=-1).astype(jnp.bfloat16),
        "context",
        scatter_dimension=0,
        tiled=True,
    ).astype(jnp.float32)
    query_grad = query_parts[0]
    pullback = jax.vjp(prepare, query_raw, key_raw, gain_query, gain_key)[1]
    query_back, key_back, q_gain_term, k_gain_term = pullback(
        (query_grad, pair_grad[:, :, :head_size])
    )
    projected_grad = (
        jnp.concatenate(
            [
                query_back.reshape(tok_rows, head_groups, queries_per_group, head_size),
                key_back[:, :, None],
                pair_grad[:, :, None, head_size:],
            ],
            axis=2,
        )
        .reshape(tok_rows, -1)
        .astype(jnp.bfloat16)
    )
    normed_grad = lax.psum(
        times_transposed(projected_grad, attn_in).astype(jnp.bfloat16), "tensor"
    ).astype(jnp.float32)
    w_qkv_grad = lax.psum_scatter(
        outer_rows(normalized_input, projected_grad).astype(jnp.bfloat16),
        ("fsdp", "context"),
        scatter_dimension=0,
        tiled=True,
    ).astype(jnp.float32)
    unit_back = normed_grad * gain_attn
    inputs_grad = (
        state_grad
        + inverse_attn
        * (unit_back - unit_attn * jnp.mean(unit_back * unit_attn, axis=-1, keepdims=True))
    ).astype(jnp.bfloat16)
    attn_gain_term = jnp.sum(normed_grad * unit_attn, axis=0) * first_tensor
    attn_gain_grad, q_gain_grad, k_gain_grad, moe_gain_grad, router_grad = lax.psum(
        (attn_gain_term, q_gain_term, k_gain_term, moe_gain_term, router_term),
        ("fsdp", "context", "tensor"),
    )
    return (
        output,
        inputs_grad,
        attn_gain_grad,
        w_qkv_grad,
        q_gain_grad,
        k_gain_grad,
        w_o_grad,
        moe_gain_grad,
        router_grad,
        w_experts_grad,
    )


def solution(mesh):
    return jax.shard_map(
        shards,
        mesh=mesh,
        in_specs=(
            P(("fsdp", "context"), None),
            P(),
            P(("fsdp", "context"), "tensor"),
            P(),
            P(),
            P(("fsdp", "context"), "tensor"),
            P(),
            P(),
            P(("fsdp", "context"), None, None, "tensor"),
            P("fsdp"),
            P(("fsdp", "context"), None),
            P(("fsdp", "context"), None),
        ),
        out_specs=(
            P(("fsdp", "context"), None),
            P(("fsdp", "context"), None),
            P(),
            P(("fsdp", "context"), "tensor"),
            P(),
            P(),
            P(("fsdp", "context"), "tensor"),
            P(),
            P(),
            P(("fsdp", "context"), None, None, "tensor"),
        ),
        check_vma=False,
    )
```

profile of v0, /device:TPU:0, one launch (start us, length us, event | category | flops | bytes accessed | tf_op | source)
XLA Modules:
  0.0 2946.0 jit_solution(903376558071003758)
XLA Ops:
  18.1 81.1 %all-gather.4.cloned.1.call-done = bf16[2048,1280]{1,0:T(8,128)(2,1)} async-done(((bf16[256,1280]{1,0:T(8,128)(2,1)}), bf16[2048,1280]{1,0:T(8,128)(2,1)}) %all-gather.4.cloned.1.call-update) | async-done | bytes 5242896 | tf_op jit(solution)/shard_map/all_gather | solution.py:98
  230.1 33.7 %all-reduce.11.cloned.1.call-done = f32[512,2048]{1,0:T(8,128)} async-done(((f32[512,2048]{1,0:T(8,128)}), f32[512,2048]{1,0:T(8,128)}) %all-reduce.11.cloned.1.call-update) | async-done | bytes 4194320 | tf_op jit(solution)/shard_map/psum | solution.py:149
  291.1 33.0 %gather_fusion.1 = f32[4096]{0:T(1024)S(1)} fusion(f32[512,16]{0,1:T(8,128)S(1)} %fusion.100, s32[4096]{0:T(1024)S(1)} %reshape.749), kind=kCustom, calls=%fused_computation.5 | custom fusion | bytes 65536 | tf_op jit(solution)/shard_map/jit(take_along_axis)/gather | solution.py:155
  346.4 871.3 %all-gather.8.cloned.1.call-done = bf16[2048,16,3,192]{3,0,1,2:T(8,128)(2,1)} async-done(((bf16[256,16,3,192]{3,0,1,2:T(8,128)(2,1)}), bf16[2048,16,3,192]{3,0,1,2:T(8,128)(2,1)}) %all-gather.8.cloned.1.call-update) | async-done | bytes 37748752 | tf_op jit(solution)/shard_map/all_gather | solution.py:158
  1217.7 32.4 %slice_bitcast_fusion = (bf16[16,2,192,2048]{2,3,0,1:T(8,128)(2,1)}, bf16[16,2048,2,192]{3,1,0,2:T(8,128)(2,1)}) fusion(bf16[2048,16,3,192]{3,0,1,2:T(8,128)(2,1)} %all-gather.8.cloned.1.call-done), kind=kLoop, calls=%fused_computation.11 | loop fusion | bytes 75497472 | tf_op jit(solution)/shard_map/transpose | solution.py:224
  1250.1 40.2 %copy.169 = bf16[16,2048,2,192]{1,3,2,0:T(8,128)(2,1)} copy(bf16[16,2048,2,192]{3,1,0,2:T(8,128)(2,1)} %get-tuple-element.79) | data formatting | bytes 50331648 | tf_op jit(solution)/shard_map/transpose | solution.py:168
  1290.3 32.6 %copy.170 = bf16[16,2048,384]{2,1,0:T(8,128)(2,1)} copy(bf16[16,2048,384]{1,2,0:T(8,128)(2,1)} %bitcast.224) | data formatting | bytes 50331648 | tf_op jit(solution)/shard_map/reshape | solution.py:168
  1471.1 25.6 gather_fusion.5
  1505.0 23.0 gather_fusion.2
  1584.9 40.4 %copy.177 = bf16[16,2,192,2048]{3,2,1,0:T(8,128)(2,1)} copy(bf16[16,2,192,2048]{2,3,0,1:T(8,128)(2,1)} %get-tuple-element.78) | data formatting | bytes 50331648 | tf_op jit(solution)/shard_map/transpose | solution.py:224
  1627.0 23.3 ragged-dot-none.2
  1652.1 27.1 ragged-dot-none.4
  1679.2 29.4 scatter_custom_fusion.2
  1708.5 31.3 %scatter_fusion = f32[512,2048]{1,0:T(8,128)} fusion(f32[512,2048]{1,0:T(8,128)} %scatter_custom_fusion.2, s32[2048]{0:T(1024)S(1)} %copy-done.74, f32[2048,2048]{1,0:T(8,128)} %ragged-dot-none.2), kind=kCustom, calls=%fused_computation.9 | custom fusion | flops 4194304 | bytes 50339840 | tf_op jit(solution)/shard_map/scatter-add | solution.py:250
  1740.6 30.9 %scatter_custom_fusion = f32[512,2048]{1,0:T(8,128)} fusion(s32[2048]{0:T(1024)} %get-tuple-element.106, f32[2048,2048]{1,0:T(8,128)} %ragged-dot-none.8, f32[2048]{0:T(1024)S(1)} %get-tuple-element.102, f32[]{:T(128)} %constant.65.clone.1), kind=kCustom, calls=%fused_computation.32 | custom fusion | flops 8388608 | bytes 20980224 | tf_op jit(solution)/shard_map/scatter-add | solution.py:194
  1771.7 33.3 %scatter_custom_fusion.1 = f32[512,2048]{1,0:T(8,128)} fusion(f32[512,2048]{1,0:T(8,128)} %scatter_custom_fusion, s32[2048]{0:T(1024)S(1)} %copy-done.74, f32[2048,2048]{1,0:T(8,128)} %ragged-dot-none.6, f32[2048]{0:T(1024)S(1)} %copy-done.65), kind=kCustom, calls=%fused_computation.30 | custom fusion | flops 8388608 | bytes 20979712 | tf_op jit(solution)/shard_map/scatter-add | solution.py:194
  1940.1 51.5 %ragged-dot-none.1 = f32[16,2048,384]{2,1,0:T(8,128)} custom-call(s32[1]{0:T(128)} %get-tuple-element.20, s32[17]{0:T(128)} %get-tuple-element.21, s32[31]{0:T(128)} %get-tuple-element.22, s32[31]{0:T(128)} %get-tuple-element.23, s32[1]{0:T(128)} %get-tuple-element.20, bf16[4096,2048]{1,0:T(8,128)(2,1)} %copy-done.5, bf16[4096,384]{1,0:T(8,128)(2,1)} %maximum_maximum_fusion), custom_call_target="tpu_custom_call" | custom-call | flops 6442450944 | bytes 70254656 | tf_op jit(solution)/shard_map/ragged_dot_general/ragged-dot-none
  1991.6 25.9 convert.64
  2017.5 33.0 %copy.190 = bf16[16,2048,384]{1,2,0:T(8,128)(2,1)} copy(bf16[16,2048,384]{2,1,0:T(8,128)(2,1)} %convert.64) | data formatting | bytes 50331648 | tf_op jit(solution)/shard_map/convert.6
  2066.0 43.4 %ragged-dot-none = f32[16,2048,192]{2,1,0:T(8,128)} custom-call(s32[1]{0:T(128)} %get-tuple-element.20, s32[17]{0:T(128)} %get-tuple-element.21, s32[31]{0:T(128)} %get-tuple-element.22, s32[31]{0:T(128)} %get-tuple-element.23, s32[1]{0:T(128)} %get-tuple-element.20, bf16[4096,2048]{1,0:T(8,128)(2,1)} %pad_maximum_fusion, bf16[4096,192]{1,0:T(8,128)(2,1)} %pad_maximum_fusion.1), custom_call_target="tpu_custom_call" | custom-call | flops 3221225472 | bytes 43515968 | tf_op jit(solution)/shard_map/ragged_dot_general/ragged-dot-none
  2147.6 25.7 maximum_bitcast_fusion
  2187.0 41.9 %all-reduce.4 = (f32[2048]{0:T(1024)}, f32[128]{0:T(128)}, f32[128]{0:T(128)}, f32[2048]{0:T(1024)}) all-reduce(f32[2048]{0:T(1024)S(1)} %broadcast_multiply_fusion.1, f32[128]{0:T(128)S(1)} %copy-done.96, f32[128]{0:T(128)S(1)} %copy-done.95, ...), channel_id=1, replica_groups=mesh['fsdp'=4,'context'=2,'tensor'=4] {'fsdp','context','tensor'}, use_global_device_ids=true, to_apply=%region_33.36 | all-reduce | flops 4352 | bytes 34816 | tf_op jit(solution)/shard_map/psum | solution.py:371
  2233.3 576.7 %reduce-scatter.11.cloned.1.call-done = bf16[256,16,3,192]{0,3,2,1:T(8,128)(2,1)} async-done(((bf16[2048,16,3,192]{0,3,2,1:T(8,128)(2,1)}), bf16[256,16,3,192]{0,3,2,1:T(8,128)(2,1)}) %reduce-scatter.11.cloned.1.call-update) | async-done | bytes 4718608 | tf_op jit(solution)/shard_map/reduce_scatter | solution.py:280
  2817.3 120.4 %all-reduce.15.cloned.1.call-done = f32[2048,16]{0,1:T(8,128)} async-done(((f32[2048,16]{0,1:T(8,128)}), f32[2048,16]{0,1:T(8,128)}) %all-reduce.15.cloned.1.call-update) | async-done | bytes 131088 | tf_op jit(solution)/shard_map/psum | solution.py:371
  (390 shorter events, 623.6 us)
Async XLA Ops:
  7.2 283.3 %copy-start = (bf16[2048,16]{0,1:T(8,128)(2,1)S(1)}, bf16[2048,16]{0,1:T(8,128)(2,1)}, u32[]{:S(2)}) copy-start(bf16[2048,16]{0,1:T(8,128)(2,1)} %param.23) | copy-start | bytes 196612
  7.2 92.0 %all-gather.4.cloned.1.call-start = ((), (), s32[]{:S(2)}) async-start(), calls=%async_computation.4 | async-start | bytes 5898240 | tf_op jit(solution)/shard_map/all_gather | solution.py:98
  7.9 165.0 %all-gather.6.cloned.1.call-start = ((), (), s32[]{:S(2)}) async-start(), calls=%async_computation.5 | async-start | bytes 4718592 | tf_op jit(solution)/shard_map/all_gather | solution.py:99
  8.7 255.1 %all-reduce.11.cloned.1.call-start = ((), (), s32[]{:S(2)}) async-start(), calls=%async_computation.6 | async-start | bytes 8388608 | tf_op jit(solution)/shard_map/psum | solution.py:149
  9.4 95.5 %copy-start.62 = (f32[2048]{0:T(1024)}, f32[2048]{0:T(1024)S(1)}, u32[]{:S(2)}) copy-start(f32[2048]{0:T(1024)S(1)} %convert_element_type.164) | copy-start | bytes 24580
  12.2 96.5 %copy-start.87 = (f32[128]{0:T(128)}, f32[128]{0:T(128)S(1)}, u32[]{:S(2)}) copy-start(f32[128]{0:T(128)S(1)} %convert_element_type.166) | copy-start | bytes 1540
  15.2 111.9 %copy-start.91 = (f32[128]{0:T(128)}, f32[128]{0:T(128)S(1)}, u32[]{:S(2)}) copy-start(f32[128]{0:T(128)S(1)} %convert_element_type.168) | copy-start | bytes 1540
  18.1 86.8 %copy-start.84 = (f32[512]{0:T(512)}, f32[512]{0:T(512)S(1)}, u32[]{:S(2)}) copy-start(f32[512]{0:T(512)S(1)} %add_rsqrt_fusion.1) | copy-start | bytes 6148
  179.6 1038.1 %all-gather.8.cloned.1.call-start = ((), (), s32[]{:S(2)}) async-start(), calls=%async_computation.7 | async-start | bytes 56623104 | tf_op jit(solution)/shard_map/all_gather | solution.py:158
  187.7 1637.9 %all-reduce.13.cloned.1.call-start = ((), (), s32[]{:S(2)}) async-start(), calls=%async_computation.8 | async-start | bytes 8388608 | tf_op jit(solution)/shard_map/psum | solution.py:286
  188.4 78.9 %copy-start.58 = (f32[2048]{0:T(1024)}, f32[2048]{0:T(1024)S(1)}, u32[]{:S(2)}) copy-start(f32[2048]{0:T(1024)S(1)} %convert_element_type.175) | copy-start | bytes 24580
  194.4 34.4 %copy-start.48 = (s32[4096]{0:T(1024)}, s32[4096]{0:T(1024)S(1)}, u32[]{:S(2)}) copy-start(s32[4096]{0:T(1024)S(1)} %get-tuple-element.14) | copy-start | bytes 49156
  227.9 39.3 %copy-start.67 = (s32[4096]{0:T(1024)}, s32[4096]{0:T(1024)S(1)}, u32[]{:S(2)}) copy-start(s32[4096]{0:T(1024)S(1)} %get-tuple-element.15) | copy-start | bytes 49156
  291.1 34.0 %copy-start.86 = (pred[4096]{0:T(1024)(128)(4,1)S(1)}, pred[4096]{0:T(1024)(128)(4,1)}, u32[]{:S(2)}) copy-start(pred[4096]{0:T(1024)(128)(4,1)} %get-tuple-element.74) | copy-start | bytes 12292
  1471.1 33.9 %copy-start.71 = (s32[4096]{0:T(1024)S(1)}, s32[4096]{0:T(1024)}, u32[]{:S(2)}) copy-start(s32[4096]{0:T(1024)} %fusion.86) | copy-start | bytes 49156
  1584.9 40.4 %copy-start.22 = (bf16[2048,192]{1,0:T(8,128)(2,1)S(1)}, bf16[2048,192]{1,0:T(8,128)(2,1)}, u32[]{:S(2)}) copy-start(bf16[2048,192]{1,0:T(8,128)(2,1)} %get-tuple-element.86) | copy-start | bytes 2359300
  1584.9 40.4 %copy-start.24 = (bf16[2048,192]{1,0:T(8,128)(2,1)S(1)}, bf16[2048,192]{1,0:T(8,128)(2,1)}, u32[]{:S(2)}) copy-start(bf16[2048,192]{1,0:T(8,128)(2,1)} %get-tuple-element.87) | copy-start | bytes 2359300
  1739.9 168.1 %reduce-scatter.5.cloned.1.call-start = ((), (), s32[]{:S(2)}) async-start(), calls=%async_computation.9 | async-start | bytes 786432 | tf_op jit(solution)/shard_map/reduce_scatter | solution.py:332
  1771.7 53.8 %copy-start.41 = (bf16[512,16]{1,0:T(8,128)(2,1)}, bf16[512,16]{1,0:T(8,128)(2,1)S(1)}, u32[]{:S(2)}) copy-start(bf16[512,16]{1,0:T(8,128)(2,1)S(1)} %copy.200) | copy-start | bytes 49156
  1893.0 283.0 %all-reduce.17.cloned.1.call-start = ((), (), s32[]{:S(2)}) async-start(), calls=%async_computation.14 | async-start | bytes 8388608 | tf_op jit(solution)/shard_map/psum | solution.py:206
  1919.3 309.6 %reduce-scatter.9.cloned.1.call-start = ((), (), s32[]{:S(2)}) async-start(), calls=%async_computation.11 | async-start | bytes 4718592 | tf_op jit(solution)/shard_map/reduce_scatter | solution.py:296
  1927.1 303.9 %reduce-scatter.7.cloned.1.call-start = ((), (), s32[]{:S(2)}) async-start(), calls=%async_computation.10 | async-start | bytes 5898240 | tf_op jit(solution)/shard_map/reduce_scatter | solution.py:358
  1933.9 876.1 %reduce-scatter.11.cloned.1.call-start = ((), (), s32[]{:S(2)}) async-start(), calls=%async_computation.13 | async-start | bytes 42467328 | tf_op jit(solution)/shard_map/reduce_scatter | solution.py:280
  2173.4 764.3 %all-reduce.15.cloned.1.call-start = ((), (), s32[]{:S(2)}) async-start(), calls=%async_computation.12 | async-start | bytes 262144 | tf_op jit(solution)/shard_map/psum | solution.py:371
  (90 other events, 1069.5 us)
Sparse Core Ops, SparseCore 0:
  10.2 88.9 all-gather.3
  101.3 71.5 all-gather.5
  179.7 84.0 all-reduce.10
  265.2 952.4 all-gather.7
  1740.0 85.5 all-reduce.12
  1893.2 14.7 reduce-scatter.4
  1919.5 85.6 all-reduce.16
  2008.8 88.0 reduce-scatter.8
  2100.9 102.2 reduce-scatter.6
  2207.5 602.4 reduce-scatter.10
  2816.1 121.5 all-reduce.14
where the time goes:
time: 2960 us; the launch traced here: 2950 us
  waiting for transfers between devices  1730 us (58%)
  local copies, waits for them, and re-layouts  422 us (14%)
  other arithmetic  368 us (12%)
  Pallas kernels  269 us (9%)
  matrix products  83 us (3%)
  blocking collectives  57 us (2%)
    all_gather x1, waiting for transfers between devices, shards(): lax.all_gather(w_experts, ('fsdp', 'context'), axis=0, tiled=True)  871 us
    reduce_scatter x1, waiting for transfers between devices, shards(): lax.psum_scatter(jnp.transpose(stacked, (1, 0, 2, 3)).astype(jnp.bfloat16...  577 us
    another operation x10, Pallas kernels  264 us
    psum x1, waiting for transfers between devices, shards(): lax.psum((attn_gain_term, q_gain_term, k_gain_term, moe_gain_term, router...  120 us
    all_gather x1, waiting for transfers between devices, shards(): lax.all_gather(joined_projection_weight, ('fsdp', 'context'), axis=0, til...  81.1 us
    transpose x2, local copies, waits for them, and re-layouts, shards(): jnp.transpose(expert_all[:, :, :2], (1, 2, 3, 0))  72.8 us
    scatter-add x2, other arithmetic, shards(): moe_part.at[slab_tokens]  64.2 us
    scatter-add x2, other arithmetic, shards(): back_part.at[slab_tokens]  60.7 us
  transfers between devices with their start and end apart: 11, of which 8 were waited for; matrix products, arithmetic and copies ran while one was open for 14% of the time, Pallas kernels for 3%

commit v1 on v0

--- a/solution.py
+++ b/solution.py
@@ -1,6 +1,10 @@
+import functools
+
 import jax
 import jax.numpy as jnp
 from jax import lax
+from jax.experimental import pallas as pl
+from jax.experimental.pallas import tpu as pltpu
 from jax.sharding import PartitionSpec as P
 
 QUERY_HEADS = 32
@@ -386,9 +390,658 @@
     )
 
 
+SPREAD = ("fsdp", "context")
+VMEM_BYTES = 60 * 2**20
+
+
+def flip_pairs(size, bit):
+    return [(place, place ^ bit) for place in range(size)]
+
+
+def flip(array, name, bit):
+    return lax.ppermute(array, name, flip_pairs(lax.axis_size(name), bit))
+
+
+def add_low(left_side, right_side):
+    return (left_side.astype(jnp.float32) + right_side.astype(jnp.float32)).astype(jnp.bfloat16)
+
+
+def partner_bits():
+    size = lax.axis_size("tensor")
+    return [size >> step for step in range(1, size.bit_length())]
+
+
+def partner_order():
+    order = [0]
+    for bit in partner_bits():
+        order = order + [offset ^ bit for offset in order]
+    return order
+
+
+def own_first(array):
+    place = lax.axis_index("tensor")
+    rows = array.shape[0] // lax.axis_size("tensor")
+    return jnp.concatenate(
+        [
+            lax.dynamic_slice_in_dim(array, (place ^ offset) * rows, rows)
+            for offset in partner_order()
+        ],
+        axis=0,
+    )
+
+
+def own_back(array):
+    place = lax.axis_index("tensor")
+    order = partner_order()
+    rows = array.shape[0] // len(order)
+    slot_of = jnp.array([order.index(offset) for offset in range(len(order))], jnp.int32)
+    return jnp.concatenate(
+        [
+            lax.dynamic_slice_in_dim(array, slot_of[place ^ block] * rows, rows)
+            for block in range(len(order))
+        ],
+        axis=0,
+    )
+
+
+def tensor_gather_rows(piece):
+    for bit in partner_bits():
+        piece = jnp.concatenate([piece, flip(piece, "tensor", bit)], axis=0)
+    return piece
+
+
+def tensor_scatter_rows(half_of):
+    bits = partner_bits()
+    theirs = flip(half_of(1), "tensor", bits[-1])
+    total = add_low(half_of(0), theirs)
+    for bit in bits[-2::-1]:
+        rows = total.shape[0] // 2
+        total = add_low(total[:rows], flip(total[rows:], "tensor", bit))
+    return total
+
+
+def split_halves(array, axis, place):
+    mine = lax.dynamic_index_in_dim(array, place, axis, keepdims=False)
+    theirs = lax.dynamic_index_in_dim(array, 1 - place, axis, keepdims=False)
+    return mine, theirs
+
+
+def spread_scatter(array):
+    fsdp_size, place = lax.axis_size("fsdp"), lax.axis_index("context")
+    blocks = array.reshape(fsdp_size, 2, -1, array.shape[1])
+    mine, theirs = split_halves(blocks, 1, place)
+    summed = add_low(mine, flip(theirs, "context", 1))
+    parts = lax.all_to_all(summed, "fsdp", 0, 0, tiled=True)
+    return jnp.sum(parts.astype(jnp.float32), axis=0)
+
+
+def spread_gather(piece):
+    fsdp_size, place = lax.axis_size("fsdp"), lax.axis_index("context")
+    sent = jnp.broadcast_to(piece[None], (fsdp_size,) + piece.shape)
+    column = lax.all_to_all(sent, "fsdp", 0, 0, tiled=True)
+    other = flip(column, "context", 1)
+    first = jnp.where(place == 0, column, other)
+    second = jnp.where(place == 0, other, column)
+    return jnp.stack([first, second], axis=1).reshape(-1, piece.shape[1])
+
+
+def sum_everywhere(array):
+    for name in ("tensor", "context", "fsdp"):
+        bit = 1
+        while bit < lax.axis_size(name):
+            array = array + flip(array, name, bit)
+            bit *= 2
+    return array
+
+
+def nt_dot(left_side, right_side):
+    return lax.dot_general(
+        left_side, right_side, (((1,), (1,)), ((), ())), preferred_element_type=jnp.float32
+    )
+
+
+def nn_dot(left_side, right_side):
+    return jnp.dot(left_side, right_side, preferred_element_type=jnp.float32)
+
+
+def unit_rows(raw):
+    inverse = lax.rsqrt(jnp.mean(raw * raw, axis=-1, keepdims=True) + EPSILON)
+    return raw * inverse, inverse
+
+
+def turn(array, half_size):
+    return pltpu.roll(array, half_size, 1)
+
+
+def attend_kernel(scale, raw_ref, cosine_ref, sine_ref, gain_ref, key_ref, value_ref, bias_ref, out_ref):
+    half_size = raw_ref.shape[1] // 2
+    unit, _ = unit_rows(raw_ref[...])
+    scaled = unit * gain_ref[...]
+    query = scaled * cosine_ref[...] + turn(scaled, half_size) * sine_ref[...]
+    scores = nt_dot(key_ref[...], query.astype(jnp.bfloat16)) * scale + bias_ref[...]
+    raised = jnp.exp(scores - jnp.max(scores, axis=0, keepdims=True))
+    probs = (raised / jnp.sum(raised, axis=0, keepdims=True)).astype(jnp.bfloat16)
+    out_ref[...] = nn_dot(value_ref[...], probs).T.astype(jnp.bfloat16)
+
+
+def attend(projected, cosine, sine, gain, keys, values_turned, bias, heads, scale):
+    rows, size = cosine.shape
+    length = keys.shape[0]
+    whole = lambda shape: pl.BlockSpec(shape, lambda head: (0, 0))
+    by_head = pl.BlockSpec((rows, size), lambda head: (0, head))
+    return pl.pallas_call(
+        functools.partial(attend_kernel, scale),
+        grid=(heads,),
+        in_specs=[
+            by_head,
+            whole((rows, size)),
+            whole((rows, size)),
+            whole((1, size)),
+            whole((length, size)),
+            whole((size, length)),
+            whole((length, rows)),
+        ],
+        out_specs=by_head,
+        out_shape=jax.ShapeDtypeStruct((rows, heads * size), jnp.bfloat16),
+        compiler_params=pltpu.CompilerParams(vmem_limit_bytes=VMEM_BYTES),
+        cost_estimate=pl.CostEstimate(
+            flops=8 * heads * rows * length * size,
+            bytes_accessed=8 * heads * rows * size + 4 * rows * length,
+            transcendentals=heads * rows * length,
+        ),
+        name="attend",
+    )(projected, cosine, sine, gain, keys, values_turned, bias)
+
+
+def attend_back_kernel(
+    scale,
+    raw_ref,
+    cosine_ref,
+    sine_ref,
+    gain_ref,
+    key_ref,
+    key_turned_ref,
+    value_ref,
+    bias_ref,
+    grad_ref,
+    raw_grad_ref,
+    key_grad_ref,
+    value_grad_ref,
+    gain_grad_ref,
+):
+    half_size = raw_ref.shape[1] // 2
+    first = pl.program_id(0) == 0
+    unit, inverse = unit_rows(raw_ref[...])
+    scaled = unit * gain_ref[...]
+    query = (scaled * cosine_ref[...] + turn(scaled, half_size) * sine_ref[...]).astype(
+        jnp.bfloat16
+    )
+    out_grad = grad_ref[...]
+    scores = nt_dot(key_ref[...], query) * scale + bias_ref[...]
+    raised = jnp.exp(scores - jnp.max(scores, axis=0, keepdims=True))
+    probs = raised / jnp.sum(raised, axis=0, keepdims=True)
+    prob_grad = nt_dot(value_ref[...], out_grad)
+    weighted = probs * prob_grad
+    score_grad = (weighted - probs * jnp.sum(weighted, axis=0, keepdims=True)).astype(jnp.bfloat16)
+    key_part = nn_dot(score_grad, query) * scale
+    value_part = nn_dot(probs.astype(jnp.bfloat16), out_grad)
+    query_grad = (nn_dot(key_turned_ref[...], score_grad) * scale).T
+    scaled_grad = query_grad * cosine_ref[...] + turn(query_grad * sine_ref[...], half_size)
+    gain_part = jnp.sum(
+        (scaled_grad * unit).reshape(-1, 8, scaled_grad.shape[1]), axis=0
+    )
+    unit_grad = scaled_grad * gain_ref[...]
+    raw_grad = inverse * (unit_grad - unit * jnp.mean(unit_grad * unit, axis=-1, keepdims=True))
+    raw_grad_ref[...] = raw_grad.astype(jnp.bfloat16)
+
+    @pl.when(first)
+    def _():
+        key_grad_ref[...] = key_part
+        value_grad_ref[...] = value_part
+        gain_grad_ref[...] = gain_part
+
+    @pl.when(jnp.logical_not(first))
+    def _():
+        key_grad_ref[...] += key_part
+        value_grad_ref[...] += value_part
+        gain_grad_ref[...] += gain_part
+
+
+def attend_back(projected, cosine, sine, gain, keys, values, bias, grads, heads, scale):
+    rows, size = cosine.shape
+    length = keys.shape[0]
+    whole = lambda shape: pl.BlockSpec(shape, lambda head: (0, 0))
+    by_head = pl.BlockSpec((rows, size), lambda head: (0, head))
+    return pl.pallas_call(
+        functools.partial(attend_back_kernel, scale),
+        grid=(heads,),
+        in_specs=[
+            by_head,
+            whole((rows, size)),
+            whole((rows, size)),
+            whole((1, size)),
+            whole((length, size)),
+            whole((size, length)),
+            whole((length, size)),
+            whole((length, rows)),
+            by_head,
+        ],
+        out_specs=[by_head, whole((length, size)), whole((length, size)), whole((8, size))],
+        out_shape=[
+            jax.ShapeDtypeStruct((rows, heads * size), jnp.bfloat16),
+            jax.ShapeDtypeStruct((length, size), jnp.float32),
+            jax.ShapeDtypeStruct((length, size), jnp.float32),
+            jax.ShapeDtypeStruct((8, size), jnp.float32),
+        ],
+        compiler_params=pltpu.CompilerParams(vmem_limit_bytes=VMEM_BYTES),
+        cost_estimate=pl.CostEstimate(
+            flops=20 * heads * rows * length * size,
+            bytes_accessed=8 * heads * rows * size + 4 * rows * length,
+            transcendentals=heads * rows * length,
+        ),
+        name="attend_back",
+    )(projected, cosine, sine, gain, keys, keys.T, values, bias, grads)
+
+
+def experts_kernel(
+    local_experts,
+    chunks,
+    gate_lanes,
+    first_ref,
+    token_ref,
+    gate_ref,
+    grad_ref,
+    weight_ref,
+    result_ref,
+    back_ref,
+    active_ref,
+    slope_ref,
+    result_sum,
+    back_sum,
+    dot_sum,
+):
+    chunk = pl.program_id(1)
+    expert = first_ref[0] + lax.rem(chunk, local_experts)
+    units = weight_ref.shape[2]
+    width = token_ref.shape[1]
+    inward = weight_ref[0, :2].reshape(2 * units, width)
+    outward = weight_ref[0, 2]
+    gate_up = nt_dot(token_ref[...], inward)
+    down_back = nt_dot(grad_ref[...], outward)
+    lanes = lax.broadcasted_iota(jnp.int32, gate_ref.shape, 1)
+    here = (lanes == expert) | (lanes == expert + gate_lanes)
+    gate = jnp.sum(
+        jnp.where(here, gate_ref[...].astype(jnp.float32), 0.0), axis=-1, keepdims=True
+    )
+    gate_half, up_half = gate_up[:, :units], gate_up[:, units:]
+    sigmoid = jax.nn.sigmoid(gate_half)
+    silu = gate_half * sigmoid
+    active = silu * up_half
+    scaled_active = active * gate
+    act_grad = down_back * gate
+    gate_slope = act_grad * up_half * (sigmoid + silu * (1.0 - sigmoid))
+    slopes = jnp.concatenate([gate_slope, act_grad * silu], axis=1)
+    gate_dot = jnp.sum(active * down_back, axis=-1, keepdims=True)
+    dots = jnp.where(lanes == expert, gate_dot, 0.0)
+    low_active = scaled_active.astype(jnp.bfloat16)
+    low_slopes = slopes.astype(jnp.bfloat16)
+    active_ref[...] = low_active.T
+    slope_ref[...] = low_slopes.T
+    result = nn_dot(low_active, outward)
+    back = nn_dot(low_slopes, inward)
+
+    @pl.when(chunk == 0)
+    def _():
+        result_sum[...] = result
+        back_sum[...] = back
+        dot_sum[...] = dots
+
+    @pl.when((chunk > 0) & (chunk < chunks - 1))
+    def _():
+        result_sum[...] += result
+        back_sum[...] += back
+        dot_sum[...] += dots
+
+    @pl.when(chunk == chunks - 1)
+    def _():
+        result_ref[...] = (result_sum[...] + result).astype(jnp.bfloat16)
+        back_ref[:, :width] = (back_sum[...] + back).astype(jnp.bfloat16)
+        back_ref[:, width:] = (dot_sum[...] + dots).astype(jnp.bfloat16)
+
+
+def run_experts(first_expert, tokens, grads, weights, local_experts, gate_lanes):
+    rows, width = grads.shape
+    lanes = tokens.shape[1] - width
+    chunks, _, units, _ = weights.shape
+    block = min(512, rows)
+    return pl.pallas_call(
+        functools.partial(experts_kernel, local_experts, chunks, gate_lanes),
+        grid_spec=pltpu.PrefetchScalarGridSpec(
+            num_scalar_prefetch=1,
+            grid=(rows // block, chunks),
+            in_specs=[
+                pl.BlockSpec((block, width), lambda row, chunk, first: (row, 0)),
+                pl.BlockSpec((block, lanes), lambda row, chunk, first: (row, width // lanes)),
+                pl.BlockSpec((block, width), lambda row, chunk, first: (row, 0)),
+                pl.BlockSpec((1, 3, units, width), lambda row, chunk, first: (chunk, 0, 0, 0)),
+            ],
+            out_specs=[
+                pl.BlockSpec((block, width), lambda row, chunk, first: (row, 0)),
+                pl.BlockSpec((block, width + lanes), lambda row, chunk, first: (row, 0)),
+                pl.BlockSpec((units, block), lambda row, chunk, first: (chunk, row)),
+                pl.BlockSpec((2 * units, block), lambda row, chunk, first: (chunk, row)),
+            ],
+            scratch_shapes=[
+                pltpu.VMEM((block, width), jnp.float32),
+                pltpu.VMEM((block, width), jnp.float32),
+                pltpu.VMEM((block, lanes), jnp.float32),
+            ],
+        ),
+        out_shape=[
+            jax.ShapeDtypeStruct((rows, width), jnp.bfloat16),
+            jax.ShapeDtypeStruct((rows, width + lanes), jnp.bfloat16),
+            jax.ShapeDtypeStruct((chunks * units, rows), jnp.bfloat16),
+            jax.ShapeDtypeStruct((2 * chunks * units, rows), jnp.bfloat16),
+        ],
+        compiler_params=pltpu.CompilerParams(vmem_limit_bytes=VMEM_BYTES),
+        cost_estimate=pl.CostEstimate(
+            flops=12 * rows * width * chunks * units,
+            bytes_accessed=2 * weights.size * (rows // block) + 10 * rows * width,
+            transcendentals=rows * chunks * units,
+        ),
+        name="experts",
+    )(first_expert.reshape(1), tokens, tokens, grads, weights)
+
+
+def expert_grads_kernel(local_experts, sides, slope_ref, active_ref, token_ref, grad_ref, out_ref):
+    hidden_units = active_ref.shape[0] // (local_experts * sides)
+    inward = nn_dot(slope_ref[...], token_ref[...]).astype(jnp.bfloat16)
+    outward = nn_dot(active_ref[...], grad_ref[...]).astype(jnp.bfloat16)
+    for expert in range(local_experts):
+        for side in range(sides):
+            for kind in range(3):
+                place = ((side * local_experts + expert) * 3 + kind) * hidden_units
+                if kind < 2:
+                    start = ((expert * 2 + kind) * sides + side) * hidden_units
+                    rows = inward[start : start + hidden_units]
+                else:
+                    start = (expert * sides + side) * hidden_units
+                    rows = outward[start : start + hidden_units]
+                out_ref[0, place : place + hidden_units] = rows
+
+
+def expert_grads(part, slopes, actives, tokens, grads, local_experts, sides, blocks):
+    rows, width = grads.shape
+    block = width // blocks
+    units = actives.shape[0] // 2
+    return pl.pallas_call(
+        functools.partial(expert_grads_kernel, local_experts, sides),
+        grid=(blocks,),
+        in_specs=[
+            pl.BlockSpec((2 * units, rows), lambda column: (part, 0)),
+            pl.BlockSpec((units, rows), lambda column: (part, 0)),
+            pl.BlockSpec((rows, block), lambda column: (0, column)),
+            pl.BlockSpec((rows, block), lambda column: (0, column)),
+        ],
+        out_specs=pl.BlockSpec((1, 3 * units, block), lambda column: (column, 0, 0)),
+        out_shape=jax.ShapeDtypeStruct((blocks, 3 * units, block), jnp.bfloat16),
+        compiler_params=pltpu.CompilerParams(vmem_limit_bytes=VMEM_BYTES),
+        cost_estimate=pl.CostEstimate(
+            flops=6 * units * rows * width,
+            bytes_accessed=6 * units * (rows + width) + 4 * rows * width,
+            transcendentals=0,
+        ),
+        name="expert_grads",
+    )(slopes, actives, tokens, grads)
+
+
+def expert_parallel_shards(
+    inputs,
+    attn_gain,
+    joined_projection_weight,
+    q_gain,
+    k_gain,
+    w_o,
+    moe_gain,
+    router,
+    w_experts,
+    segments,
+    experts,
+    out_grad,
+):
+    tok_rows, model_width = inputs.shape
+    head_size = q_gain.shape[0]
+    half_size = head_size // 2
+    tensor_size = lax.axis_size("tensor")
+    heads = QUERY_HEADS // KEY_VALUE_HEADS
+    expert_count = router.shape[1]
+    spread_size = lax.axis_size(SPREAD)
+    local_experts = expert_count // spread_size
+    hidden_units = w_experts.shape[3]
+    slice_rows = w_experts.shape[0]
+    own_rows = tok_rows // tensor_size
+    sides = tensor_size // 2
+    context_place = lax.axis_index("context")
+    own_start = lax.axis_index("tensor") * own_rows
+    first_expert = lax.axis_index(SPREAD) * local_experts
+    gain_attn = attn_gain.astype(jnp.float32)
+    gain_moe = moe_gain.astype(jnp.float32)
+    gain_query = q_gain.astype(jnp.float32)[None]
+    gain_key = k_gain.astype(jnp.float32)
+    score_scale = head_size ** (-0.5)
+
+    attn_in = lax.all_gather(joined_projection_weight, SPREAD, axis=0, tiled=True)
+    attn_out = lax.all_gather(w_o, SPREAD, axis=0, tiled=True)
+    own_grad = lax.dynamic_slice_in_dim(out_grad, own_start, own_rows)
+    all_grads = spread_gather(own_grad)
+
+    sent_weights = jnp.transpose(w_experts, (1, 2, 3, 0)).reshape(
+        spread_size, local_experts, 3, hidden_units, slice_rows
+    )
+    expert_weights = []
+    for expert in range(local_experts):
+        own_part = lax.all_to_all(sent_weights[:, expert], SPREAD, 0, 0, tiled=True)
+        side_parts = own_part[None]
+        for bit in partner_bits()[:-1]:
+            side_parts = jnp.concatenate([side_parts, flip(side_parts, "tensor", bit)], axis=0)
+        expert_weights.append(jnp.stack([side_parts, flip(side_parts, "tensor", 1)]))
+    weights = (
+        jnp.stack(expert_weights, axis=1)
+        .transpose(0, 1, 4, 2, 5, 3, 6)
+        .reshape(2 * local_experts, 3, sides * hidden_units, model_width)
+    )
+
+    ordered = own_first(inputs)
+    own_index = own_first(jnp.arange(tok_rows, dtype=jnp.int32))
+    own_tokens = context_place * tok_rows + own_index
+    all_tokens = jnp.concatenate([own_tokens, (1 - context_place) * tok_rows + own_index])
+    token_segments = jnp.take(segments, all_tokens)
+    positions = jnp.take(doc_positions(segments), own_tokens)
+    allowed = (token_segments[:, None] == token_segments[None, :tok_rows]) & (
+        all_tokens[:, None] <= own_tokens[None, :]
+    )
+    bias = jnp.where(allowed, 0.0, NEGATIVE).astype(jnp.float32)
+    inverse_angles = ROPE_THETA ** (
+        -2.0 * jnp.arange(half_size, dtype=jnp.float32) / head_size
+    )
+    angles = positions.astype(jnp.float32)[:, None] * inverse_angles[None, :]
+    cosine = jnp.concatenate([jnp.cos(angles)] * 2, axis=-1)
+    half_sine = jnp.sin(angles)
+    sine = jnp.concatenate([-half_sine, half_sine], axis=-1)
+
+    residual = ordered.astype(jnp.float32)
+    inverse_attn = lax.rsqrt(jnp.mean(residual * residual, axis=-1, keepdims=True) + EPSILON)
+    normalized_input = (residual * inverse_attn * gain_attn).astype(jnp.bfloat16)
+    projected = nn_dot(normalized_input, attn_in)
+    key_raw = projected[:, heads * head_size : (heads + 1) * head_size]
+    value_raw = projected[:, (heads + 1) * head_size :]
+
+    def prepare_key(raw, gain):
+        scaled = norm_rows(raw, gain)
+        swapped = jnp.concatenate([scaled[:, half_size:], scaled[:, :half_size]], axis=-1)
+        return scaled * cosine + swapped * sine
+
+    key_values = jnp.concatenate([prepare_key(key_raw, gain_key), value_raw], axis=-1).astype(
+        jnp.bfloat16
+    )
+    pairs = jnp.concatenate([key_values, flip(key_values, "context", 1)], axis=0)
+    keys, values = pairs[:, :head_size], pairs[:, head_size:]
+    attended = attend(
+        projected, cosine, sine, gain_query, keys, values.T, bias, heads, score_scale
+    )
+    half_rows = tok_rows // 2
+    attn_sum = tensor_scatter_rows(
+        lambda half: nt_dot(
+            attended[half * half_rows : (half + 1) * half_rows], attn_out
+        ).astype(jnp.bfloat16)
+    )
+
+    own_inputs = ordered[:own_rows].astype(jnp.float32)
+    own_experts = lax.dynamic_slice_in_dim(experts, own_start, own_rows)
+    hidden_state = own_inputs + attn_sum.astype(jnp.float32)
+    inverse_moe = lax.rsqrt(jnp.mean(hidden_state * hidden_state, axis=-1, keepdims=True) + EPSILON)
+    unit_moe = hidden_state * inverse_moe
+    mixed_in = (unit_moe * gain_moe).astype(jnp.bfloat16)
+    logits = nn_dot(mixed_in, router)
+    expert_ids = jnp.arange(expert_count, dtype=jnp.int32)
+    picked = jnp.any(own_experts[:, :, None] == expert_ids[None, None, :], axis=1)
+    peak = jnp.max(jnp.where(picked, logits, -jnp.inf), axis=-1, keepdims=True)
+    raised_gate = jnp.where(picked, jnp.exp(jnp.minimum(logits - peak, 0.0)), 0.0)
+    gate_values = raised_gate / jnp.sum(raised_gate, axis=-1, keepdims=True)
+    gate_high = gate_values.astype(jnp.bfloat16)
+    gate_low = (gate_values - gate_high.astype(jnp.float32)).astype(jnp.bfloat16)
+    lane_pad = 128 - 2 * expert_count
+    payload = jnp.concatenate(
+        [mixed_in, gate_high, gate_low, jnp.zeros((own_rows, lane_pad), jnp.bfloat16)], axis=1
+    )
+    tokens = lax.all_gather(payload, SPREAD, axis=0, tiled=True)
+
+    results, backs, actives, slopes = run_experts(
+        first_expert, tokens, all_grads, weights, local_experts, expert_count
+    )
+    back_total = lax.psum_scatter(backs, SPREAD, scatter_dimension=0, tiled=True)
+    moe_sum = spread_scatter(results)
+    own_output = (hidden_state + moe_sum).astype(jnp.bfloat16)
+    output = own_back(tensor_gather_rows(own_output))
+
+    other_part = expert_grads(
+        1, slopes, actives, tokens, all_grads, local_experts, sides, spread_size
+    )
+    own_part = expert_grads(
+        0, slopes, actives, tokens, all_grads, local_experts, sides, spread_size
+    )
+    weight_sum = add_low(own_part, flip(other_part, "tensor", 1))
+    for bit in partner_bits()[-2::-1]:
+        rows = weight_sum.shape[1] // 2
+        weight_sum = add_low(
+            weight_sum[:, :rows], flip(weight_sum[:, rows:], "tensor", bit)
+        )
+    w_experts_grad = (
+        lax.all_to_all(weight_sum, SPREAD, 0, 0, tiled=True)
+        .reshape(expert_count, 3, hidden_units, slice_rows)
+        .astype(jnp.float32)
+        .transpose(3, 0, 1, 2)
+    )
+
+    cotangent = own_grad.astype(jnp.float32)
+    gate_dot = back_total[:, model_width : model_width + expert_count].astype(jnp.float32)
+    logit_grad = (
+        gate_values * (gate_dot - jnp.sum(gate_values * gate_dot, axis=-1, keepdims=True))
+    ).astype(jnp.bfloat16)
+    router_term = outer_rows(logit_grad, mixed_in)
+    moe_back = back_total[:, :model_width].astype(jnp.float32) + nt_dot(logit_grad, router)
+    unit_grad = moe_back * gain_moe
+    state_grad = cotangent + inverse_moe * (
+        unit_grad - unit_moe * jnp.mean(unit_grad * unit_moe, axis=-1, keepdims=True)
+    )
+    moe_gain_term = jnp.sum(moe_back * unit_moe, axis=0, keepdims=True)
+    early_sums = sum_everywhere(jnp.concatenate([router_term, moe_gain_term], axis=0))
+    router_grad = early_sums[:expert_count].T
+    moe_gain_grad = early_sums[expert_count]
+    branch_grad = tensor_gather_rows(state_grad.astype(jnp.bfloat16))
+    attended_grad = nn_dot(branch_grad, attn_out).astype(jnp.bfloat16)
+    w_o_grad = spread_scatter(outer_rows(branch_grad, attended).astype(jnp.bfloat16))
+
+    query_back, key_grad, value_grad, q_gain_rows = attend_back(
+        projected, cosine, sine, gain_query, keys, values, bias, attended_grad, heads, score_scale
+    )
+    pair_grad = jnp.concatenate([key_grad, value_grad], axis=-1)
+    pair_grad = pair_grad[:tok_rows] + flip(
+        pair_grad[tok_rows:].astype(jnp.bfloat16), "context", 1
+    ).astype(jnp.float32)
+    key_back, k_gain_term = jax.vjp(prepare_key, key_raw, gain_key)[1](pair_grad[:, :head_size])
+    projected_grad = jnp.concatenate(
+        [
+            query_back,
+            key_back.astype(jnp.bfloat16),
+            pair_grad[:, head_size:].astype(jnp.bfloat16),
+        ],
+        axis=1,
+    )
+    w_qkv_grad = lax.psum_scatter(
+        outer_rows(normalized_input, projected_grad).astype(jnp.bfloat16),
+        SPREAD,
+        scatter_dimension=0,
+        tiled=True,
+    ).astype(jnp.float32)
+    normed_grad = tensor_scatter_rows(
+        lambda half: nt_dot(
+            projected_grad[half * half_rows : (half + 1) * half_rows], attn_in
+        ).astype(jnp.bfloat16)
+    ).astype(jnp.float32)
+    own_inverse = inverse_attn[:own_rows]
+    own_unit = own_inputs * own_inverse
+    unit_back = normed_grad * gain_attn
+    own_inputs_grad = (
+        state_grad
+        + own_inverse
+        * (unit_back - own_unit * jnp.mean(unit_back * own_unit, axis=-1, keepdims=True))
+    ).astype(jnp.bfloat16)
+    inputs_grad = own_back(tensor_gather_rows(own_inputs_grad))
+    attn_gain_term = jnp.sum(normed_grad * own_unit, axis=0)
+    late_sums = sum_everywhere(
+        jnp.concatenate([attn_gain_term, jnp.sum(q_gain_rows, axis=0), k_gain_term]).reshape(
+            -1, head_size
+        )
+    ).reshape(-1)
+    return (
+        output,
+        inputs_grad,
+        late_sums[:model_width],
+        w_qkv_grad,
+        late_sums[model_width : model_width + head_size],
+        late_sums[model_width + head_size :],
+        w_o_grad,
+        moe_gain_grad,
+        router_grad,
+        w_experts_grad,
+    )
+
+
+def choose_shards(mesh, arrays):
+    sizes = mesh.shape
+    spread = sizes["fsdp"] * sizes["context"]
+    tok_rows, width = arrays[0].shape
+    head_size, expert_count = arrays[3].shape[0], arrays[7].shape[1]
+    fits = (
+        expert_count % spread == 0
+        and 2 * expert_count <= 128
+        and tok_rows % (32 * sizes["tensor"]) == 0
+        and width % 128 == 0
+        and head_size % 128 == 0
+        and sizes["tensor"] == KEY_VALUE_HEADS
+        and sizes["context"] == 2
+        and sizes["fsdp"] & (sizes["fsdp"] - 1) == 0
+    )
+    return expert_parallel_shards if fits else shards
+
+
 def solution(mesh):
+    def by_shapes(*arrays):
+        return choose_shards(mesh, arrays)(*arrays)
+
     return jax.shard_map(
-        shards,
+        by_shapes,
         mesh=mesh,
         in_specs=(
             P(("fsdp", "context"), None),

time: 2960 us -> 1040 us (0.35)
  waiting for transfers between devices: 1730 us -> 534 us
  local copies, waits for them, and re-layouts: 422 us -> 105 us
  other arithmetic: 368 us -> 117 us
  Pallas kernels: 269 us -> 138 us
  starting transfers between devices: 1.24 us -> 79.2 us
  blocking collectives: 57 us -> 0 us
  matrix products: 83 us -> 39.4 us
    all_gather x3, waiting for transfers between devices: 973 us -> 168 us  [the longest x1 106 us: expert_parallel_shards(): lax.all_gather(joined_projection_weight, SPREAD, axis=0, tiled=True)]
    reduce_scatter x4 -> x2, waiting for transfers between devices: 585 us -> 58.4 us  [the longest x1 58.4 us: expert_parallel_shards(): lax.psum_scatter(backs, SPREAD, scatter_dimension=0, tiled=True)]
    ppermute x0 -> x31, waiting for transfers between devices: none -> 266 us  [flip(): return lax.ppermute(array, name, flip_pairs(lax.axis_size(name), bit))]
    another operation x10 -> x0, Pallas kernels: 264 us -> none
    psum x4 -> x0, waiting for transfers between devices: 171 us -> none  [the longest x1 120 us: shards(): lax.psum((attn_gain_term, q_gain_term, k_gain_term, moe_gain_term, router...]
    pallas_call x0 -> x5, Pallas kernels: none -> 138 us  [the longest x1 58.6 us: run_experts(): pl.pallas_call(functools.partial(experts_kernel, local_experts, chunks, g...]
    transpose x5 -> x4, local copies, waits for them, and re-layouts: 152 us -> 25.4 us  [the longest x1 23.1 us: expert_parallel_shards(): weights = jnp.stack(expert_weights, axis=1).transpose(0, 1, 4, 2, 5, 3, 6...]
    scatter-add x4 -> x0, other arithmetic: 125 us -> none  [the longest x2 64.2 us: shards(): moe_part.at[slab_tokens]]
  transfers between devices with their start and end apart: 11 -> 42, of which waited for: 8 -> 20; matrix products, arithmetic and copies ran while one was open for 14% -> 24% of each run, Pallas kernels for 3% -> 8%
where the time goes in v1:
time: 1040 us; the launch traced here: 1030 us
  waiting for transfers between devices  534 us (51%)
  Pallas kernels  138 us (13%)
  other arithmetic  117 us (11%)
  local copies, waits for them, and re-layouts  105 us (10%)
  starting transfers between devices  79.2 us (8%)
  matrix products  39.4 us (4%)
  between operations  17.8 us (2%)
    ppermute x31, waiting for transfers between devices, flip(): return lax.ppermute(array, name, flip_pairs(lax.axis_size(name), bit))  266 us
    all_gather x1, waiting for transfers between devices, expert_parallel_shards(): lax.all_gather(joined_projection_weight, SPREAD, axis=0, tiled=True)  106 us
    all_gather x1, waiting for transfers between devices, expert_parallel_shards(): attn_out = lax.all_gather(w_o, SPREAD, axis=0, tiled=True)  62.1 us
    pallas_call x1, Pallas kernels, run_experts(): pl.pallas_call(functools.partial(experts_kernel, local_experts, chunks, g...  58.6 us
    reduce_scatter x1, waiting for transfers between devices, expert_parallel_shards(): lax.psum_scatter(backs, SPREAD, scatter_dimension=0, tiled=True)  58.4 us
    ppermute x31, starting transfers between devices, flip(): return lax.ppermute(array, name, flip_pairs(lax.axis_size(name), bit))  50.4 us
    pallas_call x2, Pallas kernels, expert_grads(): pl.pallas_call(functools.partial(expert_grads_kernel, local_experts, side...  41.2 us
    all_to_all x2, waiting for transfers between devices, spread_scatter(): parts = lax.all_to_all(summed, 'fsdp', 0, 0, tiled=True)  40.2 us
  transfers between devices with their start and end apart: 42, of which 20 were waited for; matrix products, arithmetic and copies ran while one was open for 24% of the time, Pallas kernels for 8%

profile of v1, /device:TPU:0, one launch (start us, length us, event | category | flops | bytes accessed | tf_op | source)
XLA Modules:
  0.0 1029.9 jit_solution(10912697548195547980)
XLA Ops:
  34.7 106.1 %all-gather.4.cloned.1.call-done = bf16[2048,1280]{1,0:T(8,128)(2,1)} async-done(((bf16[256,1280]{1,0:T(8,128)(2,1)}), bf16[2048,1280]{1,0:T(8,128)(2,1)}) %all-gather.4.cloned.1.call-update) | async-done | bytes 5242896 | tf_op jit(solution)/shard_map/all_gather | solution.py:833
  160.9 16.1 %collective-permute-done = bf16[512,256]{1,0:T(8,128)(2,1)S(1)} collective-permute-done((bf16[512,256]{1,0:T(8,128)(2,1)S(1)}, bf16[512,256]{1,0:T(8,128)(2,1)S(1)}, u32[]{:S(2)}, u32[]{:S(2)}) %collective-permute-start) | collective-permute-done | bytes 262176 | tf_op jit(solution)/shard_map/ppermute | solution.py:402
  178.9 14.1 %attend.1 = bf16[512,1024]{1,0:T(8,128)(2,1)} custom-call(f32[512,1280]{1,0:T(8,128)} %copy-done.21, f32[512,128]{1,0:T(8,128)} %get-tuple-element.70.cosine_ref, f32[512,128]{1,0:T(8,128)} %get-tuple-element.39.sine_ref, f32[1,128]{1,0:T(1,128)} %bitcast_convert_fusion.gain_ref, bf16[1024,128]{1,0:T(8,128)(2,1)} %get-tuple-element.67.key_ref, ...), custom_call_target="tpu_custom_call" | custom-call | flops 4294967296 | bytes 6291456 | tf_op jit(solution)/shard_map/attend/pallas_call | solution.py:532
  193.0 62.1 %all-gather.6.cloned.1.call-done = bf16[2048,1024]{1,0:T(8,128)(2,1)} async-done(((bf16[256,1024]{1,0:T(8,128)(2,1)}), bf16[2048,1024]{1,0:T(8,128)(2,1)}) %all-gather.6.cloned.1.call-update) | async-done | bytes 4194320 | tf_op jit(solution)/shard_map/all_gather | solution.py:834
  290.3 40.2 %collective-permute-done.4 = bf16[1,8,3,192,256]{4,3,2,1,0:T(8,128)(2,1)} collective-permute-done((bf16[1,8,3,192,256]{4,3,2,1,0:T(8,128)(2,1)S(1)}, bf16[1,8,3,192,256]{4,3,2,1,0:T(8,128)(2,1)}, u32[]{:S(2)}, u32[]{:S(2)}) %collective-permute-start.4) | collective-permute-done | bytes 2359328 | tf_op jit(solution)/shard_map/ppermute | solution.py:402
  336.3 43.9 %collective-permute-done.6 = bf16[1,8,3,192,256]{4,3,2,1,0:T(8,128)(2,1)} collective-permute-done((bf16[1,8,3,192,256]{4,3,2,1,0:T(8,128)(2,1)}, bf16[1,8,3,192,256]{4,3,2,1,0:T(8,128)(2,1)}, u32[]{:S(2)}, u32[]{:S(2)}) %collective-permute-start.6) | collective-permute-done | bytes 2359328 | tf_op jit(solution)/shard_map/ppermute | solution.py:402
  387.9 47.3 %collective-permute-done.3 = bf16[4,128,2048]{2,1,0:T(8,128)(2,1)} collective-permute-done((bf16[4,128,2048]{2,1,0:T(8,128)(2,1)}, bf16[4,128,2048]{2,1,0:T(8,128)(2,1)}, u32[]{:S(2)}, u32[]{:S(2)}) %collective-permute-start.3) | collective-permute-done | bytes 2097184 | tf_op jit(solution)/shard_map/ppermute | solution.py:402
  440.0 8.3 maximum_bitcast_fusion.1
  448.3 8.4 maximum_bitcast_fusion.2
  456.7 9.2 maximum_bitcast_fusion
  466.0 23.1 %copy.58 = bf16[2,2,3,2,192,8,256]{6,5,4,3,2,1,0:T(8,128)(2,1)} copy(bf16[2,2,3,2,192,8,256]{6,4,2,5,3,0,1:T(8,128)(2,1)S(1)} %maximum_bitcast_fusion) | data formatting | bytes 37748736 | tf_op jit(solution)/shard_map/transpose | solution.py:850
  489.0 28.7 %reshape.549.weight_ref = bf16[4,3,384,2048]{3,2,1,0:T(8,128)(2,1)} reshape(bf16[2,2,3,2,192,8,256]{6,5,4,3,2,1,0:T(8,128)(2,1)} %copy.58) | data formatting | bytes 37748736 | tf_op jit(solution)/shard_map/reshape | solution.py:851
  517.7 58.6 %experts.1 = (bf16[1024,2048]{1,0:T(8,128)(2,1)}, bf16[1024,2176]{1,0:T(8,128)(2,1)}, bf16[1536,1024]{1,0:T(8,128)(2,1)}, bf16[3072,1024]{1,0:T(8,128)(2,1)}) custom-call(s32[1]{0:T(128)} %bitcast.12.first_ref, bf16[1024,2176]{1,0:T(8,128)(2,1)} %all-gather.8.cloned.1.call-done.token_ref.gate_ref, ...), custom_call_target="tpu_custom_call" | custom-call | flops 38654705664 | bytes 58720256 | tf_op jit(solution)/shard_map/experts/pallas_call | solution.py:717
  576.3 15.9 %expert_grads.3 = bf16[8,2304,256]{2,1,0:T(8,128)(2,1)} custom-call(bf16[3072,1024]{1,0:T(8,128)(2,1)} %get-tuple-element.24.slope_ref, bf16[1536,1024]{1,0:T(8,128)(2,1)} %get-tuple-element.25.active_ref, bf16[1024,2176]{1,0:T(8,128)(2,1)} %all-gather.8.cloned.1.call-done.token_ref.gate_ref, bf16[1024,2048]{1,0:T(8,128)(2,1)} %bitcast.111), custom_call_target="tpu_custom_call" | custom-call | flops 9663676416 | bytes 22544384 | tf_op jit(solution)/shard_map/expert_grads/pallas_call | solution.py:777
  597.2 25.3 %expert_grads.2 = bf16[8,2304,256]{2,1,0:T(8,128)(2,1)} custom-call(bf16[3072,1024]{1,0:T(8,128)(2,1)} %get-tuple-element.24.slope_ref, bf16[1536,1024]{1,0:T(8,128)(2,1)} %get-tuple-element.25.active_ref, bf16[1024,2176]{1,0:T(8,128)(2,1)} %all-gather.8.cloned.1.call-done.token_ref.gate_ref, bf16[1024,2048]{1,0:T(8,128)(2,1)} %bitcast.112), custom_call_target="tpu_custom_call" | custom-call | flops 9663676416 | bytes 22544384 | tf_op jit(solution)/shard_map/expert_grads/pallas_call | solution.py:777
  622.5 58.4 %reduce-scatter.3.cloned.1.call-done = bf16[128,2176]{1,0:T(8,128)(2,1)} async-done(((bf16[1024,2176]{1,0:T(8,128)(2,1)}), bf16[128,2176]{1,0:T(8,128)(2,1)}) %reduce-scatter.3.cloned.1.call-update) | async-done | bytes 557072 | tf_op jit(solution)/shard_map/reduce_scatter | solution.py:922
  729.8 24.2 %attend_back.1 = (bf16[512,1024]{1,0:T(8,128)(2,1)}, f32[1024,128]{1,0:T(8,128)}, f32[1024,128]{1,0:T(8,128)}, f32[8,128]{1,0:T(8,128)}) custom-call(f32[512,1280]{1,0:T(8,128)} %copy-done.21, f32[512,128]{1,0:T(8,128)} %get-tuple-element.70.cosine_ref, f32[512,128]{1,0:T(8,128)} %get-tuple-element.39.sine_ref, f32[1,128]{1,0:T(1,128)} %bitcast_convert_fusion.gain_ref, ...), custom_call_target="tpu_custom_call" | custom-call | flops 10737418240 | bytes 6291456 | tf_op jit(solution)/shard_map/attend_back/pallas_call | solution.py:615
  758.2 17.7 %collective-permute-done.13 = bf16[512,256]{1,0:T(8,128)(2,1)S(1)} collective-permute-done((bf16[512,256]{1,0:T(8,128)(2,1)S(1)}, bf16[512,256]{1,0:T(8,128)(2,1)S(1)}, u32[]{:S(2)}, u32[]{:S(2)}) %collective-permute-start.13) | collective-permute-done | bytes 262176 | tf_op jit(solution)/shard_map/ppermute | solution.py:402
  798.4 21.8 %collective-permute-done.30 = bf16[8,1152,256]{2,1,0:T(8,128)(2,1)} collective-permute-done((bf16[8,1152,256]{2,1,0:T(8,128)(2,1)}, bf16[8,1152,256]{2,1,0:T(8,128)(2,1)}, u32[]{:S(2)}, u32[]{:S(2)}) %collective-permute-start.30) | collective-permute-done | bytes 4718624 | tf_op jit(solution)/shard_map/ppermute | solution.py:402
  827.4 40.2 %all-to-all-done.4 = bf16[4,256,1024]{2,1,0:T(8,128)(2,1)S(1)} async-done(((bf16[4,256,1024]{2,1,0:T(8,128)(2,1)}), bf16[4,256,1024]{2,1,0:T(8,128)(2,1)S(1)}, u32[]{:S(2)}, u32[]{:S(2)}) %all-to-all-start.4) | async-done | bytes 2097184 | tf_op jit(solution)/shard_map/all_to_all | solution.py:474
  888.9 15.0 %collective-permute-done.25 = f32[17,2048]{1,0:T(8,128)S(1)} collective-permute-done((f32[17,2048]{1,0:T(8,128)S(1)}, f32[17,2048]{1,0:T(8,128)S(1)}, u32[]{:S(2)}, u32[]{:S(2)}) %collective-permute-start.25) | collective-permute-done | bytes 139296 | tf_op jit(solution)/shard_map/ppermute | solution.py:402
  911.8 11.4 %collective-permute-done.26 = f32[17,2048]{1,0:T(8,128)} collective-permute-done((f32[17,2048]{1,0:T(8,128)S(1)}, f32[17,2048]{1,0:T(8,128)}, u32[]{:S(2)}, u32[]{:S(2)}) %collective-permute-start.26) | collective-permute-done | bytes 139296 | tf_op jit(solution)/shard_map/ppermute | solution.py:402
  926.4 28.7 %collective-permute-done.27 = f32[17,2048]{1,0:T(8,128)S(1)} collective-permute-done((f32[17,2048]{1,0:T(8,128)S(1)}, f32[17,2048]{1,0:T(8,128)S(1)}, u32[]{:S(2)}, u32[]{:S(2)}) %collective-permute-start.27) | collective-permute-done | bytes 139296 | tf_op jit(solution)/shard_map/ppermute | solution.py:402
  955.1 26.2 %collective-permute-start.28 = (f32[17,2048]{1,0:T(8,128)S(1)}, f32[17,2048]{1,0:T(8,128)}, u32[]{:S(2)}, u32[]{:S(2)}) collective-permute-start(f32[17,2048]{1,0:T(8,128)S(1)} %add.353), channel_id=1, source_target_pairs={{0,16},{8,24},{16,0},{24,8},{1,17},{9,25},{17,1},{25,9},{2,18},{10... | collective-permute-start | bytes 417800 | tf_op jit(solution)/shard_map/ppermute | solution.py:402
  (323 shorter events, 261.3 us)
Async XLA Ops:
  7.2 133.6 %all-gather.4.cloned.1.call-start = ((), (), s32[]{:S(2)}) async-start(), calls=%async_computation.8 | async-start | bytes 5898240 | tf_op jit(solution)/shard_map/all_gather | solution.py:833
  7.9 247.2 %all-gather.6.cloned.1.call-start = ((), (), s32[]{:S(2)}) async-start(), calls=%async_computation.9 | async-start | bytes 4718592 | tf_op jit(solution)/shard_map/all_gather | solution.py:834
  13.8 134.5 %all-to-all-start.1 = ((bf16[8,3,192,256]{3,2,1,0:T(8,128)(2,1)}), bf16[8,3,192,256]{3,2,1,0:T(8,128)(2,1)S(1)}, u32[]{:S(2)}, u32[]{:S(2)}) async-start(bf16[8,3,192,256]{3,2,1,0:T(8,128)(2,1)} %get-tuple-element.44), calls=%async_computation.1 | async-start | bytes 4718592 | tf_op jit(solution)/shard_map/all_to_all | solution.py:843
  148.3 120.6 %all-to-all-start.2 = ((bf16[8,3,192,256]{3,2,1,0:T(8,128)(2,1)}), bf16[8,3,192,256]{3,2,1,0:T(8,128)(2,1)}, u32[]{:S(2)}, u32[]{:S(2)}) async-start(bf16[8,3,192,256]{3,2,1,0:T(8,128)(2,1)} %get-tuple-element.45), calls=%async_computation.2 | async-start | bytes 4718592 | tf_op jit(solution)/shard_map/all_to_all | solution.py:843
  268.1 62.3 %collective-permute-start.4 = (bf16[1,8,3,192,256]{4,3,2,1,0:T(8,128)(2,1)S(1)}, bf16[1,8,3,192,256]{4,3,2,1,0:T(8,128)(2,1)}, u32[]{:S(2)}, u32[]{:S(2)}) collective-permute-start(bf16[1,8,3,192,256]{4,3,2,1,0:T(8,128)(2,1)S(1)} %bitcast.103), channel_id=1, source_target_pairs={{0,2},{1,3},{2,0},{3,1},{4,6},{5,7},{6,4},{7,5},{8,10},{9,11},{10,... | collective-permute-start | bytes 7077896 | tf_op jit(solution)/shard_map/ppermute | solution.py:402
  270.4 116.4 %all-to-all-start = ((bf16[4,128,2048]{2,1,0:T(8,128)(2,1)}), bf16[4,128,2048]{2,1,0:T(8,128)(2,1)}, u32[]{:S(2)}, u32[]{:S(2)}) async-start(bf16[4,128,2048]{2,1,0:T(8,128)(2,1)} %broadcast_in_dim.82), calls=%async_computation | async-start | bytes 4194304 | tf_op jit(solution)/shard_map/all_to_all | solution.py:481
  274.9 242.8 %all-gather.8.cloned.1.call-start = ((), (), s32[]{:S(2)}) async-start(), calls=%async_computation.10 | async-start | bytes 5013504 | tf_op jit(solution)/shard_map/all_gather | solution.py:917
  275.2 105.0 %collective-permute-start.6 = (bf16[1,8,3,192,256]{4,3,2,1,0:T(8,128)(2,1)}, bf16[1,8,3,192,256]{4,3,2,1,0:T(8,128)(2,1)}, u32[]{:S(2)}, u32[]{:S(2)}) collective-permute-start(bf16[1,8,3,192,256]{4,3,2,1,0:T(8,128)(2,1)} %bitcast.26), channel_id=1, source_target_pairs={{0,2},{1,3},{2,0},{3,1},{4,6},{5,7},{6,4},{7,5},{8,10},{9,11},{10,... | collective-permute-start | bytes 7077896 | tf_op jit(solution)/shard_map/ppermute | solution.py:402
  290.2 390.7 %reduce-scatter.3.cloned.1.call-start = ((), (), s32[]{:S(2)}) async-start(), calls=%async_computation.11 | async-start | bytes 5013504 | tf_op jit(solution)/shard_map/reduce_scatter | solution.py:922
  336.3 103.7 %collective-permute-start.5 = (bf16[2,8,3,192,256]{4,3,2,1,0:T(8,128)(2,1)}, bf16[2,8,3,192,256]{4,3,2,1,0:T(8,128)(2,1)}, u32[]{:S(2)}, u32[]{:S(2)}) collective-permute-start(bf16[2,8,3,192,256]{4,3,2,1,0:T(8,128)(2,1)} %get-tuple-element.43), channel_id=1, source_target_pairs={{0,1},{1,0},{2,3},{3,2},{4,5},{5,4},{6,7},{7,6},{8,9},{9,8},{10,11... | collective-permute-start | bytes 14155784 | tf_op jit(solution)/shard_map/ppermute | solution.py:402
  386.8 61.5 %collective-permute-start.7 = (bf16[2,8,3,192,256]{4,3,2,1,0:T(8,128)(2,1)}, bf16[2,8,3,192,256]{4,3,2,1,0:T(8,128)(2,1)}, u32[]{:S(2)}, u32[]{:S(2)}) collective-permute-start(bf16[2,8,3,192,256]{4,3,2,1,0:T(8,128)(2,1)} %get-tuple-element.47), channel_id=1, source_target_pairs={{0,1},{1,0},{2,3},{3,2},{4,5},{5,4},{6,7},{7,6},{8,9},{9,8},{10,11... | collective-permute-start | bytes 14155784 | tf_op jit(solution)/shard_map/ppermute | solution.py:402
  386.8 48.4 %collective-permute-start.3 = (bf16[4,128,2048]{2,1,0:T(8,128)(2,1)}, bf16[4,128,2048]{2,1,0:T(8,128)(2,1)}, u32[]{:S(2)}, u32[]{:S(2)}) collective-permute-start(bf16[4,128,2048]{2,1,0:T(8,128)(2,1)} %all-to-all-done), channel_id=1, source_target_pairs={{0,4},{4,0},{1,5},{5,1},{2,6},{6,2},{3,7},{7,3},{8,12},{12,8},{9,1... | collective-permute-start | bytes 6291464 | tf_op jit(solution)/shard_map/ppermute | solution.py:402
  592.2 110.4 %collective-permute-start.29 = (bf16[8,2304,256]{2,1,0:T(8,128)(2,1)}, bf16[8,2304,256]{2,1,0:T(8,128)(2,1)}, u32[]{:S(2)}, u32[]{:S(2)}) collective-permute-start(bf16[8,2304,256]{2,1,0:T(8,128)(2,1)} %expert_grads.3), channel_id=1, source_target_pairs={{0,1},{1,0},{2,3},{3,2},{4,5},{5,4},{6,7},{7,6},{8,9},{9,8},{10,11... | collective-permute-start | bytes 28311560 | tf_op jit(solution)/shard_map/ppermute | solution.py:402
  595.4 93.2 %collective-permute-start.8 = (bf16[4,128,2048]{2,1,0:T(8,128)(2,1)}, bf16[4,128,2048]{2,1,0:T(8,128)(2,1)}, u32[]{:S(2)}, u32[]{:S(2)}) collective-permute-start(bf16[4,128,2048]{2,1,0:T(8,128)(2,1)} %dynamic-slice_bitcast_fusion.1), channel_id=1, source_target_pairs={{0,4},{4,0},{1,5},{5,1},{2,6},{6,2},{3,7},{7,3},{8,12},{12,8},{9,1... | collective-permute-start | bytes 6291464 | tf_op jit(solution)/shard_map/ppermute | solution.py:402
  692.4 90.2 %all-to-all-start.3 = ((bf16[4,128,2048]{2,1,0:T(8,128)(2,1)}), bf16[4,128,2048]{2,1,0:T(8,128)(2,1)S(1)}, u32[]{:S(2)}, u32[]{:S(2)}) async-start(bf16[4,128,2048]{2,1,0:T(8,128)(2,1)} %fusion.4), calls=%async_computation.3 | async-start | bytes 4194304 | tf_op jit(solution)/shard_map/all_to_all | solution.py:474
  715.8 104.5 %collective-permute-start.30 = (bf16[8,1152,256]{2,1,0:T(8,128)(2,1)}, bf16[8,1152,256]{2,1,0:T(8,128)(2,1)}, u32[]{:S(2)}, u32[]{:S(2)}) collective-permute-start(bf16[8,1152,256]{2,1,0:T(8,128)(2,1)} %slice.190), channel_id=1, source_target_pairs={{0,2},{1,3},{2,0},{3,1},{4,6},{5,7},{6,4},{7,5},{8,10},{9,11},{10,... | collective-permute-start | bytes 14155784 | tf_op jit(solution)/shard_map/ppermute | solution.py:402
  722.4 56.3 %collective-permute-start.23 = (bf16[4,256,1024]{2,1,0:T(8,128)(2,1)}, bf16[4,256,1024]{2,1,0:T(8,128)(2,1)}, u32[]{:S(2)}, u32[]{:S(2)}) collective-permute-start(bf16[4,256,1024]{2,1,0:T(8,128)(2,1)} %dynamic-slice_bitcast_fusion), channel_id=1, source_target_pairs={{0,4},{4,0},{1,5},{5,1},{2,6},{6,2},{3,7},{7,3},{8,12},{12,8},{9,1... | collective-permute-start | bytes 6291464 | tf_op jit(solution)/shard_map/ppermute | solution.py:402
  783.9 83.7 %all-to-all-start.4 = ((bf16[4,256,1024]{2,1,0:T(8,128)(2,1)}), bf16[4,256,1024]{2,1,0:T(8,128)(2,1)S(1)}, u32[]{:S(2)}, u32[]{:S(2)}) async-start(bf16[4,256,1024]{2,1,0:T(8,128)(2,1)} %fusion.3), calls=%async_computation.6 | async-start | bytes 4194304 | tf_op jit(solution)/shard_map/all_to_all | solution.py:474
  787.5 226.0 %reduce-scatter.5.cloned.1.call-start = ((), (), s32[]{:S(2)}) async-start(), calls=%async_computation.12 | async-start | bytes 5898240 | tf_op jit(solution)/shard_map/reduce_scatter | solution.py:981
  867.5 148.2 %all-to-all-start.5 = ((bf16[8,1152,256]{2,1,0:T(8,128)(2,1)}), bf16[8,1152,256]{2,1,0:T(8,128)(2,1)}, u32[]{:S(2)}, u32[]{:S(2)}) async-start(bf16[8,1152,256]{2,1,0:T(8,128)(2,1)} %add_convert_fusion.1), calls=%async_computation.7 | async-start | bytes 9437184 | tf_op jit(solution)/shard_map/all_to_all | solution.py:940
  911.5 87.7 %collective-permute-start.16 = (bf16[128,2048]{1,0:T(8,128)(2,1)}, bf16[128,2048]{1,0:T(8,128)(2,1)S(1)}, u32[]{:S(2)}, u32[]{:S(2)}) collective-permute-start(bf16[128,2048]{1,0:T(8,128)(2,1)} %get-tuple-element.62), channel_id=1, source_target_pairs={{0,2},{1,3},{2,0},{3,1},{4,6},{5,7},{6,4},{7,5},{8,10},{9,11},{10,... | collective-permute-start | bytes 1572872 | tf_op jit(solution)/shard_map/ppermute | solution.py:402
  924.2 76.1 %collective-permute-start.9 = (bf16[128,2048]{1,0:T(8,128)(2,1)}, bf16[128,2048]{1,0:T(8,128)(2,1)S(1)}, u32[]{:S(2)}, u32[]{:S(2)}) collective-permute-start(bf16[128,2048]{1,0:T(8,128)(2,1)} %get-tuple-element.63), channel_id=1, source_target_pairs={{0,2},{1,3},{2,0},{3,1},{4,6},{5,7},{6,4},{7,5},{8,10},{9,11},{10,... | collective-permute-start | bytes 1572872 | tf_op jit(solution)/shard_map/ppermute | solution.py:402
  924.3 57.0 %collective-permute-start.19 = (f32[18,128]{1,0:T(8,128)S(1)}, f32[18,128]{1,0:T(8,128)S(1)}, u32[]{:S(2)}, u32[]{:S(2)}) collective-permute-start(f32[18,128]{1,0:T(8,128)S(1)} %fusion.40), channel_id=1, source_target_pairs={{0,2},{1,3},{2,0},{3,1},{4,6},{5,7},{6,4},{7,5},{8,10},{9,11},{10,... | collective-permute-start | bytes 27656 | tf_op jit(solution)/shard_map/ppermute | solution.py:402
  955.1 43.0 %collective-permute-start.28 = (f32[17,2048]{1,0:T(8,128)S(1)}, f32[17,2048]{1,0:T(8,128)}, u32[]{:S(2)}, u32[]{:S(2)}) collective-permute-start(f32[17,2048]{1,0:T(8,128)S(1)} %add.353), channel_id=1, source_target_pairs={{0,16},{8,24},{16,0},{24,8},{1,17},{9,25},{17,1},{25,9},{2,18},{10... | collective-permute-start | bytes 417800 | tf_op jit(solution)/shard_map/ppermute | solution.py:402
  (74 other events, 1757.4 us)
Sparse Core Ops, SparseCore 0:
  10.2 130.5 all-gather.3
  142.9 112.1 all-gather.5
  290.4 94.4 all-gather.7
  576.4 104.5 reduce-scatter.2
  798.6 213.3 reduce-scatter.4

commit v2 on v1

--- a/solution.py
+++ b/solution.py
@@ -402,6 +402,22 @@
     return lax.ppermute(array, name, flip_pairs(lax.axis_size(name), bit))
 
 
+def nothing_kernel(*refs):
+    pass
+
+
+def after(array, *others):
+    anywhere = pl.BlockSpec(memory_space=pl.ANY)
+    return pl.pallas_call(
+        nothing_kernel,
+        in_specs=[anywhere] * (1 + len(others)),
+        out_specs=anywhere,
+        out_shape=jax.ShapeDtypeStruct(array.shape, array.dtype),
+        input_output_aliases={0: 0},
+        name="after",
+    )(array, *others)
+
+
 def add_low(left_side, right_side):
     return (left_side.astype(jnp.float32) + right_side.astype(jnp.float32)).astype(jnp.bfloat16)
 
@@ -460,29 +476,49 @@
     return total
 
 
-def split_halves(array, axis, place):
-    mine = lax.dynamic_index_in_dim(array, place, axis, keepdims=False)
-    theirs = lax.dynamic_index_in_dim(array, 1 - place, axis, keepdims=False)
-    return mine, theirs
-
-
-def spread_scatter(array):
-    fsdp_size, place = lax.axis_size("fsdp"), lax.axis_index("context")
-    blocks = array.reshape(fsdp_size, 2, -1, array.shape[1])
-    mine, theirs = split_halves(blocks, 1, place)
-    summed = add_low(mine, flip(theirs, "context", 1))
-    parts = lax.all_to_all(summed, "fsdp", 0, 0, tiled=True)
-    return jnp.sum(parts.astype(jnp.float32), axis=0)
-
-
-def spread_gather(piece):
-    fsdp_size, place = lax.axis_size("fsdp"), lax.axis_index("context")
-    sent = jnp.broadcast_to(piece[None], (fsdp_size,) + piece.shape)
-    column = lax.all_to_all(sent, "fsdp", 0, 0, tiled=True)
-    other = flip(column, "context", 1)
-    first = jnp.where(place == 0, column, other)
-    second = jnp.where(place == 0, other, column)
-    return jnp.stack([first, second], axis=1).reshape(-1, piece.shape[1])
+def shift(array, step):
+    size = lax.axis_size("fsdp")
+    return lax.ppermute(array, "fsdp", [(start, (start + step) % size) for start in range(size)])
+
+
+def spread_pieces(piece, waits=()):
+    pairs = []
+    for step in range(lax.axis_size("fsdp")):
+        if step:
+            if step <= len(waits):
+                piece = after(piece, *waits[step - 1])
+            piece = shift(piece, 1)
+        pairs.append((piece, flip(piece, "context", 1)))
+    return pairs
+
+
+def step_place(step):
+    return (lax.axis_index("fsdp") - step) % lax.axis_size("fsdp")
+
+
+def pair_places(step):
+    column = 2 * step_place(step)
+    side = lax.axis_index("context")
+    return column + side, column + 1 - side
+
+
+def in_order(pairs):
+    rows, columns = pairs[0][0].shape
+    whole = jnp.zeros((2 * len(pairs) * rows, columns), pairs[0][0].dtype)
+    for step, pair in enumerate(pairs):
+        for place, piece in zip(pair_places(step), pair):
+            whole = lax.dynamic_update_slice_in_dim(whole, piece, place * rows, 0)
+    return whole
+
+
+def context_scatter(array, *earlier):
+    place = lax.axis_index("context")
+    blocks = array.reshape(lax.axis_size("fsdp"), 2, -1, array.shape[1])
+    mine = lax.dynamic_index_in_dim(blocks, place, 1, keepdims=False)
+    theirs = lax.dynamic_index_in_dim(blocks, 1 - place, 1, keepdims=False)
+    if earlier:
+        mine = after(mine, *earlier)
+    return add_low(mine, flip(theirs, "context", 1))
 
 
 def sum_everywhere(array):
@@ -645,146 +681,172 @@
 
 def experts_kernel(
     local_experts,
-    chunks,
+    sides,
     gate_lanes,
     first_ref,
     token_ref,
     gate_ref,
     grad_ref,
-    weight_ref,
-    result_ref,
-    back_ref,
-    active_ref,
-    slope_ref,
-    result_sum,
-    back_sum,
-    dot_sum,
+    *refs,
 ):
-    chunk = pl.program_id(1)
-    expert = first_ref[0] + lax.rem(chunk, local_experts)
-    units = weight_ref.shape[2]
+    chunks = 2 * local_experts
+    parts = refs[: chunks * sides]
+    result_ref, back_ref, active_ref, slope_ref = refs[chunks * sides : chunks * sides + 4]
+    inward, outward, actives, slopes, sems = refs[chunks * sides + 4 :]
+    blocks, _, hidden_units, depth = parts[0].shape
+    units = sides * hidden_units
     width = token_ref.shape[1]
-    inward = weight_ref[0, :2].reshape(2 * units, width)
-    outward = weight_ref[0, 2]
-    gate_up = nt_dot(token_ref[...], inward)
-    down_back = nt_dot(grad_ref[...], outward)
-    lanes = lax.broadcasted_iota(jnp.int32, gate_ref.shape, 1)
-    here = (lanes == expert) | (lanes == expert + gate_lanes)
-    gate = jnp.sum(
-        jnp.where(here, gate_ref[...].astype(jnp.float32), 0.0), axis=-1, keepdims=True
-    )
-    gate_half, up_half = gate_up[:, :units], gate_up[:, units:]
-    sigmoid = jax.nn.sigmoid(gate_half)
-    silu = gate_half * sigmoid
-    active = silu * up_half
-    scaled_active = active * gate
-    act_grad = down_back * gate
-    gate_slope = act_grad * up_half * (sigmoid + silu * (1.0 - sigmoid))
-    slopes = jnp.concatenate([gate_slope, act_grad * silu], axis=1)
-    gate_dot = jnp.sum(active * down_back, axis=-1, keepdims=True)
-    dots = jnp.where(lanes == expert, gate_dot, 0.0)
-    low_active = scaled_active.astype(jnp.bfloat16)
-    low_slopes = slopes.astype(jnp.bfloat16)
-    active_ref[...] = low_active.T
-    slope_ref[...] = low_slopes.T
-    result = nn_dot(low_active, outward)
-    back = nn_dot(low_slopes, inward)
-
-    @pl.when(chunk == 0)
+
+    @pl.when(pl.program_id(0) == 0)
     def _():
-        result_sum[...] = result
-        back_sum[...] = back
-        dot_sum[...] = dots
-
-    @pl.when((chunk > 0) & (chunk < chunks - 1))
+        for chunk in range(chunks):
+            for side in range(sides):
+                part = parts[chunk * sides + side]
+                for kind in range(3):
+                    place = inward if kind < 2 else outward
+                    rows = ((chunk * 2 + kind) if kind < 2 else chunk) * units
+                    rows = pl.ds(rows + side * hidden_units, hidden_units)
+                    for block in range(blocks):
+                        pltpu.make_async_copy(
+                            part.at[block, kind],
+                            place.at[rows, pl.ds(block * depth, depth)],
+                            sems.at[chunk, kind // 2],
+                        ).start()
+
+    def body(first_step):
+        tokens = token_ref[...]
+        grads = grad_ref[...]
+        lanes = lax.broadcasted_iota(jnp.int32, gate_ref.shape, 1)
+        all_gates = gate_ref[...].astype(jnp.float32)
+        dots = jnp.zeros(gate_ref.shape, jnp.float32)
+        for chunk in range(chunks):
+            in_rows = pl.ds(chunk * 2 * units, 2 * units)
+            out_rows = pl.ds(chunk * units, units)
+            if first_step:
+                whole_in, whole_out = inward.at[in_rows], outward.at[out_rows]
+                pltpu.make_async_copy(whole_in, whole_in, sems.at[chunk, 0]).wait()
+                pltpu.make_async_copy(whole_out, whole_out, sems.at[chunk, 1]).wait()
+            expert = first_ref[0] + chunk % local_experts
+            gate_up = nt_dot(tokens, inward[in_rows, :])
+            down_back = nt_dot(grads, outward[out_rows, :])
+            here = (lanes == expert) | (lanes == expert + gate_lanes)
+            gate = jnp.sum(jnp.where(here, all_gates, 0.0), axis=-1, keepdims=True)
+            gate_half, up_half = gate_up[:, :units], gate_up[:, units:]
+            sigmoid = jax.nn.sigmoid(gate_half)
+            silu = gate_half * sigmoid
+            active = silu * up_half
+            act_grad = down_back * gate
+            gate_slope = act_grad * up_half * (sigmoid + silu * (1.0 - sigmoid))
+            gate_dot = jnp.sum(active * down_back, axis=-1, keepdims=True)
+            dots = dots + jnp.where(lanes == expert, gate_dot, 0.0)
+            low_active = (active * gate).astype(jnp.bfloat16)
+            low_slopes = jnp.concatenate([gate_slope, act_grad * silu], axis=1)
+            low_slopes = low_slopes.astype(jnp.bfloat16)
+            actives[:, out_rows] = low_active
+            slopes[:, in_rows] = low_slopes
+            active_ref[out_rows, :] = low_active.T
+            slope_ref[in_rows, :] = low_slopes.T
+        back_ref[:, :width] = nn_dot(slopes[...], inward[...]).astype(jnp.bfloat16)
+        back_ref[:, width:] = dots.astype(jnp.bfloat16)
+        result_ref[...] = nn_dot(actives[...], outward[...]).astype(jnp.bfloat16)
+
+    @pl.when(pl.program_id(0) == 0)
     def _():
-        result_sum[...] += result
-        back_sum[...] += back
-        dot_sum[...] += dots
-
-    @pl.when(chunk == chunks - 1)
+        body(True)
+
+    @pl.when(pl.program_id(0) > 0)
     def _():
-        result_ref[...] = (result_sum[...] + result).astype(jnp.bfloat16)
-        back_ref[:, :width] = (back_sum[...] + back).astype(jnp.bfloat16)
-        back_ref[:, width:] = (dot_sum[...] + dots).astype(jnp.bfloat16)
-
-
-def run_experts(first_expert, tokens, grads, weights, local_experts, gate_lanes):
+        body(False)
+
+
+def run_experts(first_expert, tokens, grads, parts, local_experts, gate_lanes):
     rows, width = grads.shape
     lanes = tokens.shape[1] - width
-    chunks, _, units, _ = weights.shape
-    block = min(512, rows)
+    sides = len(parts) // (2 * local_experts)
+    units = 2 * local_experts * sides * parts[0].shape[2]
+    block = min(256, rows)
+    by_row = lambda columns, place: pl.BlockSpec((block, columns), lambda row, first: (row, place))
+    by_column = lambda count: pl.BlockSpec((count, block), lambda row, first: (0, row))
     return pl.pallas_call(
-        functools.partial(experts_kernel, local_experts, chunks, gate_lanes),
+        functools.partial(experts_kernel, local_experts, sides, gate_lanes),
         grid_spec=pltpu.PrefetchScalarGridSpec(
             num_scalar_prefetch=1,
-            grid=(rows // block, chunks),
-            in_specs=[
-                pl.BlockSpec((block, width), lambda row, chunk, first: (row, 0)),
-                pl.BlockSpec((block, lanes), lambda row, chunk, first: (row, width // lanes)),
-                pl.BlockSpec((block, width), lambda row, chunk, first: (row, 0)),
-                pl.BlockSpec((1, 3, units, width), lambda row, chunk, first: (chunk, 0, 0, 0)),
-            ],
+            grid=(rows // block,),
+            in_specs=[by_row(width, 0), by_row(lanes, width // lanes), by_row(width, 0)]
+            + [pl.BlockSpec(memory_space=pl.ANY)] * len(parts),
             out_specs=[
-                pl.BlockSpec((block, width), lambda row, chunk, first: (row, 0)),
-                pl.BlockSpec((block, width + lanes), lambda row, chunk, first: (row, 0)),
-                pl.BlockSpec((units, block), lambda row, chunk, first: (chunk, row)),
-                pl.BlockSpec((2 * units, block), lambda row, chunk, first: (chunk, row)),
+                by_row(width, 0),
+                by_row(width + lanes, 0),
+                by_column(units),
+                by_column(2 * units),
             ],
             scratch_shapes=[
-                pltpu.VMEM((block, width), jnp.float32),
-                pltpu.VMEM((block, width), jnp.float32),
-                pltpu.VMEM((block, lanes), jnp.float32),
+                pltpu.VMEM((2 * units, width), jnp.bfloat16),
+                pltpu.VMEM((units, width), jnp.bfloat16),
+                pltpu.VMEM((block, units), jnp.bfloat16),
+                pltpu.VMEM((block, 2 * units), jnp.bfloat16),
+                pltpu.SemaphoreType.DMA((2 * local_experts, 2)),
             ],
         ),
         out_shape=[
             jax.ShapeDtypeStruct((rows, width), jnp.bfloat16),
             jax.ShapeDtypeStruct((rows, width + lanes), jnp.bfloat16),
-            jax.ShapeDtypeStruct((chunks * units, rows), jnp.bfloat16),
-            jax.ShapeDtypeStruct((2 * chunks * units, rows), jnp.bfloat16),
+            jax.ShapeDtypeStruct((units, rows), jnp.bfloat16),
+            jax.ShapeDtypeStruct((2 * units, rows), jnp.bfloat16),
         ],
         compiler_params=pltpu.CompilerParams(vmem_limit_bytes=VMEM_BYTES),
         cost_estimate=pl.CostEstimate(
-            flops=12 * rows * width * chunks * units,
-            bytes_accessed=2 * weights.size * (rows // block) + 10 * rows * width,
-            transcendentals=rows * chunks * units,
+            flops=12 * rows * width * units,
+            bytes_accessed=6 * units * (width + rows) + 8 * rows * width,
+            transcendentals=rows * units,
         ),
         name="experts",
-    )(first_expert.reshape(1), tokens, tokens, grads, weights)
-
-
-def expert_grads_kernel(local_experts, sides, slope_ref, active_ref, token_ref, grad_ref, out_ref):
-    hidden_units = active_ref.shape[0] // (local_experts * sides)
-    inward = nn_dot(slope_ref[...], token_ref[...]).astype(jnp.bfloat16)
-    outward = nn_dot(active_ref[...], grad_ref[...]).astype(jnp.bfloat16)
-    for expert in range(local_experts):
-        for side in range(sides):
-            for kind in range(3):
-                place = ((side * local_experts + expert) * 3 + kind) * hidden_units
-                if kind < 2:
-                    start = ((expert * 2 + kind) * sides + side) * hidden_units
-                    rows = inward[start : start + hidden_units]
-                else:
-                    start = (expert * sides + side) * hidden_units
-                    rows = outward[start : start + hidden_units]
-                out_ref[0, place : place + hidden_units] = rows
-
-
-def expert_grads(part, slopes, actives, tokens, grads, local_experts, sides, blocks):
+    )(first_expert.reshape(1), tokens, tokens, grads, *parts)
+
+
+def expert_grads_kernel(hidden_units, slope_ref, active_ref, token_ref, grad_ref, *refs):
+    sides = active_ref.shape[0] // hidden_units
+    depth = refs[-1].shape[2]
+    inward = nn_dot(slope_ref[...], token_ref[...])
+    outward = nn_dot(active_ref[...], grad_ref[...])
+    received, outs = refs[: len(refs) - sides], refs[len(refs) - sides :]
+    if len(refs) == 1:
+        received, outs = (), refs * sides
+    for side in range(sides):
+        for kind in range(3):
+            start = ((kind * sides if kind < 2 else 0) + side) * hidden_units
+            wide = (inward if kind < 2 else outward)[start : start + hidden_units]
+            place = kind * hidden_units
+            whole = (side * 3 + kind) * hidden_units
+            for block in range(refs[-1].shape[0]):
+                rows = wide[:, block * depth : (block + 1) * depth]
+                if received:
+                    more = received[0][block, whole : whole + hidden_units]
+                    rows = rows + more.astype(jnp.float32)
+                into = place if received else whole
+                outs[side][block, into : into + hidden_units] = rows.astype(jnp.bfloat16)
+
+
+def expert_grads(chunk, slopes, actives, tokens, grads, chunks, sides, blocks, received=None):
     rows, width = grads.shape
-    block = width // blocks
-    units = actives.shape[0] // 2
+    depth = width // blocks
+    units = actives.shape[0] // chunks
+    step = 2 if blocks % 2 == 0 else 1
+    by_block = lambda count: pl.BlockSpec((step, count, depth), lambda column: (column, 0, 0))
+    shape = lambda count: jax.ShapeDtypeStruct((blocks, count, depth), jnp.bfloat16)
+    alone = received is None
     return pl.pallas_call(
-        functools.partial(expert_grads_kernel, local_experts, sides),
-        grid=(blocks,),
+        functools.partial(expert_grads_kernel, units // sides),
+        grid=(blocks // step,),
         in_specs=[
-            pl.BlockSpec((2 * units, rows), lambda column: (part, 0)),
-            pl.BlockSpec((units, rows), lambda column: (part, 0)),
-            pl.BlockSpec((rows, block), lambda column: (0, column)),
-            pl.BlockSpec((rows, block), lambda column: (0, column)),
-        ],
-        out_specs=pl.BlockSpec((1, 3 * units, block), lambda column: (column, 0, 0)),
-        out_shape=jax.ShapeDtypeStruct((blocks, 3 * units, block), jnp.bfloat16),
+            pl.BlockSpec((2 * units, rows), lambda column: (chunk, 0)),
+            pl.BlockSpec((units, rows), lambda column: (chunk, 0)),
+            pl.BlockSpec((rows, step * depth), lambda column: (0, column)),
+            pl.BlockSpec((rows, step * depth), lambda column: (0, column)),
+        ]
+        + ([] if alone else [by_block(3 * units)]),
+        out_specs=by_block(3 * units) if alone else [by_block(3 * units // sides)] * sides,
+        out_shape=shape(3 * units) if alone else [shape(3 * units // sides)] * sides,
         compiler_params=pltpu.CompilerParams(vmem_limit_bytes=VMEM_BYTES),
         cost_estimate=pl.CostEstimate(
             flops=6 * units * rows * width,
@@ -792,7 +854,7 @@
             transcendentals=0,
         ),
         name="expert_grads",
-    )(slopes, actives, tokens, grads)
+    )(slopes, actives, tokens, grads, *([] if alone else [received]))
 
 
 def expert_parallel_shards(
@@ -820,7 +882,6 @@
     hidden_units = w_experts.shape[3]
     slice_rows = w_experts.shape[0]
     own_rows = tok_rows // tensor_size
-    sides = tensor_size // 2
     context_place = lax.axis_index("context")
     own_start = lax.axis_index("tensor") * own_rows
     first_expert = lax.axis_index(SPREAD) * local_experts
@@ -830,27 +891,16 @@
     gain_key = k_gain.astype(jnp.float32)
     score_scale = head_size ** (-0.5)
 
-    attn_in = lax.all_gather(joined_projection_weight, SPREAD, axis=0, tiled=True)
-    attn_out = lax.all_gather(w_o, SPREAD, axis=0, tiled=True)
+    attn_in_pairs = spread_pieces(joined_projection_weight)
+    attn_in = in_order(attn_in_pairs)
+    attn_out = lax.all_gather(
+        after(w_o, attn_in_pairs[len(attn_in_pairs) // 2][0]), SPREAD, axis=0, tiled=True
+    )
     own_grad = lax.dynamic_slice_in_dim(out_grad, own_start, own_rows)
-    all_grads = spread_gather(own_grad)
 
     sent_weights = jnp.transpose(w_experts, (1, 2, 3, 0)).reshape(
         spread_size, local_experts, 3, hidden_units, slice_rows
     )
-    expert_weights = []
-    for expert in range(local_experts):
-        own_part = lax.all_to_all(sent_weights[:, expert], SPREAD, 0, 0, tiled=True)
-        side_parts = own_part[None]
-        for bit in partner_bits()[:-1]:
-            side_parts = jnp.concatenate([side_parts, flip(side_parts, "tensor", bit)], axis=0)
-        expert_weights.append(jnp.stack([side_parts, flip(side_parts, "tensor", 1)]))
-    weights = (
-        jnp.stack(expert_weights, axis=1)
-        .transpose(0, 1, 4, 2, 5, 3, 6)
-        .reshape(2 * local_experts, 3, sides * hidden_units, model_width)
-    )
-
     ordered = own_first(inputs)
     own_index = own_first(jnp.arange(tok_rows, dtype=jnp.int32))
     own_tokens = context_place * tok_rows + own_index
@@ -872,7 +922,16 @@
     residual = ordered.astype(jnp.float32)
     inverse_attn = lax.rsqrt(jnp.mean(residual * residual, axis=-1, keepdims=True) + EPSILON)
     normalized_input = (residual * inverse_attn * gain_attn).astype(jnp.bfloat16)
-    projected = nn_dot(normalized_input, attn_in)
+    projected = jnp.zeros((tok_rows, joined_projection_weight.shape[1]), jnp.float32)
+    for step, pair in enumerate(attn_in_pairs):
+        for place, piece in zip(pair_places(step), pair):
+            columns = lax.dynamic_slice_in_dim(
+                normalized_input, place * slice_rows, slice_rows, axis=1
+            )
+            projected = projected + nn_dot(columns, piece)
+    weight_parts = [
+        lax.all_to_all(after(sent_weights[:, 0], projected), SPREAD, 0, 0, tiled=True)
+    ]
     key_raw = projected[:, heads * head_size : (heads + 1) * head_size]
     value_raw = projected[:, (heads + 1) * head_size :]
 
@@ -887,8 +946,23 @@
     pairs = jnp.concatenate([key_values, flip(key_values, "context", 1)], axis=0)
     keys, values = pairs[:, :head_size], pairs[:, head_size:]
     attended = attend(
-        projected, cosine, sine, gain_query, keys, values.T, bias, heads, score_scale
-    )
+        projected,
+        cosine,
+        sine,
+        gain_query,
+        keys,
+        values.T,
+        bias,
+        heads,
+        score_scale,
+    )
+    all_grads = lax.all_gather(after(own_grad, attn_out), SPREAD, axis=0, tiled=True)
+    weight_parts = [after(weight_parts[0], attended)]
+    for expert in range(1, local_experts):
+        sent = after(sent_weights[:, expert], weight_parts[-1])
+        weight_parts.append(lax.all_to_all(sent, SPREAD, 0, 0, tiled=True))
+    wide_bit, core_bit = partner_bits()
+    wide_parts = [flip(part, "tensor", wide_bit) for part in weight_parts]
     half_rows = tok_rows // 2
     attn_sum = tensor_scatter_rows(
         lambda half: nt_dot(
@@ -914,35 +988,46 @@
     payload = jnp.concatenate(
         [mixed_in, gate_high, gate_low, jnp.zeros((own_rows, lane_pad), jnp.bfloat16)], axis=1
     )
-    tokens = lax.all_gather(payload, SPREAD, axis=0, tiled=True)
+    tokens = in_order(
+        spread_pieces(payload, [(weight_parts[0],), (wide_parts[0],), (weight_parts[-1],)])
+    )
+    own_parts, other_parts = [], []
+    for pair in zip(weight_parts, wide_parts):
+        pair = [pair[0], after(pair[1], tokens)]
+        own_parts += pair
+        other_parts += [flip(array, "tensor", core_bit) for array in pair]
 
     results, backs, actives, slopes = run_experts(
-        first_expert, tokens, all_grads, weights, local_experts, expert_count
-    )
-    back_total = lax.psum_scatter(backs, SPREAD, scatter_dimension=0, tiled=True)
-    moe_sum = spread_scatter(results)
-    own_output = (hidden_state + moe_sum).astype(jnp.bfloat16)
-    output = own_back(tensor_gather_rows(own_output))
-
-    other_part = expert_grads(
-        1, slopes, actives, tokens, all_grads, local_experts, sides, spread_size
-    )
-    own_part = expert_grads(
-        0, slopes, actives, tokens, all_grads, local_experts, sides, spread_size
-    )
-    weight_sum = add_low(own_part, flip(other_part, "tensor", 1))
-    for bit in partner_bits()[-2::-1]:
-        rows = weight_sum.shape[1] // 2
-        weight_sum = add_low(
-            weight_sum[:, :rows], flip(weight_sum[:, rows:], "tensor", bit)
-        )
-    w_experts_grad = (
-        lax.all_to_all(weight_sum, SPREAD, 0, 0, tiled=True)
-        .reshape(expert_count, 3, hidden_units, slice_rows)
-        .astype(jnp.float32)
-        .transpose(3, 0, 1, 2)
-    )
-
+        first_expert, tokens, all_grads, own_parts + other_parts, local_experts, expert_count
+    )
+    grads_of = functools.partial(
+        expert_grads,
+        slopes=slopes,
+        actives=actives,
+        tokens=tokens,
+        grads=all_grads,
+        chunks=2 * local_experts,
+        sides=len(partner_bits()),
+        blocks=spread_size,
+    )
+    received = [
+        flip(grads_of(local_experts + expert), "tensor", core_bit)
+        for expert in range(local_experts)
+    ]
+    own_sums = [
+        grads_of(expert, received=received[expert]) for expert in range(local_experts)
+    ]
+    exchange = lambda sums: add_low(sums[0], flip(sums[1], "tensor", wide_bit))
+    expert_sums = [exchange(own_sums[0])]
+    result_sum = context_scatter(results)
+    back_total = after(
+        lax.psum_scatter(backs, SPREAD, scatter_dimension=0, tiled=True),
+        expert_sums[0],
+        own_sums[-1][0],
+        result_sum,
+    )
+    moe_sum = lax.psum_scatter(after(result_sum, back_total), "fsdp")
+    expert_backs = [lax.all_to_all(expert_sums[0], SPREAD, 0, 0, tiled=True)]
     cotangent = own_grad.astype(jnp.float32)
     gate_dot = back_total[:, model_width : model_width + expert_count].astype(jnp.float32)
     logit_grad = (
@@ -955,20 +1040,32 @@
         unit_grad - unit_moe * jnp.mean(unit_grad * unit_moe, axis=-1, keepdims=True)
     )
     moe_gain_term = jnp.sum(moe_back * unit_moe, axis=0, keepdims=True)
-    early_sums = sum_everywhere(jnp.concatenate([router_term, moe_gain_term], axis=0))
-    router_grad = early_sums[:expert_count].T
-    moe_gain_grad = early_sums[expert_count]
     branch_grad = tensor_gather_rows(state_grad.astype(jnp.bfloat16))
-    attended_grad = nn_dot(branch_grad, attn_out).astype(jnp.bfloat16)
-    w_o_grad = spread_scatter(outer_rows(branch_grad, attended).astype(jnp.bfloat16))
+    for mine, theirs in own_sums[1:]:
+        expert_sums.append(exchange((mine, after(theirs, branch_grad))))
+    w_o_part = outer_rows(branch_grad, attended).astype(jnp.bfloat16)
+    attended_grad = after(nn_dot(branch_grad, attn_out).astype(jnp.bfloat16), w_o_part)
 
     query_back, key_grad, value_grad, q_gain_rows = attend_back(
         projected, cosine, sine, gain_query, keys, values, bias, attended_grad, heads, score_scale
     )
+    w_o_sum = context_scatter(w_o_part, key_grad)
+    for sums in expert_sums[1:]:
+        expert_backs.append(
+            lax.all_to_all(after(sums, expert_backs[-1]), SPREAD, 0, 0, tiled=True)
+        )
+    w_experts_grad = (
+        jnp.stack(expert_backs, axis=1)
+        .reshape(expert_count, 3, hidden_units, slice_rows)
+        .astype(jnp.float32)
+        .transpose(3, 0, 1, 2)
+    )
+    w_o_grad = lax.psum_scatter(w_o_sum, "fsdp").astype(jnp.float32)
     pair_grad = jnp.concatenate([key_grad, value_grad], axis=-1)
-    pair_grad = pair_grad[:tok_rows] + flip(
-        pair_grad[tok_rows:].astype(jnp.bfloat16), "context", 1
-    ).astype(jnp.float32)
+    sent_pairs = after(
+        pair_grad[tok_rows:].astype(jnp.bfloat16), expert_backs[0], *expert_sums[1:]
+    )
+    pair_grad = pair_grad[:tok_rows] + flip(sent_pairs, "context", 1).astype(jnp.float32)
     key_back, k_gain_term = jax.vjp(prepare_key, key_raw, gain_key)[1](pair_grad[:, :head_size])
     projected_grad = jnp.concatenate(
         [
@@ -978,6 +1075,10 @@
         ],
         axis=1,
     )
+    own_output = (
+        hidden_state + after(moe_sum, projected_grad).astype(jnp.float32)
+    ).astype(jnp.bfloat16)
+    output = own_back(tensor_gather_rows(own_output))
     w_qkv_grad = lax.psum_scatter(
         outer_rows(normalized_input, projected_grad).astype(jnp.bfloat16),
         SPREAD,
@@ -999,21 +1100,29 @@
     ).astype(jnp.bfloat16)
     inputs_grad = own_back(tensor_gather_rows(own_inputs_grad))
     attn_gain_term = jnp.sum(normed_grad * own_unit, axis=0)
-    late_sums = sum_everywhere(
-        jnp.concatenate([attn_gain_term, jnp.sum(q_gain_rows, axis=0), k_gain_term]).reshape(
-            -1, head_size
-        )
-    ).reshape(-1)
+    gain_terms = jnp.concatenate([jnp.sum(q_gain_rows, axis=0), k_gain_term])
+    sums = sum_everywhere(
+        jnp.concatenate(
+            [
+                router_term,
+                moe_gain_term,
+                attn_gain_term[None],
+                jnp.pad(gain_terms, (0, model_width - gain_terms.shape[0]))[None],
+            ],
+            axis=0,
+        )
+    )
+    gain_sums = sums[expert_count + 2]
     return (
         output,
         inputs_grad,
-        late_sums[:model_width],
+        sums[expert_count + 1],
         w_qkv_grad,
-        late_sums[model_width : model_width + head_size],
-        late_sums[model_width + head_size :],
+        gain_sums[:head_size],
+        gain_sums[head_size : 2 * head_size],
         w_o_grad,
-        moe_gain_grad,
-        router_grad,
+        sums[expert_count],
+        sums[:expert_count].T,
         w_experts_grad,
     )
 

time: 1040 us -> 859 us (0.83)
  waiting for transfers between devices: 534 us -> 432 us
  other arithmetic: 117 us -> 56.9 us
  local copies, waits for them, and re-layouts: 105 us -> 83.2 us
    all_gather x3 -> x2, waiting for transfers between devices: 168 us -> 0.01 us  [the longest x1 0.01 us: expert_parallel_shards(): lax.all_gather(after(w_o, attn_in_pairs[len(attn_in_pairs) // 2][0]), SPR...]
    ppermute x0 -> x6, waiting for transfers between devices: none -> 89.2 us  [shift(): lax.ppermute(array, 'fsdp', [(start, (start + step) % size) for start in...]
    reduce_scatter x1, waiting for transfers between devices: 58.4 us -> 0.01 us  [expert_parallel_shards(): lax.psum_scatter(backs, SPREAD, scatter_dimension=0, tiled=True)]
    another operation x9 -> x3, other arithmetic: 36.6 us -> 2.53 us  [the longest x2 16.7 us: expert_parallel_shards(): jnp.stack(expert_weights, axis=1).transpose(0, 1, 4, 2, 5, 3, 6)]
    ppermute x31 -> x37, waiting for transfers between devices: 266 us -> 297 us  [flip(): return lax.ppermute(array, name, flip_pairs(lax.axis_size(name), bit))]
    reshape x1 -> x0, local copies, waits for them, and re-layouts: 28.7 us -> none  [expert_parallel_shards(): weights = jnp.stack(expert_weights, axis=1).transpose(0, 1, 4, 2, 5, 3, 6...]
    ppermute x0 -> x6, starting transfers between devices: none -> 23.4 us  [shift(): lax.ppermute(array, 'fsdp', [(start, (start + step) % size) for start in...]
    dynamic_update_slice x0 -> x16, local copies, waits for them, and re-layouts: none -> 21.5 us  [in_order(): whole = lax.dynamic_update_slice_in_dim(whole, piece, place * rows, 0)]
  transfers between devices with their start and end apart: 42 -> 53, of which waited for: 20 -> 31; matrix products, arithmetic and copies ran while one was open for 24% -> 19% of each run, Pallas kernels for 8% -> 9%
where the time goes in v2:
time: 859 us; the launch traced here: 850 us
  waiting for transfers between devices  432 us (50%)
  Pallas kernels  132 us (15%)
  starting transfers between devices  87.4 us (10%)
  local copies, waits for them, and re-layouts  83.2 us (10%)
  other arithmetic  56.9 us (7%)
  matrix products  40.3 us (5%)
  between operations  18.3 us (2%)
    ppermute x37, waiting for transfers between devices, flip(): return lax.ppermute(array, name, flip_pairs(lax.axis_size(name), bit))  297 us
    ppermute x6, waiting for transfers between devices, shift(): lax.ppermute(array, 'fsdp', [(start, (start + step) % size) for start in...  89.2 us
    pallas_call x1, Pallas kernels, run_experts(): pl.pallas_call(functools.partial(experts_kernel, local_experts, sides, ga...  52.6 us
    ppermute x37, starting transfers between devices, flip(): return lax.ppermute(array, name, flip_pairs(lax.axis_size(name), bit))  46.6 us
    pallas_call x4, Pallas kernels, expert_grads(): pl.pallas_call(functools.partial(expert_grads_kernel, units // sides), gr...  40.5 us
    pallas_call x1, Pallas kernels, attend_back(): pl.pallas_call(functools.partial(attend_back_kernel, scale), grid=(heads,...  24.4 us
    ppermute x6, starting transfers between devices, shift(): lax.ppermute(array, 'fsdp', [(start, (start + step) % size) for start in...  23.4 us
    dynamic_update_slice x16, local copies, waits for them, and re-layouts, in_order(): whole = lax.dynamic_update_slice_in_dim(whole, piece, place * rows, 0)  21.5 us
  transfers between devices with their start and end apart: 53, of which 31 were waited for; matrix products, arithmetic and copies ran while one was open for 19% of the time, Pallas kernels for 9%

profile of v2, /device:TPU:0, one launch (start us, length us, event | category | flops | bytes accessed | tf_op | source)
XLA Modules:
  0.0 850.0 jit_solution(8362100466585668844)
XLA Ops:
  18.1 12.3 %collective-permute-done.1 = bf16[256,1280]{1,0:T(8,128)(2,1)S(1)} collective-permute-done((bf16[256,1280]{1,0:T(8,128)(2,1)}, bf16[256,1280]{1,0:T(8,128)(2,1)S(1)}, u32[]{:S(2)}, u32[]{:S(2)}) %collective-permute-start.1) | collective-permute-done | bytes 655392 | tf_op jit(solution)/shard_map/ppermute | solution.py:481
  36.7 10.8 %collective-permute-done.3.refs_1_ = bf16[256,1280]{1,0:T(8,128)(2,1)S(1)} collective-permute-done((bf16[256,1280]{1,0:T(8,128)(2,1)S(1)}, bf16[256,1280]{1,0:T(8,128)(2,1)S(1)}, u32[]{:S(2)}, u32[]{:S(2)}) %collective-permute-start.3) | collective-permute-done | bytes 655392 | tf_op jit(solution)/shard_map/ppermute | solution.py:481
  67.7 12.4 %collective-permute-done.2 = bf16[256,1280]{1,0:T(8,128)(2,1)S(1)} collective-permute-done((bf16[256,1280]{1,0:T(8,128)(2,1)S(1)}, bf16[256,1280]{1,0:T(8,128)(2,1)S(1)}, u32[]{:S(2)}, u32[]{:S(2)}) %collective-permute-start.2) | collective-permute-done | bytes 655392 | tf_op jit(solution)/shard_map/ppermute | solution.py:402
  98.0 25.5 %collective-permute-done.6 = bf16[256,1280]{1,0:T(8,128)(2,1)S(1)} collective-permute-done((bf16[256,1280]{1,0:T(8,128)(2,1)S(1)}, bf16[256,1280]{1,0:T(8,128)(2,1)S(1)}, u32[]{:S(2)}, u32[]{:S(2)}) %collective-permute-start.6) | collective-permute-done | bytes 655392 | tf_op jit(solution)/shard_map/ppermute | solution.py:402
  147.1 14.1 %attend.1.refs_1_ = bf16[512,1024]{1,0:T(8,128)(2,1)} custom-call(f32[512,1280]{1,0:T(8,128)} %convolution_add_fusion.raw_ref.refs_1_, f32[512,128]{1,0:T(8,128)} %get-tuple-element.76.cosine_ref, f32[512,128]{1,0:T(8,128)} %get-tuple-element.49.sine_ref, f32[1,128]{1,0:T(1,128)} %bitcast_convert_fusion.1.gain_ref, ...), custom_call_target="tpu_custom_call" | custom-call | flops 4294967296 | bytes 6291456 | tf_op jit(solution)/shard_map/attend/pallas_call | solution.py:568
  173.2 18.0 %all-to-all-done.refs_0_ = bf16[8,3,192,256]{3,2,1,0:T(8,128)(2,1)S(1)} async-done(((bf16[8,3,192,256]{3,2,1,0:T(8,128)(2,1)}), bf16[8,3,192,256]{3,2,1,0:T(8,128)(2,1)S(1)}, u32[]{:S(2)}, u32[]{:S(2)}) %all-to-all-start) | async-done | bytes 2359328 | tf_op jit(solution)/shard_map/all_to_all | solution.py:933
  215.7 21.5 %collective-permute-done.10 = bf16[128,2176]{1,0:T(8,128)(2,1)} collective-permute-done((bf16[128,2176]{1,0:T(8,128)(2,1)}, bf16[128,2176]{1,0:T(8,128)(2,1)}, u32[]{:S(2)}, u32[]{:S(2)}) %collective-permute-start.10) | collective-permute-done | bytes 557088 | tf_op jit(solution)/shard_map/ppermute | solution.py:402
  237.2 30.2 %collective-permute-done.11.refs_0_ = bf16[128,2176]{1,0:T(8,128)(2,1)} collective-permute-done((bf16[128,2176]{1,0:T(8,128)(2,1)}, bf16[128,2176]{1,0:T(8,128)(2,1)}, u32[]{:S(2)}, u32[]{:S(2)}) %collective-permute-start.11) | collective-permute-done | bytes 557088 | tf_op jit(solution)/shard_map/ppermute | solution.py:481
  272.7 19.7 %collective-permute-done.12 = bf16[128,2176]{1,0:T(8,128)(2,1)} collective-permute-done((bf16[128,2176]{1,0:T(8,128)(2,1)}, bf16[128,2176]{1,0:T(8,128)(2,1)}, u32[]{:S(2)}, u32[]{:S(2)}) %collective-permute-start.12) | collective-permute-done | bytes 557088 | tf_op jit(solution)/shard_map/ppermute | solution.py:402
  292.4 19.4 %collective-permute-start.14 = (bf16[128,2176]{1,0:T(8,128)(2,1)}, bf16[128,2176]{1,0:T(8,128)(2,1)}, u32[]{:S(2)}, u32[]{:S(2)}) collective-permute-start(bf16[128,2176]{1,0:T(8,128)(2,1)} %after.22), channel_id=1, source_target_pairs={{0,8},{8,16},{16,24},{24,0},{1,9},{9,17},{17,25},{25,1},{2,10},{10... | collective-permute-start | bytes 1671176 | tf_op jit(solution)/shard_map/ppermute | solution.py:481
  313.2 13.4 %collective-permute-done.14.refs_0_ = bf16[128,2176]{1,0:T(8,128)(2,1)} collective-permute-done((bf16[128,2176]{1,0:T(8,128)(2,1)}, bf16[128,2176]{1,0:T(8,128)(2,1)}, u32[]{:S(2)}, u32[]{:S(2)}) %collective-permute-start.14) | collective-permute-done | bytes 557088 | tf_op jit(solution)/shard_map/ppermute | solution.py:481
  347.0 13.7 %collective-permute-done.16 = bf16[128,2176]{1,0:T(8,128)(2,1)} collective-permute-done((bf16[128,2176]{1,0:T(8,128)(2,1)}, bf16[128,2176]{1,0:T(8,128)(2,1)}, u32[]{:S(2)}, u32[]{:S(2)}) %collective-permute-start.16) | collective-permute-done | bytes 557088 | tf_op jit(solution)/shard_map/ppermute | solution.py:481
  383.1 52.6 %experts.1 = (bf16[1024,2048]{1,0:T(8,128)(2,1)}, bf16[1024,2176]{1,0:T(8,128)(2,1)}, bf16[1536,1024]{1,0:T(8,128)(2,1)}, bf16[3072,1024]{1,0:T(8,128)(2,1)}) custom-call(s32[1]{0:T(128)} %bitcast.12.first_ref, bf16[1024,2176]{1,0:T(8,128)(2,1)} %constant_dynamic-update-slice_fusion.8.refs_1_.token_ref.gate_ref, ...), custom_call_target="tpu_custom_call" | custom-call | flops 38654705664 | bytes 45088768 | tf_op jit(solution)/shard_map/experts/pallas_call | solution.py:770
  435.8 9.7 %expert_grads.4 = bf16[8,1152,256]{2,1,0:T(8,128)(2,1)} custom-call(bf16[3072,1024]{1,0:T(8,128)(2,1)} %get-tuple-element.24.slope_ref, bf16[1536,1024]{1,0:T(8,128)(2,1)} %get-tuple-element.25.active_ref, bf16[1024,2176]{1,0:T(8,128)(2,1)} %constant_dynamic-update-slice_fusion.8.refs_1_.token_ref.gate_ref, ...), custom_call_target="tpu_custom_call" | custom-call | flops 4831838208 | bytes 15466496 | tf_op jit(solution)/shard_map/expert_grads/pallas_call | solution.py:838
  459.0 10.6 %expert_grads.5 = (bf16[8,576,256]{2,1,0:T(8,128)(2,1)}, bf16[8,576,256]{2,1,0:T(8,128)(2,1)}) custom-call(bf16[3072,1024]{1,0:T(8,128)(2,1)} %get-tuple-element.24.slope_ref, bf16[1536,1024]{1,0:T(8,128)(2,1)} %get-tuple-element.25.active_ref, bf16[1024,2176]{1,0:T(8,128)(2,1)} %constant_dynamic-update-slice_fusion.8.refs_1_.token_ref.gate_ref, ...), custom_call_target="tpu_custom_call" | custom-call | flops 4831838208 | bytes 15466496 | tf_op jit(solution)/shard_map/expert_grads/pallas_call | solution.py:838
  473.3 52.7 %collective-permute-done.23 = bf16[4,128,2048]{2,1,0:T(8,128)(2,1)S(1)} collective-permute-done((bf16[4,128,2048]{2,1,0:T(8,128)(2,1)}, bf16[4,128,2048]{2,1,0:T(8,128)(2,1)S(1)}, u32[]{:S(2)}, u32[]{:S(2)}) %collective-permute-start.23) | collective-permute-done | bytes 2097184 | tf_op jit(solution)/shard_map/ppermute | solution.py:402
  529.7 10.6 %expert_grads.7 = (bf16[8,576,256]{2,1,0:T(8,128)(2,1)}, bf16[8,576,256]{2,1,0:T(8,128)(2,1)}) custom-call(bf16[3072,1024]{1,0:T(8,128)(2,1)} %get-tuple-element.24.slope_ref, bf16[1536,1024]{1,0:T(8,128)(2,1)} %get-tuple-element.25.active_ref, bf16[1024,2176]{1,0:T(8,128)(2,1)} %constant_dynamic-update-slice_fusion.8.refs_1_.token_ref.gate_ref, ...), custom_call_target="tpu_custom_call" | custom-call | flops 4831838208 | bytes 15466496 | tf_op jit(solution)/shard_map/expert_grads/pallas_call | solution.py:838
  552.9 11.3 %collective-permute-done.27 = bf16[128,2048]{1,0:T(8,128)(2,1)S(1)} collective-permute-done((bf16[128,2048]{1,0:T(8,128)(2,1)S(1)}, bf16[128,2048]{1,0:T(8,128)(2,1)S(1)}, u32[]{:S(2)}, u32[]{:S(2)}) %collective-permute-start.27) | collective-permute-done | bytes 524320 | tf_op jit(solution)/shard_map/ppermute | solution.py:402
  590.6 24.4 %attend_back.1 = (bf16[512,1024]{1,0:T(8,128)(2,1)}, f32[1024,128]{1,0:T(8,128)}, f32[1024,128]{1,0:T(8,128)}, f32[8,128]{1,0:T(8,128)}) custom-call(f32[512,1280]{1,0:T(8,128)} %convolution_add_fusion.raw_ref.refs_1_, f32[512,128]{1,0:T(8,128)} %get-tuple-element.76.cosine_ref, f32[512,128]{1,0:T(8,128)} %get-tuple-element.49.sine_ref, ...), custom_call_target="tpu_custom_call" | custom-call | flops 10737418240 | bytes 6291456 | tf_op jit(solution)/shard_map/attend_back/pallas_call | solution.py:651
  615.0 27.5 %collective-permute-done.42 = bf16[4,256,1024]{2,1,0:T(8,128)(2,1)} collective-permute-done((bf16[4,256,1024]{2,1,0:T(8,128)(2,1)}, bf16[4,256,1024]{2,1,0:T(8,128)(2,1)}, u32[]{:S(2)}, u32[]{:S(2)}) %collective-permute-start.42) | collective-permute-done | bytes 2097184 | tf_op jit(solution)/shard_map/ppermute | solution.py:402
  719.3 15.1 %collective-permute-done.38 = f32[19,2048]{1,0:T(8,128)S(1)} collective-permute-done((f32[19,2048]{1,0:T(8,128)S(1)}, f32[19,2048]{1,0:T(8,128)S(1)}, u32[]{:S(2)}, u32[]{:S(2)}) %collective-permute-start.38) | collective-permute-done | bytes 155680 | tf_op jit(solution)/shard_map/ppermute | solution.py:402
  743.5 41.0 %collective-permute-done.40 = f32[19,2048]{1,0:T(8,128)S(1)} collective-permute-done((f32[19,2048]{1,0:T(8,128)S(1)}, f32[19,2048]{1,0:T(8,128)S(1)}, u32[]{:S(2)}, u32[]{:S(2)}) %collective-permute-start.40) | collective-permute-done | bytes 155680 | tf_op jit(solution)/shard_map/ppermute | solution.py:402
  789.3 15.1 %collective-permute-done.41 = f32[19,2048]{1,0:T(8,128)S(1)} collective-permute-done((f32[19,2048]{1,0:T(8,128)S(1)}, f32[19,2048]{1,0:T(8,128)S(1)}, u32[]{:S(2)}, u32[]{:S(2)}) %collective-permute-start.41) | collective-permute-done | bytes 155680 | tf_op jit(solution)/shard_map/ppermute | solution.py:402
  819.5 21.2 %reduce-scatter.9.cloned.1.call-done = bf16[256,1280]{1,0:T(8,128)(2,1)} async-done(((bf16[2048,1280]{1,0:T(8,128)(2,1)}), bf16[256,1280]{1,0:T(8,128)(2,1)}) %reduce-scatter.9.cloned.1.call-update) | async-done | bytes 655376 | tf_op jit(solution)/shard_map/reduce_scatter | solution.py:1082
  (411 shorter events, 329.0 us)
Async XLA Ops:
  7.2 154.0 %all-gather.3.cloned.1.call-start = ((), (), s32[]{:S(2)}) async-start(), calls=%async_computation.8 | async-start | bytes 4718592 | tf_op jit(solution)/shard_map/all_gather | solution.py:896
  9.1 54.1 %collective-permute-start = (bf16[256,1280]{1,0:T(8,128)(2,1)}, bf16[256,1280]{1,0:T(8,128)(2,1)}, u32[]{:S(2)}, u32[]{:S(2)}) collective-permute-start(bf16[256,1280]{1,0:T(8,128)(2,1)} %param.16), channel_id=1, source_target_pairs={{0,4},{4,0},{1,5},{5,1},{2,6},{6,2},{3,7},{7,3},{8,12},{12,8},{9,1... | collective-permute-start | bytes 1966088 | tf_op jit(solution)/shard_map/ppermute | solution.py:402
  65.9 31.2 %collective-permute-start.4 = (bf16[256,1280]{1,0:T(8,128)(2,1)S(1)}, bf16[256,1280]{1,0:T(8,128)(2,1)S(1)}, u32[]{:S(2)}, u32[]{:S(2)}) collective-permute-start(bf16[256,1280]{1,0:T(8,128)(2,1)S(1)} %copy-done.16), channel_id=1, source_target_pairs={{0,4},{4,0},{1,5},{5,1},{2,6},{6,2},{3,7},{7,3},{8,12},{12,8},{9,1... | collective-permute-start | bytes 1966088 | tf_op jit(solution)/shard_map/ppermute | solution.py:402
  89.7 33.7 %collective-permute-start.6 = (bf16[256,1280]{1,0:T(8,128)(2,1)S(1)}, bf16[256,1280]{1,0:T(8,128)(2,1)S(1)}, u32[]{:S(2)}, u32[]{:S(2)}) collective-permute-start(bf16[256,1280]{1,0:T(8,128)(2,1)S(1)} %collective-permute-done.5), channel_id=1, source_target_pairs={{0,4},{4,0},{1,5},{5,1},{2,6},{6,2},{3,7},{7,3},{8,12},{12,8},{9,1... | collective-permute-start | bytes 1966088 | tf_op jit(solution)/shard_map/ppermute | solution.py:402
  125.5 65.7 %all-to-all-start = ((bf16[8,3,192,256]{3,2,1,0:T(8,128)(2,1)}), bf16[8,3,192,256]{3,2,1,0:T(8,128)(2,1)S(1)}, u32[]{:S(2)}, u32[]{:S(2)}) async-start(bf16[8,3,192,256]{3,2,1,0:T(8,128)(2,1)} %after.19), calls=%async_computation | async-start | bytes 4718592 | tf_op jit(solution)/shard_map/all_to_all | solution.py:933
  192.7 119.1 %all-to-all-start.1 = ((bf16[8,3,192,256]{3,2,1,0:T(8,128)(2,1)}), bf16[8,3,192,256]{3,2,1,0:T(8,128)(2,1)}, u32[]{:S(2)}, u32[]{:S(2)}) async-start(bf16[8,3,192,256]{3,2,1,0:T(8,128)(2,1)} %after.23), calls=%async_computation.1 | async-start | bytes 4718592 | tf_op jit(solution)/shard_map/all_to_all | solution.py:963
  197.2 178.2 %all-gather.5.cloned.1.call-start = ((), (), s32[]{:S(2)}) async-start(), calls=%async_computation.9 | async-start | bytes 4718592 | tf_op jit(solution)/shard_map/all_gather | solution.py:959
  199.1 73.5 %collective-permute-start.13 = (bf16[8,3,192,256]{3,2,1,0:T(8,128)(2,1)S(1)}, bf16[8,3,192,256]{3,2,1,0:T(8,128)(2,1)}, u32[]{:S(2)}, u32[]{:S(2)}) collective-permute-start(bf16[8,3,192,256]{3,2,1,0:T(8,128)(2,1)S(1)} %copy-done.5), channel_id=1, source_target_pairs={{0,2},{1,3},{2,0},{3,1},{4,6},{5,7},{6,4},{7,5},{8,10},{9,11},{10,... | collective-permute-start | bytes 7077896 | tf_op jit(solution)/shard_map/ppermute | solution.py:402
  200.6 343.3 %reduce-scatter.5.cloned.1.call-start = ((), (), s32[]{:S(2)}) async-start(), calls=%async_computation.10 | async-start | bytes 5013504 | tf_op jit(solution)/shard_map/reduce_scatter | solution.py:1024
  292.4 34.3 %collective-permute-start.14 = (bf16[128,2176]{1,0:T(8,128)(2,1)}, bf16[128,2176]{1,0:T(8,128)(2,1)}, u32[]{:S(2)}, u32[]{:S(2)}) collective-permute-start(bf16[128,2176]{1,0:T(8,128)(2,1)} %after.22), channel_id=1, source_target_pairs={{0,8},{8,16},{16,24},{24,0},{1,9},{9,17},{17,25},{25,1},{2,10},{10... | collective-permute-start | bytes 1671176 | tf_op jit(solution)/shard_map/ppermute | solution.py:481
  311.8 63.1 %collective-permute-start.18 = (bf16[8,3,192,256]{3,2,1,0:T(8,128)(2,1)}, bf16[8,3,192,256]{3,2,1,0:T(8,128)(2,1)}, u32[]{:S(2)}, u32[]{:S(2)}) collective-permute-start(bf16[8,3,192,256]{3,2,1,0:T(8,128)(2,1)} %all-to-all-done.1.refs_1_.refs_2_), channel_id=1, source_target_pairs={{0,2},{1,3},{2,0},{3,1},{4,6},{5,7},{6,4},{7,5},{8,10},{9,11},{10,... | collective-permute-start | bytes 7077896 | tf_op jit(solution)/shard_map/ppermute | solution.py:402
  435.7 271.1 %reduce-scatter.7.cloned.1.call-start = ((), (), s32[]{:S(2)}) async-start(), calls=%async_computation.11 | async-start | bytes 2621440 | tf_op jit(solution)/shard_map/reduce_scatter | solution.py:1029
  455.2 74.5 %collective-permute-start.26 = (bf16[8,1152,256]{2,1,0:T(8,128)(2,1)}, bf16[8,1152,256]{2,1,0:T(8,128)(2,1)}, u32[]{:S(2)}, u32[]{:S(2)}) collective-permute-start(bf16[8,1152,256]{2,1,0:T(8,128)(2,1)} %expert_grads.6), channel_id=1, source_target_pairs={{0,1},{1,0},{2,3},{3,2},{4,5},{5,4},{6,7},{7,6},{8,9},{9,8},{10,11... | collective-permute-start | bytes 14155784 | tf_op jit(solution)/shard_map/ppermute | solution.py:402
  458.7 67.3 %collective-permute-start.23 = (bf16[4,128,2048]{2,1,0:T(8,128)(2,1)}, bf16[4,128,2048]{2,1,0:T(8,128)(2,1)S(1)}, u32[]{:S(2)}, u32[]{:S(2)}) collective-permute-start(bf16[4,128,2048]{2,1,0:T(8,128)(2,1)} %dynamic-slice_bitcast_fusion.2), channel_id=1, source_target_pairs={{0,4},{4,0},{1,5},{5,1},{2,6},{6,2},{3,7},{7,3},{8,12},{12,8},{9,1... | collective-permute-start | bytes 6291464 | tf_op jit(solution)/shard_map/ppermute | solution.py:402
  469.6 70.6 %collective-permute-start.25 = (bf16[8,576,256]{2,1,0:T(8,128)(2,1)}, bf16[8,576,256]{2,1,0:T(8,128)(2,1)}, u32[]{:S(2)}, u32[]{:S(2)}) collective-permute-start(bf16[8,576,256]{2,1,0:T(8,128)(2,1)} %get-tuple-element.27), channel_id=1, source_target_pairs={{0,2},{1,3},{2,0},{3,1},{4,6},{5,7},{6,4},{7,5},{8,10},{9,11},{10,... | collective-permute-start | bytes 7077896 | tf_op jit(solution)/shard_map/ppermute | solution.py:402
  574.7 67.8 %collective-permute-start.42 = (bf16[4,256,1024]{2,1,0:T(8,128)(2,1)}, bf16[4,256,1024]{2,1,0:T(8,128)(2,1)}, u32[]{:S(2)}, u32[]{:S(2)}) collective-permute-start(bf16[4,256,1024]{2,1,0:T(8,128)(2,1)} %get-tuple-element.55), channel_id=1, source_target_pairs={{0,4},{4,0},{1,5},{5,1},{2,6},{6,2},{3,7},{7,3},{8,12},{12,8},{9,1... | collective-permute-start | bytes 6291464 | tf_op jit(solution)/shard_map/ppermute | solution.py:402
  575.9 85.8 %all-to-all-start.2 = ((bf16[8,576,256]{2,1,0:T(8,128)(2,1)}), bf16[8,576,256]{2,1,0:T(8,128)(2,1)S(1)}, u32[]{:S(2)}, u32[]{:S(2)}) async-start(bf16[8,576,256]{2,1,0:T(8,128)(2,1)} %add_convert_fusion.1.refs_1_), calls=%async_computation.4 | async-start | bytes 4718592 | tf_op jit(solution)/shard_map/all_to_all | solution.py:1030
  579.6 230.8 %reduce-scatter.11.cloned.1.call-start = ((), (), s32[]{:S(2)}) async-start(), calls=%async_computation.13 | async-start | bytes 2621440 | tf_op jit(solution)/shard_map/reduce_scatter | solution.py:1063
  588.9 62.3 %collective-permute-start.29 = (bf16[8,576,256]{2,1,0:T(8,128)(2,1)}, bf16[8,576,256]{2,1,0:T(8,128)(2,1)}, u32[]{:S(2)}, u32[]{:S(2)}) collective-permute-start(bf16[8,576,256]{2,1,0:T(8,128)(2,1)} %after.31), channel_id=1, source_target_pairs={{0,2},{1,3},{2,0},{3,1},{4,6},{5,7},{6,4},{7,5},{8,10},{9,11},{10,... | collective-permute-start | bytes 7077896 | tf_op jit(solution)/shard_map/ppermute | solution.py:402
  647.1 193.6 %reduce-scatter.9.cloned.1.call-start = ((), (), s32[]{:S(2)}) async-start(), calls=%async_computation.12 | async-start | bytes 5898240 | tf_op jit(solution)/shard_map/reduce_scatter | solution.py:1082
  702.1 110.4 %all-to-all-start.3 = ((bf16[8,576,256]{2,1,0:T(8,128)(2,1)}), bf16[8,576,256]{2,1,0:T(8,128)(2,1)}, u32[]{:S(2)}, u32[]{:S(2)}) async-start(bf16[8,576,256]{2,1,0:T(8,128)(2,1)} %after.35), calls=%async_computation.7 | async-start | bytes 4718592 | tf_op jit(solution)/shard_map/all_to_all | solution.py:1055
  717.6 71.6 %collective-permute-start.31 = (bf16[128,2048]{1,0:T(8,128)(2,1)S(1)}, bf16[128,2048]{1,0:T(8,128)(2,1)S(1)}, u32[]{:S(2)}, u32[]{:S(2)}) collective-permute-start(bf16[128,2048]{1,0:T(8,128)(2,1)S(1)} %get-tuple-element.69), channel_id=1, source_target_pairs={{0,2},{1,3},{2,0},{3,1},{4,6},{5,7},{6,4},{7,5},{8,10},{9,11},{10,... | collective-permute-start | bytes 1572872 | tf_op jit(solution)/shard_map/ppermute | solution.py:402
  743.2 41.3 %collective-permute-start.40 = (f32[19,2048]{1,0:T(8,128)S(1)}, f32[19,2048]{1,0:T(8,128)S(1)}, u32[]{:S(2)}, u32[]{:S(2)}) collective-permute-start(f32[19,2048]{1,0:T(8,128)S(1)} %add.515), channel_id=1, source_target_pairs={{0,8},{8,0},{16,24},{24,16},{1,9},{9,1},{17,25},{25,17},{2,10},{10... | collective-permute-start | bytes 466952 | tf_op jit(solution)/shard_map/ppermute | solution.py:402
  743.4 62.9 %collective-permute-start.36 = (bf16[256,2048]{1,0:T(8,128)(2,1)S(1)}, bf16[256,2048]{1,0:T(8,128)(2,1)S(1)}, u32[]{:S(2)}, u32[]{:S(2)}) collective-permute-start(bf16[256,2048]{1,0:T(8,128)(2,1)S(1)} %pad_maximum_fusion.9), channel_id=1, source_target_pairs={{0,1},{1,0},{2,3},{3,2},{4,5},{5,4},{6,7},{7,6},{8,9},{9,8},{10,11... | collective-permute-start | bytes 3145736 | tf_op jit(solution)/shard_map/ppermute | solution.py:402
  (102 other events, 1251.4 us)
Sparse Core Ops, SparseCore 0:
  48.5 102.6 all-gather.2
  200.7 127.9 all-gather.4
  435.9 106.5 reduce-scatter.4
  564.5 61.8 reduce-scatter.6
  647.2 43.0 reduce-scatter.10
  694.2 146.4 reduce-scatter.8

commit v3 on v2

--- a/solution.py
+++ b/solution.py
@@ -509,6 +509,25 @@
         for place, piece in zip(pair_places(step), pair):
             whole = lax.dynamic_update_slice_in_dim(whole, piece, place * rows, 0)
     return whole
+
+
+def scatter_steps(pair_of, waits):
+    total = None
+    for number, step in enumerate(reversed(range(lax.axis_size("fsdp")))):
+        mine, theirs = pair_of(step)
+        if number < len(waits) and waits[number]:
+            mine = after(mine, *waits[number])
+        part = mine.astype(jnp.float32) + flip(theirs, "context", 1).astype(jnp.float32)
+        if total is not None:
+            part = part + shift(total, -1).astype(jnp.float32)
+        total = part.astype(jnp.bfloat16)
+    return total
+
+
+def row_pairs(array, rows):
+    return lambda step: [
+        lax.dynamic_slice_in_dim(array, place * rows, rows) for place in pair_places(step)
+    ]
 
 
 def context_scatter(array, *earlier):
@@ -932,6 +951,7 @@
     weight_parts = [
         lax.all_to_all(after(sent_weights[:, 0], projected), SPREAD, 0, 0, tiled=True)
     ]
+    all_grads = lax.all_gather(after(own_grad, projected), SPREAD, axis=0, tiled=True)
     key_raw = projected[:, heads * head_size : (heads + 1) * head_size]
     value_raw = projected[:, (heads + 1) * head_size :]
 
@@ -956,7 +976,6 @@
         heads,
         score_scale,
     )
-    all_grads = lax.all_gather(after(own_grad, attn_out), SPREAD, axis=0, tiled=True)
     weight_parts = [after(weight_parts[0], attended)]
     for expert in range(1, local_experts):
         sent = after(sent_weights[:, expert], weight_parts[-1])
@@ -989,7 +1008,7 @@
         [mixed_in, gate_high, gate_low, jnp.zeros((own_rows, lane_pad), jnp.bfloat16)], axis=1
     )
     tokens = in_order(
-        spread_pieces(payload, [(weight_parts[0],), (wide_parts[0],), (weight_parts[-1],)])
+        spread_pieces(payload, [(weight_parts[0],), (wide_parts[0], all_grads), (weight_parts[-1],)])
     )
     own_parts, other_parts = [], []
     for pair in zip(weight_parts, wide_parts):
@@ -1010,24 +1029,18 @@
         sides=len(partner_bits()),
         blocks=spread_size,
     )
-    received = [
-        flip(grads_of(local_experts + expert), "tensor", core_bit)
+    far_sums = [grads_of(local_experts + expert) for expert in range(local_experts)]
+    own_sums = [
+        grads_of(expert, received=flip(far_sums[expert], "tensor", core_bit))
         for expert in range(local_experts)
     ]
-    own_sums = [
-        grads_of(expert, received=received[expert]) for expert in range(local_experts)
-    ]
     exchange = lambda sums: add_low(sums[0], flip(sums[1], "tensor", wide_bit))
+    moe_sum = lax.psum_scatter(results, SPREAD, scatter_dimension=0, tiled=True)
     expert_sums = [exchange(own_sums[0])]
-    result_sum = context_scatter(results)
-    back_total = after(
-        lax.psum_scatter(backs, SPREAD, scatter_dimension=0, tiled=True),
-        expert_sums[0],
-        own_sums[-1][0],
-        result_sum,
-    )
-    moe_sum = lax.psum_scatter(after(result_sum, back_total), "fsdp")
-    expert_backs = [lax.all_to_all(expert_sums[0], SPREAD, 0, 0, tiled=True)]
+    back_total = scatter_steps(
+        row_pairs(backs, own_rows),
+        [(), (far_sums[0],), (own_sums[0][0],), (far_sums[1], expert_sums[0])],
+    )
     cotangent = own_grad.astype(jnp.float32)
     gate_dot = back_total[:, model_width : model_width + expert_count].astype(jnp.float32)
     logit_grad = (
@@ -1041,15 +1054,15 @@
     )
     moe_gain_term = jnp.sum(moe_back * unit_moe, axis=0, keepdims=True)
     branch_grad = tensor_gather_rows(state_grad.astype(jnp.bfloat16))
-    for mine, theirs in own_sums[1:]:
-        expert_sums.append(exchange((mine, after(theirs, branch_grad))))
+    expert_backs = [lax.all_to_all(expert_sums[0], SPREAD, 0, 0, tiled=True)]
     w_o_part = outer_rows(branch_grad, attended).astype(jnp.bfloat16)
-    attended_grad = after(nn_dot(branch_grad, attn_out).astype(jnp.bfloat16), w_o_part)
+    attended_grad = nn_dot(after(branch_grad, own_sums[-1][0]), attn_out).astype(jnp.bfloat16)
 
     query_back, key_grad, value_grad, q_gain_rows = attend_back(
         projected, cosine, sine, gain_query, keys, values, bias, attended_grad, heads, score_scale
     )
-    w_o_sum = context_scatter(w_o_part, key_grad)
+    for mine, theirs in own_sums[1:]:
+        expert_sums.append(exchange((after(mine, key_grad), after(theirs, branch_grad))))
     for sums in expert_sums[1:]:
         expert_backs.append(
             lax.all_to_all(after(sums, expert_backs[-1]), SPREAD, 0, 0, tiled=True)
@@ -1060,11 +1073,8 @@
         .astype(jnp.float32)
         .transpose(3, 0, 1, 2)
     )
-    w_o_grad = lax.psum_scatter(w_o_sum, "fsdp").astype(jnp.float32)
     pair_grad = jnp.concatenate([key_grad, value_grad], axis=-1)
-    sent_pairs = after(
-        pair_grad[tok_rows:].astype(jnp.bfloat16), expert_backs[0], *expert_sums[1:]
-    )
+    sent_pairs = after(pair_grad[tok_rows:].astype(jnp.bfloat16), expert_sums[0])
     pair_grad = pair_grad[:tok_rows] + flip(sent_pairs, "context", 1).astype(jnp.float32)
     key_back, k_gain_term = jax.vjp(prepare_key, key_raw, gain_key)[1](pair_grad[:, :head_size])
     projected_grad = jnp.concatenate(
@@ -1075,19 +1085,27 @@
         ],
         axis=1,
     )
+    w_qkv_part = outer_rows(normalized_input, projected_grad).astype(jnp.bfloat16)
+    w_qkv_rows = lax.psum_scatter(
+        after(w_qkv_part, expert_sums[1], expert_backs[0]),
+        SPREAD,
+        scatter_dimension=0,
+        tiled=True,
+    )
+    w_o_sum = context_scatter(w_o_part, w_qkv_part)
+    late_grad = after(projected_grad, w_o_sum)
+    w_o_rows = lax.all_to_all(
+        after(w_o_sum, expert_backs[1]), "fsdp", 0, 0, tiled=True
+    )
+    w_o_grad = jnp.sum(w_o_rows.astype(jnp.float32), axis=0)
+    w_qkv_grad = w_qkv_rows.astype(jnp.float32)
     own_output = (
         hidden_state + after(moe_sum, projected_grad).astype(jnp.float32)
     ).astype(jnp.bfloat16)
     output = own_back(tensor_gather_rows(own_output))
-    w_qkv_grad = lax.psum_scatter(
-        outer_rows(normalized_input, projected_grad).astype(jnp.bfloat16),
-        SPREAD,
-        scatter_dimension=0,
-        tiled=True,
-    ).astype(jnp.float32)
     normed_grad = tensor_scatter_rows(
         lambda half: nt_dot(
-            projected_grad[half * half_rows : (half + 1) * half_rows], attn_in
+            late_grad[half * half_rows : (half + 1) * half_rows], attn_in
         ).astype(jnp.bfloat16)
     ).astype(jnp.float32)
     own_inverse = inverse_attn[:own_rows]

time: 859 us -> 865 us (level)
  other arithmetic: 56.9 us -> 71 us
  waiting for transfers between devices: 432 us -> 418 us
  Pallas kernels: 132 us -> 144 us
    reduce_scatter x4 -> x2, waiting for transfers between devices: 21.2 us -> 0.01 us  [the longest x1 0.01 us: expert_parallel_shards(): moe_sum = lax.psum_scatter(results, SPREAD, scatter_dimension=0, tiled=True)]
    all_to_all x0 -> x1, waiting for transfers between devices: none -> 17.8 us  [expert_parallel_shards(): lax.all_to_all(after(w_o_sum, expert_backs[1]), 'fsdp', 0, 0, tiled=True)]
    pallas_call x1, Pallas kernels: 52.6 us -> 65.6 us  [run_experts(): pl.pallas_call(functools.partial(experts_kernel, local_experts, sides, ga...]
    ppermute x37 -> x40, starting transfers between devices: 46.6 us -> 34.8 us  [flip(): return lax.ppermute(array, name, flip_pairs(lax.axis_size(name), bit))]
    ppermute x37 -> x40, waiting for transfers between devices: 297 us -> 288 us  [flip(): return lax.ppermute(array, name, flip_pairs(lax.axis_size(name), bit))]
    unnamed x148 -> x163, local copies, waits for them, and re-layouts: 14.1 us -> 20.5 us
    ppermute x6 -> x9, waiting for transfers between devices: 89.2 us -> 92.7 us  [shift(): lax.ppermute(array, 'fsdp', [(start, (start + step) % size) for start in...]
    ppermute x6 -> x9, starting transfers between devices: 23.4 us -> 23.6 us  [shift(): lax.ppermute(array, 'fsdp', [(start, (start + step) % size) for start in...]
  transfers between devices with their start and end apart: 53 -> 58, of which waited for: 31 -> 30; matrix products, arithmetic and copies ran while one was open for 19% -> 21% of each run, Pallas kernels for 9% -> 8%
where the time goes in v3:
time: 865 us; the launch traced here: 862 us
  waiting for transfers between devices  418 us (48%)
  Pallas kernels  144 us (17%)
  local copies, waits for them, and re-layouts  87.8 us (10%)
  starting transfers between devices  82.3 us (10%)
  other arithmetic  71 us (8%)
  matrix products  41 us (5%)
  between operations  17.8 us (2%)
    ppermute x40, waiting for transfers between devices, flip(): return lax.ppermute(array, name, flip_pairs(lax.axis_size(name), bit))  288 us
    ppermute x9, waiting for transfers between devices, shift(): lax.ppermute(array, 'fsdp', [(start, (start + step) % size) for start in...  92.7 us
    pallas_call x1, Pallas kernels, run_experts(): pl.pallas_call(functools.partial(experts_kernel, local_experts, sides, ga...  65.6 us
    pallas_call x4, Pallas kernels, expert_grads(): pl.pallas_call(functools.partial(expert_grads_kernel, units // sides), gr...  40 us
    ppermute x40, starting transfers between devices, flip(): return lax.ppermute(array, name, flip_pairs(lax.axis_size(name), bit))  34.8 us
    pallas_call x1, Pallas kernels, attend_back(): pl.pallas_call(functools.partial(attend_back_kernel, scale), grid=(heads,...  24.4 us
    ppermute x9, starting transfers between devices, shift(): lax.ppermute(array, 'fsdp', [(start, (start + step) % size) for start in...  23.6 us
    unnamed x163, local copies, waits for them, and re-layouts  20.5 us
  transfers between devices with their start and end apart: 58, of which 30 were waited for; matrix products, arithmetic and copies ran while one was open for 21% of the time, Pallas kernels for 8%

profile of v3, /device:TPU:0, one launch (start us, length us, event | category | flops | bytes accessed | tf_op | source)
XLA Modules:
  0.0 862.3 jit_solution(8490975855550581516)
XLA Ops:
  12.1 17.0 %collective-permute-done.1 = bf16[256,1280]{1,0:T(8,128)(2,1)S(1)} collective-permute-done((bf16[256,1280]{1,0:T(8,128)(2,1)}, bf16[256,1280]{1,0:T(8,128)(2,1)S(1)}, u32[]{:S(2)}, u32[]{:S(2)}) %collective-permute-start.1) | collective-permute-done | bytes 655392 | tf_op jit(solution)/shard_map/ppermute | solution.py:481
  31.6 15.2 %collective-permute-done.3.refs_1_ = bf16[256,1280]{1,0:T(8,128)(2,1)S(1)} collective-permute-done((bf16[256,1280]{1,0:T(8,128)(2,1)S(1)}, bf16[256,1280]{1,0:T(8,128)(2,1)S(1)}, u32[]{:S(2)}, u32[]{:S(2)}) %collective-permute-start.3) | collective-permute-done | bytes 655392 | tf_op jit(solution)/shard_map/ppermute | solution.py:481
  78.4 21.5 %collective-permute-done.2 = bf16[256,1280]{1,0:T(8,128)(2,1)S(1)} collective-permute-done((bf16[256,1280]{1,0:T(8,128)(2,1)S(1)}, bf16[256,1280]{1,0:T(8,128)(2,1)S(1)}, u32[]{:S(2)}, u32[]{:S(2)}) %collective-permute-start.2) | collective-permute-done | bytes 655392 | tf_op jit(solution)/shard_map/ppermute | solution.py:402
  107.3 20.0 %collective-permute-done.4 = bf16[256,1280]{1,0:T(8,128)(2,1)S(1)} collective-permute-done((bf16[256,1280]{1,0:T(8,128)(2,1)S(1)}, bf16[256,1280]{1,0:T(8,128)(2,1)S(1)}, u32[]{:S(2)}, u32[]{:S(2)}) %collective-permute-start.4) | collective-permute-done | bytes 655392 | tf_op jit(solution)/shard_map/ppermute | solution.py:402
  128.1 10.7 %collective-permute-done.6 = bf16[256,1280]{1,0:T(8,128)(2,1)S(1)} collective-permute-done((bf16[256,1280]{1,0:T(8,128)(2,1)S(1)}, bf16[256,1280]{1,0:T(8,128)(2,1)S(1)}, u32[]{:S(2)}, u32[]{:S(2)}) %collective-permute-start.6) | collective-permute-done | bytes 655392 | tf_op jit(solution)/shard_map/ppermute | solution.py:402
  154.2 20.6 %collective-permute-done.7 = bf16[512,256]{1,0:T(8,128)(2,1)S(1)} collective-permute-done((bf16[512,256]{1,0:T(8,128)(2,1)S(1)}, bf16[512,256]{1,0:T(8,128)(2,1)S(1)}, u32[]{:S(2)}, u32[]{:S(2)}) %collective-permute-start.7) | collective-permute-done | bytes 262176 | tf_op jit(solution)/shard_map/ppermute | solution.py:402
  176.6 14.1 %attend.1.refs_1_ = bf16[512,1024]{1,0:T(8,128)(2,1)} custom-call(f32[512,1280]{1,0:T(8,128)} %convolution_add_fusion.raw_ref.refs_1_, f32[512,128]{1,0:T(8,128)} %get-tuple-element.83.cosine_ref, f32[512,128]{1,0:T(8,128)} %get-tuple-element.49.sine_ref, f32[1,128]{1,0:T(1,128)} %bitcast_convert_fusion.gain_ref, ...), custom_call_target="tpu_custom_call" | custom-call | flops 4294967296 | bytes 6291456 | tf_op jit(solution)/shard_map/attend/pallas_call | solution.py:587
  200.5 20.0 %all-to-all-done.refs_0_ = bf16[8,3,192,256]{3,2,1,0:T(8,128)(2,1)S(1)} async-done(((bf16[8,3,192,256]{3,2,1,0:T(8,128)(2,1)}), bf16[8,3,192,256]{3,2,1,0:T(8,128)(2,1)S(1)}, u32[]{:S(2)}, u32[]{:S(2)}) %all-to-all-start) | async-done | bytes 2359328 | tf_op jit(solution)/shard_map/all_to_all | solution.py:952
  241.1 21.2 %collective-permute-done.10 = bf16[128,2176]{1,0:T(8,128)(2,1)} collective-permute-done((bf16[128,2176]{1,0:T(8,128)(2,1)}, bf16[128,2176]{1,0:T(8,128)(2,1)}, u32[]{:S(2)}, u32[]{:S(2)}) %collective-permute-start.10) | collective-permute-done | bytes 557088 | tf_op jit(solution)/shard_map/ppermute | solution.py:402
  263.7 32.4 %collective-permute-done.11.refs_0_ = bf16[128,2176]{1,0:T(8,128)(2,1)S(1)} collective-permute-done((bf16[128,2176]{1,0:T(8,128)(2,1)}, bf16[128,2176]{1,0:T(8,128)(2,1)S(1)}, u32[]{:S(2)}, u32[]{:S(2)}) %collective-permute-start.11) | collective-permute-done | bytes 557088 | tf_op jit(solution)/shard_map/ppermute | solution.py:481
  300.4 13.2 %collective-permute-done.12 = bf16[128,2176]{1,0:T(8,128)(2,1)} collective-permute-done((bf16[128,2176]{1,0:T(8,128)(2,1)S(1)}, bf16[128,2176]{1,0:T(8,128)(2,1)}, u32[]{:S(2)}, u32[]{:S(2)}) %collective-permute-start.12) | collective-permute-done | bytes 557088 | tf_op jit(solution)/shard_map/ppermute | solution.py:402
  322.9 10.5 %collective-permute-done.14.refs_0_ = bf16[128,2176]{1,0:T(8,128)(2,1)S(1)} collective-permute-done((bf16[128,2176]{1,0:T(8,128)(2,1)}, bf16[128,2176]{1,0:T(8,128)(2,1)S(1)}, u32[]{:S(2)}, u32[]{:S(2)}) %collective-permute-start.14) | collective-permute-done | bytes 557088 | tf_op jit(solution)/shard_map/ppermute | solution.py:481
  348.9 11.6 %collective-permute-done.16 = bf16[128,2176]{1,0:T(8,128)(2,1)S(1)} collective-permute-done((bf16[128,2176]{1,0:T(8,128)(2,1)}, bf16[128,2176]{1,0:T(8,128)(2,1)S(1)}, u32[]{:S(2)}, u32[]{:S(2)}) %collective-permute-start.16) | collective-permute-done | bytes 557088 | tf_op jit(solution)/shard_map/ppermute | solution.py:481
  380.8 65.6 %experts.1 = (bf16[1024,2048]{1,0:T(8,128)(2,1)}, bf16[1024,2176]{1,0:T(8,128)(2,1)}, bf16[1536,1024]{1,0:T(8,128)(2,1)}, bf16[3072,1024]{1,0:T(8,128)(2,1)}) custom-call(s32[1]{0:T(128)} %bitcast.12.first_ref, bf16[1024,2176]{1,0:T(8,128)(2,1)} %constant_dynamic-update-slice_fusion.8.refs_1_.token_ref.gate_ref, ...), custom_call_target="tpu_custom_call" | custom-call | flops 38654705664 | bytes 45088768 | tf_op jit(solution)/shard_map/experts/pallas_call | solution.py:789
  461.8 13.4 %collective-permute-done.28 = bf16[128,2176]{1,0:T(8,128)(2,1)S(1)} collective-permute-done((bf16[128,2176]{1,0:T(8,128)(2,1)S(1)}, bf16[128,2176]{1,0:T(8,128)(2,1)S(1)}, u32[]{:S(2)}, u32[]{:S(2)}) %collective-permute-start.28) | collective-permute-done | bytes 557088 | tf_op jit(solution)/shard_map/ppermute | solution.py:402
  511.5 29.1 %collective-permute-done.24 = bf16[8,576,256]{2,1,0:T(8,128)(2,1)} collective-permute-done((bf16[8,576,256]{2,1,0:T(8,128)(2,1)}, bf16[8,576,256]{2,1,0:T(8,128)(2,1)}, u32[]{:S(2)}, u32[]{:S(2)}) %collective-permute-start.24) | collective-permute-done | bytes 2359328 | tf_op jit(solution)/shard_map/ppermute | solution.py:402
  549.9 11.4 %collective-permute-done.32 = bf16[128,2048]{1,0:T(8,128)(2,1)S(1)} collective-permute-done((bf16[128,2048]{1,0:T(8,128)(2,1)S(1)}, bf16[128,2048]{1,0:T(8,128)(2,1)S(1)}, u32[]{:S(2)}, u32[]{:S(2)}) %collective-permute-start.32) | collective-permute-done | bytes 524320 | tf_op jit(solution)/shard_map/ppermute | solution.py:402
  568.8 10.4 %expert_grads.7 = (bf16[8,576,256]{2,1,0:T(8,128)(2,1)}, bf16[8,576,256]{2,1,0:T(8,128)(2,1)}) custom-call(bf16[3072,1024]{1,0:T(8,128)(2,1)} %get-tuple-element.24.slope_ref, bf16[1536,1024]{1,0:T(8,128)(2,1)} %get-tuple-element.25.active_ref, bf16[1024,2176]{1,0:T(8,128)(2,1)} %constant_dynamic-update-slice_fusion.8.refs_1_.token_ref.gate_ref, ...), custom_call_target="tpu_custom_call" | custom-call | flops 4831838208 | bytes 15466496 | tf_op jit(solution)/shard_map/expert_grads/pallas_call | solution.py:857
  592.4 24.4 %attend_back.1 = (bf16[512,1024]{1,0:T(8,128)(2,1)}, f32[1024,128]{1,0:T(8,128)}, f32[1024,128]{1,0:T(8,128)}, f32[8,128]{1,0:T(8,128)}) custom-call(f32[512,1280]{1,0:T(8,128)} %convolution_add_fusion.raw_ref.refs_1_, f32[512,128]{1,0:T(8,128)} %get-tuple-element.83.cosine_ref, f32[512,128]{1,0:T(8,128)} %get-tuple-element.49.sine_ref, ...), custom_call_target="tpu_custom_call" | custom-call | flops 10737418240 | bytes 6291456 | tf_op jit(solution)/shard_map/attend_back/pallas_call | solution.py:670
  664.7 33.6 %collective-permute-done.38 = bf16[4,256,1024]{2,1,0:T(8,128)(2,1)} collective-permute-done((bf16[4,256,1024]{2,1,0:T(8,128)(2,1)}, bf16[4,256,1024]{2,1,0:T(8,128)(2,1)}, u32[]{:S(2)}, u32[]{:S(2)}) %collective-permute-start.38) | collective-permute-done | bytes 2097184 | tf_op jit(solution)/shard_map/ppermute | solution.py:402
  745.2 15.3 %collective-permute-done.44 = f32[19,2048]{1,0:T(8,128)S(1)} collective-permute-done((f32[19,2048]{1,0:T(8,128)S(1)}, f32[19,2048]{1,0:T(8,128)S(1)}, u32[]{:S(2)}, u32[]{:S(2)}) %collective-permute-start.44) | collective-permute-done | bytes 155680 | tf_op jit(solution)/shard_map/ppermute | solution.py:402
  776.1 18.2 %collective-permute-done.46 = f32[19,2048]{1,0:T(8,128)S(1)} collective-permute-done((f32[19,2048]{1,0:T(8,128)S(1)}, f32[19,2048]{1,0:T(8,128)S(1)}, u32[]{:S(2)}, u32[]{:S(2)}) %collective-permute-start.46) | collective-permute-done | bytes 155680 | tf_op jit(solution)/shard_map/ppermute | solution.py:402
  801.9 16.6 %collective-permute-done.47 = f32[19,2048]{1,0:T(8,128)} collective-permute-done((f32[19,2048]{1,0:T(8,128)}, f32[19,2048]{1,0:T(8,128)}, u32[]{:S(2)}, u32[]{:S(2)}) %collective-permute-start.47) | collective-permute-done | bytes 155680 | tf_op jit(solution)/shard_map/ppermute | solution.py:402
  834.2 17.8 %all-to-all-done.4 = bf16[4,256,1024]{2,1,0:T(8,128)(2,1)S(1)} async-done(((bf16[4,256,1024]{2,1,0:T(8,128)(2,1)}), bf16[4,256,1024]{2,1,0:T(8,128)(2,1)S(1)}, u32[]{:S(2)}, u32[]{:S(2)}) %all-to-all-start.4) | async-done | bytes 2097184 | tf_op jit(solution)/shard_map/all_to_all | solution.py:1097
  (442 shorter events, 360.7 us)
Async XLA Ops:
  7.2 183.5 %all-gather.3.cloned.1.call-start = ((), (), s32[]{:S(2)}) async-start(), calls=%async_computation.7 | async-start | bytes 4718592 | tf_op jit(solution)/shard_map/all_gather | solution.py:915
  29.1 45.3 %collective-permute-start = (bf16[256,1280]{1,0:T(8,128)(2,1)}, bf16[256,1280]{1,0:T(8,128)(2,1)}, u32[]{:S(2)}, u32[]{:S(2)}) collective-permute-start(bf16[256,1280]{1,0:T(8,128)(2,1)} %param.16), channel_id=1, source_target_pairs={{0,4},{4,0},{1,5},{5,1},{2,6},{6,2},{3,7},{7,3},{8,12},{12,8},{9,1... | collective-permute-start | bytes 1966088 | tf_op jit(solution)/shard_map/ppermute | solution.py:402
  77.1 50.2 %collective-permute-start.4 = (bf16[256,1280]{1,0:T(8,128)(2,1)S(1)}, bf16[256,1280]{1,0:T(8,128)(2,1)S(1)}, u32[]{:S(2)}, u32[]{:S(2)}) collective-permute-start(bf16[256,1280]{1,0:T(8,128)(2,1)S(1)} %copy-done.22), channel_id=1, source_target_pairs={{0,4},{4,0},{1,5},{5,1},{2,6},{6,2},{3,7},{7,3},{8,12},{12,8},{9,1... | collective-permute-start | bytes 1966088 | tf_op jit(solution)/shard_map/ppermute | solution.py:402
  106.6 32.2 %collective-permute-start.6 = (bf16[256,1280]{1,0:T(8,128)(2,1)S(1)}, bf16[256,1280]{1,0:T(8,128)(2,1)S(1)}, u32[]{:S(2)}, u32[]{:S(2)}) collective-permute-start(bf16[256,1280]{1,0:T(8,128)(2,1)S(1)} %collective-permute-done.5), channel_id=1, source_target_pairs={{0,4},{4,0},{1,5},{5,1},{2,6},{6,2},{3,7},{7,3},{8,12},{12,8},{9,1... | collective-permute-start | bytes 1966088 | tf_op jit(solution)/shard_map/ppermute | solution.py:402
  140.8 79.8 %all-to-all-start = ((bf16[8,3,192,256]{3,2,1,0:T(8,128)(2,1)}), bf16[8,3,192,256]{3,2,1,0:T(8,128)(2,1)S(1)}, u32[]{:S(2)}, u32[]{:S(2)}) async-start(bf16[8,3,192,256]{3,2,1,0:T(8,128)(2,1)} %after.24), calls=%async_computation | async-start | bytes 4718592 | tf_op jit(solution)/shard_map/all_to_all | solution.py:952
  144.4 156.1 %all-gather.5.cloned.1.call-start = ((), (), s32[]{:S(2)}) async-start(), calls=%async_computation.8 | async-start | bytes 4718592 | tf_op jit(solution)/shard_map/all_gather | solution.py:954
  221.9 100.4 %all-to-all-start.1 = ((bf16[8,3,192,256]{3,2,1,0:T(8,128)(2,1)}), bf16[8,3,192,256]{3,2,1,0:T(8,128)(2,1)}, u32[]{:S(2)}, u32[]{:S(2)}) async-start(bf16[8,3,192,256]{3,2,1,0:T(8,128)(2,1)} %after.29), calls=%async_computation.1 | async-start | bytes 4718592 | tf_op jit(solution)/shard_map/all_to_all | solution.py:982
  226.5 438.3 %reduce-scatter.3.cloned.1.call-start = ((), (), s32[]{:S(2)}) async-start(), calls=%async_computation.9 | async-start | bytes 4718592 | tf_op jit(solution)/shard_map/reduce_scatter | solution.py:1038
  227.4 73.1 %collective-permute-start.13 = (bf16[8,3,192,256]{3,2,1,0:T(8,128)(2,1)S(1)}, bf16[8,3,192,256]{3,2,1,0:T(8,128)(2,1)}, u32[]{:S(2)}, u32[]{:S(2)}) collective-permute-start(bf16[8,3,192,256]{3,2,1,0:T(8,128)(2,1)S(1)} %copy-done.6), channel_id=1, source_target_pairs={{0,2},{1,3},{2,0},{3,1},{4,6},{5,7},{6,4},{7,5},{8,10},{9,11},{10,... | collective-permute-start | bytes 7077896 | tf_op jit(solution)/shard_map/ppermute | solution.py:402
  262.3 33.8 %collective-permute-start.11 = (bf16[128,2176]{1,0:T(8,128)(2,1)}, bf16[128,2176]{1,0:T(8,128)(2,1)S(1)}, u32[]{:S(2)}, u32[]{:S(2)}) collective-permute-start(bf16[128,2176]{1,0:T(8,128)(2,1)} %after.26), channel_id=1, source_target_pairs={{0,8},{8,16},{16,24},{24,0},{1,9},{9,17},{17,25},{25,1},{2,10},{10... | collective-permute-start | bytes 1671176 | tf_op jit(solution)/shard_map/ppermute | solution.py:481
  322.3 52.0 %collective-permute-start.18 = (bf16[8,3,192,256]{3,2,1,0:T(8,128)(2,1)}, bf16[8,3,192,256]{3,2,1,0:T(8,128)(2,1)}, u32[]{:S(2)}, u32[]{:S(2)}) collective-permute-start(bf16[8,3,192,256]{3,2,1,0:T(8,128)(2,1)} %all-to-all-done.1.refs_1_.refs_2_), channel_id=1, source_target_pairs={{0,2},{1,3},{2,0},{3,1},{4,6},{5,7},{6,4},{7,5},{8,10},{9,11},{10,... | collective-permute-start | bytes 7077896 | tf_op jit(solution)/shard_map/ppermute | solution.py:402
  488.5 52.2 %collective-permute-start.24 = (bf16[8,576,256]{2,1,0:T(8,128)(2,1)}, bf16[8,576,256]{2,1,0:T(8,128)(2,1)}, u32[]{:S(2)}, u32[]{:S(2)}) collective-permute-start(bf16[8,576,256]{2,1,0:T(8,128)(2,1)} %get-tuple-element.27), channel_id=1, source_target_pairs={{0,2},{1,3},{2,0},{3,1},{4,6},{5,7},{6,4},{7,5},{8,10},{9,11},{10,... | collective-permute-start | bytes 7077896 | tf_op jit(solution)/shard_map/ppermute | solution.py:402
  504.6 64.2 %collective-permute-start.34 = (bf16[8,1152,256]{2,1,0:T(8,128)(2,1)}, bf16[8,1152,256]{2,1,0:T(8,128)(2,1)}, u32[]{:S(2)}, u32[]{:S(2)}) collective-permute-start(bf16[8,1152,256]{2,1,0:T(8,128)(2,1)} %expert_grads.4.refs_1_), channel_id=1, source_target_pairs={{0,1},{1,0},{2,3},{3,2},{4,5},{5,4},{6,7},{7,6},{8,9},{9,8},{10,11... | collective-permute-start | bytes 14155784 | tf_op jit(solution)/shard_map/ppermute | solution.py:402
  504.6 39.9 %collective-permute-start.25 = (bf16[128,2176]{1,0:T(8,128)(2,1)}, bf16[128,2176]{1,0:T(8,128)(2,1)}, u32[]{:S(2)}, u32[]{:S(2)}) collective-permute-start(bf16[128,2176]{1,0:T(8,128)(2,1)} %get-tuple-element.60), channel_id=1, source_target_pairs={{0,4},{4,0},{1,5},{5,1},{2,6},{6,2},{3,7},{7,3},{8,12},{12,8},{9,1... | collective-permute-start | bytes 1671176 | tf_op jit(solution)/shard_map/ppermute | solution.py:402
  508.2 36.3 %collective-permute-start.31 = (bf16[128,2176]{1,0:T(8,128)(2,1)}, bf16[128,2176]{1,0:T(8,128)(2,1)}, u32[]{:S(2)}, u32[]{:S(2)}) collective-permute-start(bf16[128,2176]{1,0:T(8,128)(2,1)} %add_convert_fusion.4), channel_id=1, source_target_pairs={{0,24},{8,0},{16,8},{24,16},{1,25},{9,1},{17,9},{25,17},{2,26},{10... | collective-permute-start | bytes 1671176 | tf_op jit(solution)/shard_map/ppermute | solution.py:481
  579.2 74.1 %all-to-all-start.2 = ((bf16[8,576,256]{2,1,0:T(8,128)(2,1)}), bf16[8,576,256]{2,1,0:T(8,128)(2,1)S(1)}, u32[]{:S(2)}, u32[]{:S(2)}) async-start(bf16[8,576,256]{2,1,0:T(8,128)(2,1)} %add_convert_fusion.1.refs_2_.refs_1_), calls=%async_computation.3 | async-start | bytes 4718592 | tf_op jit(solution)/shard_map/all_to_all | solution.py:1057
  582.8 270.5 %reduce-scatter.5.cloned.1.call-start = ((), (), s32[]{:S(2)}) async-start(), calls=%async_computation.10 | async-start | bytes 5898240 | tf_op jit(solution)/shard_map/reduce_scatter | solution.py:1089
  586.0 63.7 %collective-permute-start.48 = (bf16[8,576,256]{2,1,0:T(8,128)(2,1)}, bf16[8,576,256]{2,1,0:T(8,128)(2,1)}, u32[]{:S(2)}, u32[]{:S(2)}) collective-permute-start(bf16[8,576,256]{2,1,0:T(8,128)(2,1)} %after.42), channel_id=1, source_target_pairs={{0,2},{1,3},{2,0},{3,1},{4,6},{5,7},{6,4},{7,5},{8,10},{9,11},{10,... | collective-permute-start | bytes 7077896 | tf_op jit(solution)/shard_map/ppermute | solution.py:402
  633.7 64.7 %collective-permute-start.38 = (bf16[4,256,1024]{2,1,0:T(8,128)(2,1)}, bf16[4,256,1024]{2,1,0:T(8,128)(2,1)}, u32[]{:S(2)}, u32[]{:S(2)}) collective-permute-start(bf16[4,256,1024]{2,1,0:T(8,128)(2,1)} %get-tuple-element.62), channel_id=1, source_target_pairs={{0,4},{4,0},{1,5},{5,1},{2,6},{6,2},{3,7},{7,3},{8,12},{12,8},{9,1... | collective-permute-start | bytes 6291464 | tf_op jit(solution)/shard_map/ppermute | solution.py:402
  707.5 88.0 %all-to-all-start.3 = ((bf16[8,576,256]{2,1,0:T(8,128)(2,1)}), bf16[8,576,256]{2,1,0:T(8,128)(2,1)S(1)}, u32[]{:S(2)}, u32[]{:S(2)}) async-start(bf16[8,576,256]{2,1,0:T(8,128)(2,1)} %after.44), calls=%async_computation.5 | async-start | bytes 4718592 | tf_op jit(solution)/shard_map/all_to_all | solution.py:1068
  741.4 32.6 %collective-permute-start.41 = (bf16[128,2048]{1,0:T(8,128)(2,1)}, bf16[128,2048]{1,0:T(8,128)(2,1)S(1)}, u32[]{:S(2)}, u32[]{:S(2)}) collective-permute-start(bf16[128,2048]{1,0:T(8,128)(2,1)} %get-tuple-element.75), channel_id=1, source_target_pairs={{0,2},{1,3},{2,0},{3,1},{4,6},{5,7},{6,4},{7,5},{8,10},{9,11},{10,... | collective-permute-start | bytes 1572872 | tf_op jit(solution)/shard_map/ppermute | solution.py:402
  743.5 57.1 %collective-permute-start.36 = (bf16[128,2048]{1,0:T(8,128)(2,1)}, bf16[128,2048]{1,0:T(8,128)(2,1)S(1)}, u32[]{:S(2)}, u32[]{:S(2)}) collective-permute-start(bf16[128,2048]{1,0:T(8,128)(2,1)} %get-tuple-element.76), channel_id=1, source_target_pairs={{0,2},{1,3},{2,0},{3,1},{4,6},{5,7},{6,4},{7,5},{8,10},{9,11},{10,... | collective-permute-start | bytes 1572872 | tf_op jit(solution)/shard_map/ppermute | solution.py:402
  776.1 45.2 %collective-permute-start.42 = (bf16[256,2048]{1,0:T(8,128)(2,1)}, bf16[256,2048]{1,0:T(8,128)(2,1)}, u32[]{:S(2)}, u32[]{:S(2)}) collective-permute-start(bf16[256,2048]{1,0:T(8,128)(2,1)} %pad_maximum_fusion.9), channel_id=1, source_target_pairs={{0,1},{1,0},{2,3},{3,2},{4,5},{5,4},{6,7},{7,6},{8,9},{9,8},{10,11... | collective-permute-start | bytes 3145736 | tf_op jit(solution)/shard_map/ppermute | solution.py:402
  796.9 55.0 %all-to-all-start.4 = ((bf16[4,256,1024]{2,1,0:T(8,128)(2,1)}), bf16[4,256,1024]{2,1,0:T(8,128)(2,1)S(1)}, u32[]{:S(2)}, u32[]{:S(2)}) async-start(bf16[4,256,1024]{2,1,0:T(8,128)(2,1)} %after.45), calls=%async_computation.6 | async-start | bytes 4194304 | tf_op jit(solution)/shard_map/all_to_all | solution.py:1097
  (114 other events, 1560.0 us)
Sparse Core Ops, SparseCore 0:
  47.9 94.2 all-gather.2
  147.3 150.3 all-gather.4
  511.6 105.9 reduce-scatter.2
  654.9 139.3 reduce-scatter.4

commit v4 on v3

--- a/solution.py
+++ b/solution.py
@@ -732,7 +732,7 @@
                             sems.at[chunk, kind // 2],
                         ).start()
 
-    def body(first_step):
+    def body():
         tokens = token_ref[...]
         grads = grad_ref[...]
         lanes = lax.broadcasted_iota(jnp.int32, gate_ref.shape, 1)
@@ -741,10 +741,13 @@
         for chunk in range(chunks):
             in_rows = pl.ds(chunk * 2 * units, 2 * units)
             out_rows = pl.ds(chunk * units, units)
-            if first_step:
+
+            @pl.when(pl.program_id(0) == 0)
+            def _():
                 whole_in, whole_out = inward.at[in_rows], outward.at[out_rows]
                 pltpu.make_async_copy(whole_in, whole_in, sems.at[chunk, 0]).wait()
                 pltpu.make_async_copy(whole_out, whole_out, sems.at[chunk, 1]).wait()
+
             expert = first_ref[0] + chunk % local_experts
             gate_up = nt_dot(tokens, inward[in_rows, :])
             down_back = nt_dot(grads, outward[out_rows, :])
@@ -769,13 +772,7 @@
         back_ref[:, width:] = dots.astype(jnp.bfloat16)
         result_ref[...] = nn_dot(actives[...], outward[...]).astype(jnp.bfloat16)
 
-    @pl.when(pl.program_id(0) == 0)
-    def _():
-        body(True)
-
-    @pl.when(pl.program_id(0) > 0)
-    def _():
-        body(False)
+    body()
 
 
 def run_experts(first_expert, tokens, grads, parts, local_experts, gate_lanes):

time: 865 us -> 864 us (level)
  no operation moved by 1% of the time
where the time goes in v4:
time: 864 us; the launch traced here: 855 us
  waiting for transfers between devices  418 us (48%)
  Pallas kernels  136 us (16%)
  local copies, waits for them, and re-layouts  87.8 us (10%)
  starting transfers between devices  82.2 us (10%)
  other arithmetic  71 us (8%)
  matrix products  41 us (5%)
  between operations  18.1 us (2%)
    ppermute x40, waiting for transfers between devices, flip(): return lax.ppermute(array, name, flip_pairs(lax.axis_size(name), bit))  288 us
    ppermute x9, waiting for transfers between devices, shift(): lax.ppermute(array, 'fsdp', [(start, (start + step) % size) for start in...  92.7 us
    pallas_call x1, Pallas kernels, run_experts(): pl.pallas_call(functools.partial(experts_kernel, local_experts, sides, ga...  57.7 us
    pallas_call x4, Pallas kernels, expert_grads(): pl.pallas_call(functools.partial(expert_grads_kernel, units // sides), gr...  40.1 us
    ppermute x40, starting transfers between devices, flip(): return lax.ppermute(array, name, flip_pairs(lax.axis_size(name), bit))  34.8 us
    pallas_call x1, Pallas kernels, attend_back(): pl.pallas_call(functools.partial(attend_back_kernel, scale), grid=(heads,...  24.4 us
    ppermute x9, starting transfers between devices, shift(): lax.ppermute(array, 'fsdp', [(start, (start + step) % size) for start in...  23.6 us
    unnamed x163, local copies, waits for them, and re-layouts  20.5 us
  transfers between devices with their start and end apart: 58, of which 30 were waited for; matrix products, arithmetic and copies ran while one was open for 21% of the time, Pallas kernels for 8%

profile of v4, /device:TPU:0, one launch (start us, length us, event | category | flops | bytes accessed | tf_op | source)
XLA Modules:
  0.0 854.9 jit_solution(11379929709464562060)
XLA Ops:
  12.1 17.0 %collective-permute-done.1 = bf16[256,1280]{1,0:T(8,128)(2,1)S(1)} collective-permute-done((bf16[256,1280]{1,0:T(8,128)(2,1)}, bf16[256,1280]{1,0:T(8,128)(2,1)S(1)}, u32[]{:S(2)}, u32[]{:S(2)}) %collective-permute-start.1) | collective-permute-done | bytes 655392 | tf_op jit(solution)/shard_map/ppermute | solution.py:481
  31.6 15.2 %collective-permute-done.3.refs_1_ = bf16[256,1280]{1,0:T(8,128)(2,1)S(1)} collective-permute-done((bf16[256,1280]{1,0:T(8,128)(2,1)S(1)}, bf16[256,1280]{1,0:T(8,128)(2,1)S(1)}, u32[]{:S(2)}, u32[]{:S(2)}) %collective-permute-start.3) | collective-permute-done | bytes 655392 | tf_op jit(solution)/shard_map/ppermute | solution.py:481
  78.4 21.5 %collective-permute-done.2 = bf16[256,1280]{1,0:T(8,128)(2,1)S(1)} collective-permute-done((bf16[256,1280]{1,0:T(8,128)(2,1)S(1)}, bf16[256,1280]{1,0:T(8,128)(2,1)S(1)}, u32[]{:S(2)}, u32[]{:S(2)}) %collective-permute-start.2) | collective-permute-done | bytes 655392 | tf_op jit(solution)/shard_map/ppermute | solution.py:402
  107.3 20.0 %collective-permute-done.4 = bf16[256,1280]{1,0:T(8,128)(2,1)S(1)} collective-permute-done((bf16[256,1280]{1,0:T(8,128)(2,1)S(1)}, bf16[256,1280]{1,0:T(8,128)(2,1)S(1)}, u32[]{:S(2)}, u32[]{:S(2)}) %collective-permute-start.4) | collective-permute-done | bytes 655392 | tf_op jit(solution)/shard_map/ppermute | solution.py:402
  128.1 10.7 %collective-permute-done.6 = bf16[256,1280]{1,0:T(8,128)(2,1)S(1)} collective-permute-done((bf16[256,1280]{1,0:T(8,128)(2,1)S(1)}, bf16[256,1280]{1,0:T(8,128)(2,1)S(1)}, u32[]{:S(2)}, u32[]{:S(2)}) %collective-permute-start.6) | collective-permute-done | bytes 655392 | tf_op jit(solution)/shard_map/ppermute | solution.py:402
  154.1 20.6 %collective-permute-done.7 = bf16[512,256]{1,0:T(8,128)(2,1)S(1)} collective-permute-done((bf16[512,256]{1,0:T(8,128)(2,1)S(1)}, bf16[512,256]{1,0:T(8,128)(2,1)S(1)}, u32[]{:S(2)}, u32[]{:S(2)}) %collective-permute-start.7) | collective-permute-done | bytes 262176 | tf_op jit(solution)/shard_map/ppermute | solution.py:402
  176.6 14.1 %attend.1.refs_1_ = bf16[512,1024]{1,0:T(8,128)(2,1)} custom-call(f32[512,1280]{1,0:T(8,128)} %convolution_add_fusion.raw_ref.refs_1_, f32[512,128]{1,0:T(8,128)} %get-tuple-element.83.cosine_ref, f32[512,128]{1,0:T(8,128)} %get-tuple-element.49.sine_ref, f32[1,128]{1,0:T(1,128)} %bitcast_convert_fusion.gain_ref, ...), custom_call_target="tpu_custom_call" | custom-call | flops 4294967296 | bytes 6291456 | tf_op jit(solution)/shard_map/attend/pallas_call | solution.py:587
  200.5 20.0 %all-to-all-done.refs_0_ = bf16[8,3,192,256]{3,2,1,0:T(8,128)(2,1)S(1)} async-done(((bf16[8,3,192,256]{3,2,1,0:T(8,128)(2,1)}), bf16[8,3,192,256]{3,2,1,0:T(8,128)(2,1)S(1)}, u32[]{:S(2)}, u32[]{:S(2)}) %all-to-all-start) | async-done | bytes 2359328 | tf_op jit(solution)/shard_map/all_to_all | solution.py:949
  241.1 21.2 %collective-permute-done.10 = bf16[128,2176]{1,0:T(8,128)(2,1)} collective-permute-done((bf16[128,2176]{1,0:T(8,128)(2,1)}, bf16[128,2176]{1,0:T(8,128)(2,1)}, u32[]{:S(2)}, u32[]{:S(2)}) %collective-permute-start.10) | collective-permute-done | bytes 557088 | tf_op jit(solution)/shard_map/ppermute | solution.py:402
  263.7 32.4 %collective-permute-done.11.refs_0_ = bf16[128,2176]{1,0:T(8,128)(2,1)S(1)} collective-permute-done((bf16[128,2176]{1,0:T(8,128)(2,1)}, bf16[128,2176]{1,0:T(8,128)(2,1)S(1)}, u32[]{:S(2)}, u32[]{:S(2)}) %collective-permute-start.11) | collective-permute-done | bytes 557088 | tf_op jit(solution)/shard_map/ppermute | solution.py:481
  300.4 13.2 %collective-permute-done.12 = bf16[128,2176]{1,0:T(8,128)(2,1)} collective-permute-done((bf16[128,2176]{1,0:T(8,128)(2,1)S(1)}, bf16[128,2176]{1,0:T(8,128)(2,1)}, u32[]{:S(2)}, u32[]{:S(2)}) %collective-permute-start.12) | collective-permute-done | bytes 557088 | tf_op jit(solution)/shard_map/ppermute | solution.py:402
  322.9 10.5 %collective-permute-done.14.refs_0_ = bf16[128,2176]{1,0:T(8,128)(2,1)S(1)} collective-permute-done((bf16[128,2176]{1,0:T(8,128)(2,1)}, bf16[128,2176]{1,0:T(8,128)(2,1)S(1)}, u32[]{:S(2)}, u32[]{:S(2)}) %collective-permute-start.14) | collective-permute-done | bytes 557088 | tf_op jit(solution)/shard_map/ppermute | solution.py:481
  348.9 11.6 %collective-permute-done.16 = bf16[128,2176]{1,0:T(8,128)(2,1)S(1)} collective-permute-done((bf16[128,2176]{1,0:T(8,128)(2,1)}, bf16[128,2176]{1,0:T(8,128)(2,1)S(1)}, u32[]{:S(2)}, u32[]{:S(2)}) %collective-permute-start.16) | collective-permute-done | bytes 557088 | tf_op jit(solution)/shard_map/ppermute | solution.py:481
  380.8 57.7 %experts.1 = (bf16[1024,2048]{1,0:T(8,128)(2,1)}, bf16[1024,2176]{1,0:T(8,128)(2,1)}, bf16[1536,1024]{1,0:T(8,128)(2,1)}, bf16[3072,1024]{1,0:T(8,128)(2,1)}) custom-call(s32[1]{0:T(128)} %bitcast.12.first_ref, bf16[1024,2176]{1,0:T(8,128)(2,1)} %constant_dynamic-update-slice_fusion.8.refs_1_.token_ref.gate_ref, ...), custom_call_target="tpu_custom_call" | custom-call | flops 38654705664 | bytes 45088768 | tf_op jit(solution)/shard_map/experts/pallas_call | solution.py:786
  454.1 13.4 %collective-permute-done.28 = bf16[128,2176]{1,0:T(8,128)(2,1)S(1)} collective-permute-done((bf16[128,2176]{1,0:T(8,128)(2,1)S(1)}, bf16[128,2176]{1,0:T(8,128)(2,1)S(1)}, u32[]{:S(2)}, u32[]{:S(2)}) %collective-permute-start.28) | collective-permute-done | bytes 557088 | tf_op jit(solution)/shard_map/ppermute | solution.py:402
  470.4 10.4 %expert_grads.6 = (bf16[8,576,256]{2,1,0:T(8,128)(2,1)}, bf16[8,576,256]{2,1,0:T(8,128)(2,1)}) custom-call(bf16[3072,1024]{1,0:T(8,128)(2,1)} %get-tuple-element.24.slope_ref, bf16[1536,1024]{1,0:T(8,128)(2,1)} %get-tuple-element.25.active_ref, bf16[1024,2176]{1,0:T(8,128)(2,1)} %constant_dynamic-update-slice_fusion.8.refs_1_.token_ref.gate_ref, ...), custom_call_target="tpu_custom_call" | custom-call | flops 4831838208 | bytes 15466496 | tf_op jit(solution)/shard_map/expert_grads/pallas_call | solution.py:854
  503.8 29.1 %collective-permute-done.24 = bf16[8,576,256]{2,1,0:T(8,128)(2,1)} collective-permute-done((bf16[8,576,256]{2,1,0:T(8,128)(2,1)}, bf16[8,576,256]{2,1,0:T(8,128)(2,1)}, u32[]{:S(2)}, u32[]{:S(2)}) %collective-permute-start.24) | collective-permute-done | bytes 2359328 | tf_op jit(solution)/shard_map/ppermute | solution.py:402
  542.1 11.4 %collective-permute-done.32 = bf16[128,2048]{1,0:T(8,128)(2,1)S(1)} collective-permute-done((bf16[128,2048]{1,0:T(8,128)(2,1)S(1)}, bf16[128,2048]{1,0:T(8,128)(2,1)S(1)}, u32[]{:S(2)}, u32[]{:S(2)}) %collective-permute-start.32) | collective-permute-done | bytes 524320 | tf_op jit(solution)/shard_map/ppermute | solution.py:402
  584.7 24.4 %attend_back.1 = (bf16[512,1024]{1,0:T(8,128)(2,1)}, f32[1024,128]{1,0:T(8,128)}, f32[1024,128]{1,0:T(8,128)}, f32[8,128]{1,0:T(8,128)}) custom-call(f32[512,1280]{1,0:T(8,128)} %convolution_add_fusion.raw_ref.refs_1_, f32[512,128]{1,0:T(8,128)} %get-tuple-element.83.cosine_ref, f32[512,128]{1,0:T(8,128)} %get-tuple-element.49.sine_ref, ...), custom_call_target="tpu_custom_call" | custom-call | flops 10737418240 | bytes 6291456 | tf_op jit(solution)/shard_map/attend_back/pallas_call | solution.py:670
  657.0 33.8 %collective-permute-done.38 = bf16[4,256,1024]{2,1,0:T(8,128)(2,1)} collective-permute-done((bf16[4,256,1024]{2,1,0:T(8,128)(2,1)}, bf16[4,256,1024]{2,1,0:T(8,128)(2,1)}, u32[]{:S(2)}, u32[]{:S(2)}) %collective-permute-start.38) | collective-permute-done | bytes 2097184 | tf_op jit(solution)/shard_map/ppermute | solution.py:402
  737.6 15.4 %collective-permute-done.44 = f32[19,2048]{1,0:T(8,128)S(1)} collective-permute-done((f32[19,2048]{1,0:T(8,128)S(1)}, f32[19,2048]{1,0:T(8,128)S(1)}, u32[]{:S(2)}, u32[]{:S(2)}) %collective-permute-start.44) | collective-permute-done | bytes 155680 | tf_op jit(solution)/shard_map/ppermute | solution.py:402
  768.4 18.2 %collective-permute-done.46 = f32[19,2048]{1,0:T(8,128)S(1)} collective-permute-done((f32[19,2048]{1,0:T(8,128)S(1)}, f32[19,2048]{1,0:T(8,128)S(1)}, u32[]{:S(2)}, u32[]{:S(2)}) %collective-permute-start.46) | collective-permute-done | bytes 155680 | tf_op jit(solution)/shard_map/ppermute | solution.py:402
  794.3 16.6 %collective-permute-done.47 = f32[19,2048]{1,0:T(8,128)} collective-permute-done((f32[19,2048]{1,0:T(8,128)}, f32[19,2048]{1,0:T(8,128)}, u32[]{:S(2)}, u32[]{:S(2)}) %collective-permute-start.47) | collective-permute-done | bytes 155680 | tf_op jit(solution)/shard_map/ppermute | solution.py:402
  826.6 17.8 %all-to-all-done.4 = bf16[4,256,1024]{2,1,0:T(8,128)(2,1)S(1)} async-done(((bf16[4,256,1024]{2,1,0:T(8,128)(2,1)}), bf16[4,256,1024]{2,1,0:T(8,128)(2,1)S(1)}, u32[]{:S(2)}, u32[]{:S(2)}) %all-to-all-start.4) | async-done | bytes 2097184 | tf_op jit(solution)/shard_map/all_to_all | solution.py:1094
  (442 shorter events, 360.8 us)
Async XLA Ops:
  7.2 183.5 %all-gather.3.cloned.1.call-start = ((), (), s32[]{:S(2)}) async-start(), calls=%async_computation.7 | async-start | bytes 4718592 | tf_op jit(solution)/shard_map/all_gather | solution.py:912
  29.1 45.3 %collective-permute-start = (bf16[256,1280]{1,0:T(8,128)(2,1)}, bf16[256,1280]{1,0:T(8,128)(2,1)}, u32[]{:S(2)}, u32[]{:S(2)}) collective-permute-start(bf16[256,1280]{1,0:T(8,128)(2,1)} %param.16), channel_id=1, source_target_pairs={{0,4},{4,0},{1,5},{5,1},{2,6},{6,2},{3,7},{7,3},{8,12},{12,8},{9,1... | collective-permute-start | bytes 1966088 | tf_op jit(solution)/shard_map/ppermute | solution.py:402
  77.1 50.2 %collective-permute-start.4 = (bf16[256,1280]{1,0:T(8,128)(2,1)S(1)}, bf16[256,1280]{1,0:T(8,128)(2,1)S(1)}, u32[]{:S(2)}, u32[]{:S(2)}) collective-permute-start(bf16[256,1280]{1,0:T(8,128)(2,1)S(1)} %copy-done.22), channel_id=1, source_target_pairs={{0,4},{4,0},{1,5},{5,1},{2,6},{6,2},{3,7},{7,3},{8,12},{12,8},{9,1... | collective-permute-start | bytes 1966088 | tf_op jit(solution)/shard_map/ppermute | solution.py:402
  106.6 32.2 %collective-permute-start.6 = (bf16[256,1280]{1,0:T(8,128)(2,1)S(1)}, bf16[256,1280]{1,0:T(8,128)(2,1)S(1)}, u32[]{:S(2)}, u32[]{:S(2)}) collective-permute-start(bf16[256,1280]{1,0:T(8,128)(2,1)S(1)} %collective-permute-done.5), channel_id=1, source_target_pairs={{0,4},{4,0},{1,5},{5,1},{2,6},{6,2},{3,7},{7,3},{8,12},{12,8},{9,1... | collective-permute-start | bytes 1966088 | tf_op jit(solution)/shard_map/ppermute | solution.py:402
  140.8 79.8 %all-to-all-start = ((bf16[8,3,192,256]{3,2,1,0:T(8,128)(2,1)}), bf16[8,3,192,256]{3,2,1,0:T(8,128)(2,1)S(1)}, u32[]{:S(2)}, u32[]{:S(2)}) async-start(bf16[8,3,192,256]{3,2,1,0:T(8,128)(2,1)} %after.24), calls=%async_computation | async-start | bytes 4718592 | tf_op jit(solution)/shard_map/all_to_all | solution.py:949
  144.4 156.1 %all-gather.5.cloned.1.call-start = ((), (), s32[]{:S(2)}) async-start(), calls=%async_computation.8 | async-start | bytes 4718592 | tf_op jit(solution)/shard_map/all_gather | solution.py:951
  221.9 100.4 %all-to-all-start.1 = ((bf16[8,3,192,256]{3,2,1,0:T(8,128)(2,1)}), bf16[8,3,192,256]{3,2,1,0:T(8,128)(2,1)}, u32[]{:S(2)}, u32[]{:S(2)}) async-start(bf16[8,3,192,256]{3,2,1,0:T(8,128)(2,1)} %after.29), calls=%async_computation.1 | async-start | bytes 4718592 | tf_op jit(solution)/shard_map/all_to_all | solution.py:979
  226.5 430.6 %reduce-scatter.3.cloned.1.call-start = ((), (), s32[]{:S(2)}) async-start(), calls=%async_computation.9 | async-start | bytes 4718592 | tf_op jit(solution)/shard_map/reduce_scatter | solution.py:1035
  227.4 73.1 %collective-permute-start.13 = (bf16[8,3,192,256]{3,2,1,0:T(8,128)(2,1)S(1)}, bf16[8,3,192,256]{3,2,1,0:T(8,128)(2,1)}, u32[]{:S(2)}, u32[]{:S(2)}) collective-permute-start(bf16[8,3,192,256]{3,2,1,0:T(8,128)(2,1)S(1)} %copy-done.6), channel_id=1, source_target_pairs={{0,2},{1,3},{2,0},{3,1},{4,6},{5,7},{6,4},{7,5},{8,10},{9,11},{10,... | collective-permute-start | bytes 7077896 | tf_op jit(solution)/shard_map/ppermute | solution.py:402
  262.3 33.8 %collective-permute-start.11 = (bf16[128,2176]{1,0:T(8,128)(2,1)}, bf16[128,2176]{1,0:T(8,128)(2,1)S(1)}, u32[]{:S(2)}, u32[]{:S(2)}) collective-permute-start(bf16[128,2176]{1,0:T(8,128)(2,1)} %after.26), channel_id=1, source_target_pairs={{0,8},{8,16},{16,24},{24,0},{1,9},{9,17},{17,25},{25,1},{2,10},{10... | collective-permute-start | bytes 1671176 | tf_op jit(solution)/shard_map/ppermute | solution.py:481
  322.3 52.0 %collective-permute-start.18 = (bf16[8,3,192,256]{3,2,1,0:T(8,128)(2,1)}, bf16[8,3,192,256]{3,2,1,0:T(8,128)(2,1)}, u32[]{:S(2)}, u32[]{:S(2)}) collective-permute-start(bf16[8,3,192,256]{3,2,1,0:T(8,128)(2,1)} %all-to-all-done.1.refs_1_.refs_2_), channel_id=1, source_target_pairs={{0,2},{1,3},{2,0},{3,1},{4,6},{5,7},{6,4},{7,5},{8,10},{9,11},{10,... | collective-permute-start | bytes 7077896 | tf_op jit(solution)/shard_map/ppermute | solution.py:402
  480.7 52.2 %collective-permute-start.24 = (bf16[8,576,256]{2,1,0:T(8,128)(2,1)}, bf16[8,576,256]{2,1,0:T(8,128)(2,1)}, u32[]{:S(2)}, u32[]{:S(2)}) collective-permute-start(bf16[8,576,256]{2,1,0:T(8,128)(2,1)} %get-tuple-element.27), channel_id=1, source_target_pairs={{0,2},{1,3},{2,0},{3,1},{4,6},{5,7},{6,4},{7,5},{8,10},{9,11},{10,... | collective-permute-start | bytes 7077896 | tf_op jit(solution)/shard_map/ppermute | solution.py:402
  496.9 64.2 %collective-permute-start.34 = (bf16[8,1152,256]{2,1,0:T(8,128)(2,1)}, bf16[8,1152,256]{2,1,0:T(8,128)(2,1)}, u32[]{:S(2)}, u32[]{:S(2)}) collective-permute-start(bf16[8,1152,256]{2,1,0:T(8,128)(2,1)} %expert_grads.4.refs_1_), channel_id=1, source_target_pairs={{0,1},{1,0},{2,3},{3,2},{4,5},{5,4},{6,7},{7,6},{8,9},{9,8},{10,11... | collective-permute-start | bytes 14155784 | tf_op jit(solution)/shard_map/ppermute | solution.py:402
  496.9 39.9 %collective-permute-start.25 = (bf16[128,2176]{1,0:T(8,128)(2,1)}, bf16[128,2176]{1,0:T(8,128)(2,1)}, u32[]{:S(2)}, u32[]{:S(2)}) collective-permute-start(bf16[128,2176]{1,0:T(8,128)(2,1)} %get-tuple-element.60), channel_id=1, source_target_pairs={{0,4},{4,0},{1,5},{5,1},{2,6},{6,2},{3,7},{7,3},{8,12},{12,8},{9,1... | collective-permute-start | bytes 1671176 | tf_op jit(solution)/shard_map/ppermute | solution.py:402
  500.4 36.3 %collective-permute-start.31 = (bf16[128,2176]{1,0:T(8,128)(2,1)}, bf16[128,2176]{1,0:T(8,128)(2,1)}, u32[]{:S(2)}, u32[]{:S(2)}) collective-permute-start(bf16[128,2176]{1,0:T(8,128)(2,1)} %add_convert_fusion.4), channel_id=1, source_target_pairs={{0,24},{8,0},{16,8},{24,16},{1,25},{9,1},{17,9},{25,17},{2,26},{10... | collective-permute-start | bytes 1671176 | tf_op jit(solution)/shard_map/ppermute | solution.py:481
  571.5 74.1 %all-to-all-start.2 = ((bf16[8,576,256]{2,1,0:T(8,128)(2,1)}), bf16[8,576,256]{2,1,0:T(8,128)(2,1)S(1)}, u32[]{:S(2)}, u32[]{:S(2)}) async-start(bf16[8,576,256]{2,1,0:T(8,128)(2,1)} %add_convert_fusion.1.refs_2_.refs_1_), calls=%async_computation.3 | async-start | bytes 4718592 | tf_op jit(solution)/shard_map/all_to_all | solution.py:1054
  575.1 270.6 %reduce-scatter.5.cloned.1.call-start = ((), (), s32[]{:S(2)}) async-start(), calls=%async_computation.10 | async-start | bytes 5898240 | tf_op jit(solution)/shard_map/reduce_scatter | solution.py:1086
  578.3 63.7 %collective-permute-start.48 = (bf16[8,576,256]{2,1,0:T(8,128)(2,1)}, bf16[8,576,256]{2,1,0:T(8,128)(2,1)}, u32[]{:S(2)}, u32[]{:S(2)}) collective-permute-start(bf16[8,576,256]{2,1,0:T(8,128)(2,1)} %after.42), channel_id=1, source_target_pairs={{0,2},{1,3},{2,0},{3,1},{4,6},{5,7},{6,4},{7,5},{8,10},{9,11},{10,... | collective-permute-start | bytes 7077896 | tf_op jit(solution)/shard_map/ppermute | solution.py:402
  626.0 64.8 %collective-permute-start.38 = (bf16[4,256,1024]{2,1,0:T(8,128)(2,1)}, bf16[4,256,1024]{2,1,0:T(8,128)(2,1)}, u32[]{:S(2)}, u32[]{:S(2)}) collective-permute-start(bf16[4,256,1024]{2,1,0:T(8,128)(2,1)} %get-tuple-element.62), channel_id=1, source_target_pairs={{0,4},{4,0},{1,5},{5,1},{2,6},{6,2},{3,7},{7,3},{8,12},{12,8},{9,1... | collective-permute-start | bytes 6291464 | tf_op jit(solution)/shard_map/ppermute | solution.py:402
  699.9 88.0 %all-to-all-start.3 = ((bf16[8,576,256]{2,1,0:T(8,128)(2,1)}), bf16[8,576,256]{2,1,0:T(8,128)(2,1)S(1)}, u32[]{:S(2)}, u32[]{:S(2)}) async-start(bf16[8,576,256]{2,1,0:T(8,128)(2,1)} %after.44), calls=%async_computation.5 | async-start | bytes 4718592 | tf_op jit(solution)/shard_map/all_to_all | solution.py:1065
  733.8 32.5 %collective-permute-start.41 = (bf16[128,2048]{1,0:T(8,128)(2,1)}, bf16[128,2048]{1,0:T(8,128)(2,1)S(1)}, u32[]{:S(2)}, u32[]{:S(2)}) collective-permute-start(bf16[128,2048]{1,0:T(8,128)(2,1)} %get-tuple-element.75), channel_id=1, source_target_pairs={{0,2},{1,3},{2,0},{3,1},{4,6},{5,7},{6,4},{7,5},{8,10},{9,11},{10,... | collective-permute-start | bytes 1572872 | tf_op jit(solution)/shard_map/ppermute | solution.py:402
  735.9 57.1 %collective-permute-start.36 = (bf16[128,2048]{1,0:T(8,128)(2,1)}, bf16[128,2048]{1,0:T(8,128)(2,1)S(1)}, u32[]{:S(2)}, u32[]{:S(2)}) collective-permute-start(bf16[128,2048]{1,0:T(8,128)(2,1)} %get-tuple-element.76), channel_id=1, source_target_pairs={{0,2},{1,3},{2,0},{3,1},{4,6},{5,7},{6,4},{7,5},{8,10},{9,11},{10,... | collective-permute-start | bytes 1572872 | tf_op jit(solution)/shard_map/ppermute | solution.py:402
  768.4 45.3 %collective-permute-start.42 = (bf16[256,2048]{1,0:T(8,128)(2,1)}, bf16[256,2048]{1,0:T(8,128)(2,1)}, u32[]{:S(2)}, u32[]{:S(2)}) collective-permute-start(bf16[256,2048]{1,0:T(8,128)(2,1)} %pad_maximum_fusion.9), channel_id=1, source_target_pairs={{0,1},{1,0},{2,3},{3,2},{4,5},{5,4},{6,7},{7,6},{8,9},{9,8},{10,11... | collective-permute-start | bytes 3145736 | tf_op jit(solution)/shard_map/ppermute | solution.py:402
  789.3 55.0 %all-to-all-start.4 = ((bf16[4,256,1024]{2,1,0:T(8,128)(2,1)}), bf16[4,256,1024]{2,1,0:T(8,128)(2,1)S(1)}, u32[]{:S(2)}, u32[]{:S(2)}) async-start(bf16[4,256,1024]{2,1,0:T(8,128)(2,1)} %after.45), calls=%async_computation.6 | async-start | bytes 4194304 | tf_op jit(solution)/shard_map/all_to_all | solution.py:1094
  (114 other events, 1559.6 us)
Sparse Core Ops, SparseCore 0:
  47.9 94.2 all-gather.2
  147.3 150.3 all-gather.4
  503.9 105.9 reduce-scatter.2
  647.2 139.3 reduce-scatter.4
